TPU v7x, 128 devices: a whole 4x4x4 slice. The times are simulated.
128 devices in a mesh: seq: 8 (over x, core), exp: 16 (over z, y).
Axes of the slice: x: 4, y: 4, z: 4, core: 2. Of those that a mesh axis runs over, the one named last changes fastest.
Arguments:
- frames: bfloat16 [16, 1024, 1024], P('exp', 'seq'), may hold values from -6 to 6
- cotangent: bfloat16 [16, 1024, 1024], P('exp', 'seq'), may hold values from -3 to 3
- lengths: int32 [16], P('exp'), may hold values from 256 to 1024, as said below
- qkv_weight: bfloat16 [1024, 1536], replicated, may hold values from -1 to 1
- out_weight: bfloat16 [512, 1024], replicated, may hold values from -0.25 to 0.25
- router: float32 [128, 1024], P(('seq', 'exp')), may hold values from -0.1875 to 0.1875
- expert_in: bfloat16 [128, 1024, 2048], P(('seq', 'exp')), may hold values from -0.1875 to 0.1875
- expert_out: bfloat16 [128, 2048, 1024], P(('seq', 'exp')), may hold values from -0.125 to 0.125
- send_index: int32 [128, 128, 3], P(('seq', 'exp')), may hold values from 0 to 127, as said below
- send_count: int32 [128, 128], P(('seq', 'exp')), may hold values from 0 to 3, as said below
Outputs:
- output: bfloat16 [16, 1024, 1024], P('exp', 'seq')
- grad_resid: bfloat16 [16, 1024, 1024], P('exp', 'seq')
- grad_expert_in: bfloat16 [128, 1024, 2048], P(('seq', 'exp'))
- grad_expert_out: bfloat16 [128, 2048, 1024], P(('seq', 'exp'))
- grad_router: float32 [128, 1024], P(('seq', 'exp'))
Inputs may be any that keep to these rules, and one draw needn't show every extreme that they name: For i < send_count[p, j], slot i of send_index[p, j] names a local frame of source p chosen by expert j; these are distinct within [p, j]. Later slots are unused. `send_count`: every column sums to 256, so each expert takes exactly 256 frames in all; every column has an entry equal to 3. `lengths`: some utterance has all 1024 frames live.
All inputs are finite; a program needn't handle non-finite values.
Results may differ from a plain program's by a relative error of at most 0.022.
Values may be sent and summed in bfloat16 or wider, within the bound.
No kernel may reach another device: no remote copies, remote signals or barrier semaphores. Data moves between devices by JAX's collectives and lax.ppermute only.
A program may use at most 128 MiB of HBM per device.

v0:
```python
import jax
import jax.numpy as jnp
from jax import lax
from jax.sharding import PartitionSpec as P

HEADS = 8
HD = 64


epsilon = 1e-05
masked_score = -1e30


def normalize(values):
    center = jnp.mean(values, axis=-1, keepdims=True)
    spread = jnp.mean(jnp.square(values - center), axis=-1, keepdims=True)
    return (values - center) * lax.rsqrt(spread + epsilon)


def norm_backward(values, upstream):
    center = jnp.mean(values, axis=-1, keepdims=True)
    spread = jnp.mean(jnp.square(values - center), axis=-1, keepdims=True)
    inverse = lax.rsqrt(spread + epsilon)
    unit_rows = (values - center) * inverse
    first_mean = jnp.mean(upstream, axis=-1, keepdims=True)
    second_mean = jnp.mean(upstream * unit_rows, axis=-1, keepdims=True)
    return inverse * (upstream - first_mean - unit_rows * second_mean)


def expert_forward(rows_x, w_first, w_second, router_row):
    logits = jnp.dot(rows_x.astype(jnp.float32), router_row, precision=lax.Precision.HIGHEST)
    gates = jax.nn.sigmoid(logits)
    before = jnp.dot(rows_x, w_first, preferred_element_type=jnp.float32)
    activated = jax.nn.gelu(before).astype(jnp.bfloat16)
    expert_rows = jnp.dot(activated, w_second, preferred_element_type=jnp.float32)
    returned = (gates[:, None] * expert_rows).astype(jnp.bfloat16)
    return (gates, before, activated, expert_rows, returned)


def expert_backward(rows_x, rows_g, w_first, w_second, router_row, saved):
    gates, before, activated, expert_rows = saved
    grads_wide = rows_g.astype(jnp.float32)
    out_grad = (gates[:, None] * grads_wide).astype(jnp.bfloat16)
    logit_grad = jnp.sum(grads_wide * expert_rows, axis=1) * gates * (1.0 - gates)
    act_grad = jnp.dot(out_grad, w_second.T, preferred_element_type=jnp.float32)
    _, gelu_pull = jax.vjp(jax.nn.gelu, before)
    before_grad = gelu_pull(act_grad)[0].astype(jnp.bfloat16)
    row_grad = jnp.dot(before_grad, w_first.T, preferred_element_type=jnp.float32)
    row_grad = (row_grad + logit_grad[:, None] * router_row[None, :]).astype(jnp.bfloat16)
    grad_second = jnp.dot(activated.T, out_grad, preferred_element_type=jnp.float32).astype(
        jnp.bfloat16
    )
    grad_first = jnp.dot(rows_x.T, before_grad, preferred_element_type=jnp.float32).astype(
        jnp.bfloat16
    )
    grad_route = jnp.dot(logit_grad, rows_x.astype(jnp.float32), precision=lax.Precision.HIGHEST)
    return (row_grad, grad_first, grad_second, grad_route)


def deliver(payload):
    return lax.all_to_all(payload, ("seq", "exp"), split_axis=0, concat_axis=0, tiled=True)


def local(
    frames,
    cotangent,
    lengths,
    qkv_weight,
    out_weight,
    router,
    expert_in,
    expert_out,
    send_index,
    send_count,
):
    own_frames = frames[0]
    upstream = cotangent[0]
    length = lengths[0]
    rows_here = own_frames.shape[0]
    model_width = own_frames.shape[1]
    head_width = out_weight.shape[0]
    chosen = send_index[0]
    counts = send_count[0]
    experts = chosen.shape[0]
    slot_count = chosen.shape[1]
    in_use = jnp.arange(slot_count, dtype=jnp.int32)[None, :] < counts[:, None]
    flat_chosen = chosen.reshape(-1)

    def select(table):
        gathered = jnp.take(table, flat_chosen, axis=0).reshape(experts, slot_count, model_width)
        return jnp.where(in_use[:, :, None], gathered, jnp.zeros((), table.dtype))

    def flatten_rows(block):
        return block.reshape(-1, model_width)

    def restore_rows(block):
        return block.reshape(experts, slot_count, model_width)

    rows_g = select(upstream)
    normed = normalize(own_frames.astype(jnp.float32)).astype(jnp.bfloat16)
    projected = jnp.dot(normed, qkv_weight, preferred_element_type=jnp.float32).astype(jnp.bfloat16)
    queries = projected[:, :head_width].reshape(rows_here, HEADS, HD)
    key_rows = projected[:, head_width : 2 * head_width]
    value_rows = projected[:, 2 * head_width :]
    score_scale = HD ** (-0.5)
    row_top = jnp.full((HEADS, rows_here), masked_score, jnp.float32)
    row_accum = jnp.zeros((rows_here, HEADS, HD), jnp.float32)
    key_block = lax.all_gather(key_rows, "seq", axis=0, tiled=True)
    value_block = lax.all_gather(value_rows, "seq", axis=0, tiled=True)
    key_count = key_block.shape[0]
    scores = (
        jnp.einsum(
            "qhd,khd->hqk",
            queries,
            key_block.reshape(key_count, HEADS, HD),
            preferred_element_type=jnp.float32,
        )
        * score_scale
    )
    in_range = jnp.arange(key_count, dtype=jnp.int32) < length
    masked = jnp.where(in_range[None, None, :], scores, masked_score)
    new_top = jnp.maximum(row_top, jnp.max(masked, axis=-1))
    weights = jnp.where(in_range[None, None, :], jnp.exp(masked - new_top[:, :, None]), 0.0)
    rescale = jnp.exp(row_top - new_top)
    row_total = jnp.sum(weights, axis=-1)
    weighted = jnp.einsum(
        "hqk,khd->qhd",
        weights.astype(jnp.bfloat16),
        value_block.reshape(key_count, HEADS, HD),
        preferred_element_type=jnp.float32,
    )
    row_accum = row_accum * rescale.T[:, :, None] + weighted
    row_top, row_total, row_accum = (new_top, row_total, row_accum)
    attended = (
        (row_accum / row_total.T[:, :, None]).astype(jnp.bfloat16).reshape(rows_here, head_width)
    )
    resid = (
        own_frames.astype(jnp.float32)
        + jnp.dot(attended, out_weight, preferred_element_type=jnp.float32)
    ).astype(jnp.bfloat16)
    resid_wide = resid.astype(jnp.float32)
    mid_rows = normalize(resid_wide).astype(jnp.bfloat16)
    rows_x = select(mid_rows)
    w_first = expert_in[0]
    w_second = expert_out[0]
    router_row = router[0]
    arrived_x = flatten_rows(deliver(rows_x))
    gates, before, activated, expert_rows, returned = expert_forward(
        arrived_x, w_first, w_second, router_row
    )
    back_out = deliver(restore_rows(returned))
    arrived_g = flatten_rows(deliver(rows_g))
    row_grad, grad_first, grad_second, grad_route = expert_backward(
        arrived_x, arrived_g, w_first, w_second, router_row, (gates, before, activated, expert_rows)
    )
    back_grad = deliver(restore_rows(row_grad))
    frame_ids = jnp.arange(rows_here, dtype=jnp.int32)[:, None]
    spread_map = ((flat_chosen[None, :] == frame_ids) & in_use.reshape(-1)[None, :]).astype(
        jnp.bfloat16
    )
    mixture = jnp.dot(
        spread_map, back_out.reshape(-1, model_width), preferred_element_type=jnp.float32
    )
    normed_grad = jnp.dot(
        spread_map, back_grad.reshape(-1, model_width), preferred_element_type=jnp.float32
    )
    output = (resid_wide + mixture).astype(jnp.bfloat16)
    grad_resid = (upstream.astype(jnp.float32) + norm_backward(resid_wide, normed_grad)).astype(
        jnp.bfloat16
    )
    return (output[None], grad_resid[None], grad_first[None], grad_second[None], grad_route[None])


def solution(mesh):
    in_specs = (
        P("exp", "seq", None),
        P("exp", "seq", None),
        P("exp"),
        P(),
        P(),
        P(("seq", "exp"), None),
        P(("seq", "exp"), None, None),
        P(("seq", "exp"), None, None),
        P(("seq", "exp"), None, None),
        P(("seq", "exp"), None),
    )
    out_specs = (
        P("exp", "seq", None),
        P("exp", "seq", None),
        P(("seq", "exp"), None, None),
        P(("seq", "exp"), None, None),
        P(("seq", "exp"), None),
    )
    return jax.shard_map(local, mesh=mesh, in_specs=in_specs, out_specs=out_specs, check_vma=False)
```

profile of v0, /device:TPU:1, one launch (start us, length us, event | category | flops | bytes accessed | tf_op | source)
XLA Modules:
  0.0 233.9 jit_solution(4755728274513231568)
XLA Ops:
  7.2 1.2 convert_reduce_fusion
  8.5 1.2 fusion.45
  9.7 1.6 convolution_convert_fusion
  11.2 0.8 fusion.65
  12.8 1.0 copy.18
  15.2 1.0 eq.15
  16.3 2.7 %gather_fusion.1 = bf16[384,1024]{1,0:T(8,128)(2,1)} fusion(bf16[128,1024]{1,0:T(8,128)(2,1)S(1)} %bitcast.80, s32[1024]{0:T(1024)S(1)} %pad_clamp_fusion), kind=kCustom, calls=%fused_computation.1.clone | custom fusion | bytes 1574400 | tf_op jit(solution)/shard_map/jit(_take)/gather | solution.py:90
  20.8 18.3 %all-gather.3.cloned.1.call-done = bf16[1024,512]{1,0:T(8,128)(2,1)} async-done(((bf16[128,512]{1,0:T(8,128)(2,1)}), bf16[1024,512]{1,0:T(8,128)(2,1)}) %all-gather.3.cloned.1.call-update) | async-done | bytes 1048592 | tf_op jit(solution)/shard_map/all_gather | solution.py:108
  39.1 2.3 copy.19
  41.4 2.1 fusion.8
  43.5 2.0 copy-done.3
  45.5 1.1 fusion.16
  46.6 18.0 %all-gather.5.cloned.1.call-done = bf16[1024,512]{1,0:T(8,128)(2,1)} async-done(((bf16[128,512]{1,0:T(8,128)(2,1)}), bf16[1024,512]{1,0:T(8,128)(2,1)}) %all-gather.5.cloned.1.call-update) | async-done | bytes 1048592 | tf_op jit(solution)/shard_map/all_gather | solution.py:109
  64.7 2.3 copy.20
  66.9 3.7 %fusion.38 = bf16[128,8,64]{0,2,1:T(8,128)(2,1)S(1)} fusion(bf16[1024,8,64]{0,2,1:T(8,128)(2,1)} %bitcast.82, f32[8,128,1024]{2,1,0:T(8,128)} %copy-done.3, f32[8,128]{1,0:T(8,128)S(1)} %get-tuple-element.16, pred[1024]{0:T(1024)(128)(4,1)S(1)} %copy-done.12, f32[128,8]{0,1:T(8,128)S(1)} %bitcast.86, f32[128,8]{0,1:T(8,128)S(1)} %get-tuple-element.15), kind=kOutput, calls=%fused_computation.45 | convolution fusion | flops 139657216 | bytes 5387264 | tf_op jit(solution)/shard_map/hqk,khd->qhd/dot_general | solution.py:126
  72.0 0.8 fusion.47
  72.8 4.4 %gather_fusion = bf16[384,1024]{1,0:T(8,128)(2,1)} fusion(bf16[128,1024]{1,0:T(8,128)(2,1)} %fusion.47, s32[1024]{0:T(1024)S(1)} %copy-done.9), kind=kCustom, calls=%fused_computation.clone | custom fusion | bytes 1574400 | tf_op jit(solution)/shard_map/jit(_take)/gather | solution.py:90
  77.2 2.7 %broadcast_select_fusion.2 = (bf16[384,1024]{1,0:T(8,128)(2,1)}, bf16[384,1024]{1,0:T(8,128)(2,1)}) fusion(bf16[384,1024]{1,0:T(8,128)(2,1)} %gather_fusion.1, pred[384]{0:T(512)(128)(4,1)S(1)} %copy-done.13, bf16[384,1024]{1,0:T(8,128)(2,1)} %gather_fusion), kind=kLoop, calls=%fused_computation.49 | loop fusion | flops 786432 | bytes 3146112 | tf_op jit(solution)/shard_map/jit(_take)/select_n | solution.py:90
  79.9 3.3 %reshape.143 = bf16[128,3,1024]{2,1,0:T(4,128)(2,1)} reshape(bf16[384,1024]{1,0:T(8,128)(2,1)} %get-tuple-element.18) | data formatting | bytes 1572864 | tf_op jit(solution)/shard_map/reshape | solution.py:90
  83.1 3.3 %reshape.147 = bf16[128,3,1024]{2,1,0:T(4,128)(2,1)} reshape(bf16[384,1024]{1,0:T(8,128)(2,1)} %get-tuple-element.17) | data formatting | bytes 1572864 | tf_op jit(solution)/shard_map/reshape | solution.py:90
  86.4 3.5 %broadcast_select_fusion = (bf16[128,3,1024]{2,1,0:T(4,128)(2,1)}, bf16[128,3,1024]{2,1,0:T(4,128)(2,1)S(1)}) fusion(bf16[128,3,1024]{2,1,0:T(4,128)(2,1)} %reshape.147, pred[128,3]{1,0:T(8,128)(4,1)S(1)} %iota_compare_fusion.1, bf16[128,3,1024]{2,1,0:T(4,128)(2,1)} %reshape.143), kind=kLoop, calls=%fused_computation.46 | loop fusion | flops 786432 | bytes 3146112 | tf_op jit(solution)/shard_map/jit(_where)/select_n | solution.py:91
  89.9 26.5 %all_to_all.20 = bf16[128,3,1024]{2,1,0:T(4,128)(2,1)} all-to-all(bf16[128,3,1024]{2,1,0:T(4,128)(2,1)S(1)} %get-tuple-element.14), channel_id=1, replica_groups=mesh['seq'=8,'exp'=16] {'seq','exp'}, dimensions={0} | all-to-all | bytes 1572864 | tf_op jit(solution)/shard_map/all_to_all | solution.py:61
  116.4 5.8 %all-to-all-start.2 = ((bf16[128,3,1024]{2,1,0:T(4,128)(2,1)}), bf16[128,3,1024]{2,1,0:T(4,128)(2,1)}, u32[]{:S(2)}, u32[]{:S(2)}) async-start(bf16[128,3,1024]{2,1,0:T(4,128)(2,1)} %get-tuple-element.13), calls=%async_computation.2 | async-start | bytes 2097152 | tf_op jit(solution)/shard_map/all_to_all | solution.py:61
  122.2 3.2 %reshape.144 = bf16[384,1024]{1,0:T(8,128)(2,1)} reshape(bf16[128,3,1024]{2,1,0:T(4,128)(2,1)} %all_to_all.20) | data formatting | bytes 1572864 | tf_op jit(solution)/shard_map/reshape | solution.py:94
  125.4 1.9 convolution_reduce_fusion
  127.5 5.9 %fusion.6 = f32[384,2048]{1,0:T(8,128)} fusion(bf16[384,1024]{1,0:T(8,128)(2,1)} %reshape.144, bf16[1,1024,2048]{2,1,0:T(8,128)(2,1)} %param.18), kind=kOutput, calls=%fused_computation.10 | convolution fusion | flops 1610612736 | bytes 8126464 | tf_op jit(solution)/shard_map/dot_general | solution.py:33
  133.4 7.4 %all-to-all-done.2 = bf16[128,3,1024]{2,1,0:T(4,128)(2,1)} async-done(((bf16[128,3,1024]{2,1,0:T(4,128)(2,1)}), bf16[128,3,1024]{2,1,0:T(4,128)(2,1)}, u32[]{:S(2)}, u32[]{:S(2)}) %all-to-all-start.2) | async-done | bytes 786464 | tf_op jit(solution)/shard_map/all_to_all | solution.py:61
  140.8 3.3 %reshape.150 = f32[384,1024]{1,0:T(8,128)} reshape(bf16[128,3,1024]{2,1,0:T(4,128)(2,1)} %all-to-all-done.2) | data formatting | bytes 2359296 | tf_op jit(solution)/shard_map/convert_element_type | solution.py:42
  144.1 6.5 %multiply_reduce_fusion = (f32[384]{0:T(512)S(1)}, bf16[384,1024]{1,0:T(8,128)(2,1)}) fusion(f32[384,1024]{1,0:T(8,128)} %reshape.150, f32[384]{0:T(512)S(1)} %add_divide_fusion, bf16[1,2048,1024]{2,1,0:T(8,128)(2,1)} %param.19, f32[384,2048]{1,0:T(8,128)} %fusion.6), kind=kOutput, calls=%fused_computation.33 | convolution fusion | flops 1619263104 | bytes 9702400 | tf_op jit(solution)/shard_map/dot_general | solution.py:35
  150.6 2.7 %multiply_convert_fusion.1 = bf16[128,3,1024]{2,1,0:T(4,128)(2,1)} fusion(f32[128,3]{1,0:T(8,128)S(1)} %mul.151, bf16[128,3,1024]{2,1,0:T(4,128)(2,1)} %all-to-all-done.2), kind=kLoop, calls=%fused_computation.28 | loop fusion | flops 1179648 | bytes 1574400 | tf_op jit(solution)/shard_map/convert_element_type | solution.py:43
  153.3 3.2 %convert_element_type.90 = bf16[384,1024]{1,0:T(8,128)(2,1)} reshape(bf16[128,3,1024]{2,1,0:T(4,128)(2,1)} %multiply_convert_fusion.1) | data formatting | bytes 1572864 | tf_op jit(solution)/shard_map/convert_element_type | solution.py:43
  156.5 6.9 %fusion.15 = bf16[384,2048]{1,0:T(8,128)(2,1)S(1)} fusion(f32[384,2048]{1,0:T(8,128)} %fusion.6, bf16[384,1024]{1,0:T(8,128)(2,1)} %convert_element_type.90, bf16[1,2048,1024]{2,1,0:T(8,128)(2,1)} %param.19), kind=kOutput, calls=%fused_computation.23 | convolution fusion | flops 1626341376 | bytes 9699328 | tf_op jit(solution)/shard_map/dot_general | solution.py:45
  163.5 1.1 copy-done.16
  164.6 2.8 %add_convert_fusion = bf16[384,1024]{1,0:T(8,128)(2,1)} fusion(bf16[384,2048]{1,0:T(8,128)(2,1)S(1)} %fusion.15, bf16[1,1024,2048]{2,1,0:T(8,128)(2,1)S(1)} %copy-done.15, f32[1024]{0:T(1024)S(1)} %bitcast.85, f32[384]{0:T(512)S(1)} %subtract_multiply_fusion.1), kind=kOutput, calls=%fused_computation.32 | convolution fusion | flops 1611792384 | bytes 6559232 | tf_op jit(solution)/shard_map/dot_general | solution.py:48
  167.4 3.3 %reshape.148 = bf16[128,3,1024]{2,1,0:T(4,128)(2,1)} reshape(bf16[384,1024]{1,0:T(8,128)(2,1)} %add_convert_fusion) | data formatting | bytes 1572864 | tf_op jit(solution)/shard_map/reshape | solution.py:97
  170.7 5.8 %all-to-all-start.3 = ((bf16[128,3,1024]{2,1,0:T(4,128)(2,1)}), bf16[128,3,1024]{2,1,0:T(4,128)(2,1)}, u32[]{:S(2)}, u32[]{:S(2)}) async-start(bf16[128,3,1024]{2,1,0:T(4,128)(2,1)} %reshape.148), calls=%async_computation.3 | async-start | bytes 2097152 | tf_op jit(solution)/shard_map/all_to_all | solution.py:61
  176.7 3.3 %reshape.145 = bf16[128,3,1024]{2,1,0:T(4,128)(2,1)} reshape(bf16[384,1024]{1,0:T(8,128)(2,1)} %get-tuple-element.9) | data formatting | bytes 1572864 | tf_op jit(solution)/shard_map/reshape | solution.py:97
  180.0 2.1 fusion.67
  182.1 6.1 %convert_bitcast_fusion.1 = bf16[1,1024,2048]{2,1,0:T(8,128)(2,1)} fusion(bf16[384,1024]{1,0:T(8,128)(2,1)} %reshape.144, bf16[384,2048]{1,0:T(8,128)(2,1)} %copy-done.16), kind=kOutput, calls=%fused_computation.13 | convolution fusion | flops 1612709888 | bytes 6553600 | tf_op jit(solution)/shard_map/dot_general | solution.py:53
  188.2 6.9 %all-to-all-done.3 = bf16[128,3,1024]{2,1,0:T(4,128)(2,1)} async-done(((bf16[128,3,1024]{2,1,0:T(4,128)(2,1)}), bf16[128,3,1024]{2,1,0:T(4,128)(2,1)}, u32[]{:S(2)}, u32[]{:S(2)}) %all-to-all-start.3) | async-done | bytes 786464 | tf_op jit(solution)/shard_map/all_to_all | solution.py:61
  195.1 5.8 %all-to-all-start.1 = ((bf16[128,3,1024]{2,1,0:T(4,128)(2,1)}), bf16[128,3,1024]{2,1,0:T(4,128)(2,1)}, u32[]{:S(2)}, u32[]{:S(2)}) async-start(bf16[128,3,1024]{2,1,0:T(4,128)(2,1)} %reshape.145), calls=%async_computation.1 | async-start | bytes 2097152 | tf_op jit(solution)/shard_map/all_to_all | solution.py:61
  200.8 7.0 %convert_bitcast_fusion = bf16[1,2048,1024]{2,1,0:T(8,128)(2,1)} fusion(f32[384,1024]{1,0:T(8,128)} %reshape.150, f32[384]{0:T(512)S(1)} %add_divide_fusion, f32[384,2048]{1,0:T(8,128)} %fusion.6), kind=kOutput, calls=%fused_computation.12 | convolution fusion | flops 1620574208 | bytes 8914432 | tf_op jit(solution)/shard_map/dot_general | solution.py:50
  207.9 3.2 %reshape.149 = bf16[384,1024]{1,0:T(8,128)(2,1)} reshape(bf16[128,3,1024]{2,1,0:T(4,128)(2,1)} %all-to-all-done.3) | data formatting | bytes 1572864 | tf_op jit(solution)/shard_map/reshape | solution.py:165
  211.1 2.4 %fusion.64 = (f32[128]{0:T(128)S(1)}, f32[128]{0:T(128)S(1)}, f32[128,1024]{1,0:T(8,128)}) fusion(f32[128]{0:T(128)S(1)} %add_rsqrt_fusion, f32[128,1024]{1,0:T(8,128)} %copy-done.2, f32[128]{0:T(128)S(1)} %broadcast_multiply_fusion.2, bf16[384,1024]{1,0:T(8,128)(2,1)} %reshape.149, s32[384]{0:T(512)S(1)} %copy-done.7, pred[384]{0:T(512)(128)(4,1)S(1)} %lt.48), kind=kOutput, calls=%fused_computation.92 | convolution fusion | flops 101416704 | bytes 1838976 | tf_op jit(solution)/shard_map/dot_general | solution.py:164
  213.5 6.0 %all-to-all-done.1 = bf16[128,3,1024]{2,1,0:T(4,128)(2,1)} async-done(((bf16[128,3,1024]{2,1,0:T(4,128)(2,1)}), bf16[128,3,1024]{2,1,0:T(4,128)(2,1)}, u32[]{:S(2)}, u32[]{:S(2)}) %all-to-all-start.1) | async-done | bytes 786464 | tf_op jit(solution)/shard_map/all_to_all | solution.py:61
  219.4 3.2 %reshape.146 = bf16[384,1024]{1,0:T(8,128)(2,1)} reshape(bf16[128,3,1024]{2,1,0:T(4,128)(2,1)} %all-to-all-done.1) | data formatting | bytes 1572864 | tf_op jit(solution)/shard_map/reshape | solution.py:162
  222.6 2.3 fusion.31
  224.9 2.2 fusion.48
  (55 shorter events, 5.1 us)
Async XLA Ops:
  7.2 2.5 %copy-start = (bf16[1024,1536]{1,0:T(8,128)(2,1)S(1)}, bf16[1024,1536]{1,0:T(8,128)(2,1)}, u32[]{:S(2)}) copy-start(bf16[1024,1536]{1,0:T(8,128)(2,1)} %param.15) | copy-start | bytes 9437188
  7.2 7.3 %copy-start.14 = (s32[1,128,3]{1,0,2:T(1,128)S(1)}, s32[1,128,3]{1,0,2:T(1,128)}, u32[]{:S(2)}) copy-start(s32[1,128,3]{1,0,2:T(1,128)} %param.20) | copy-start | bytes 4612
  7.2 9.1 %copy-start.1 = (bf16[1,128,1024]{2,1,0:T(8,128)(2,1)S(1)}, bf16[1,128,1024]{2,1,0:T(8,128)(2,1)}, u32[]{:S(2)}) copy-start(bf16[1,128,1024]{2,1,0:T(8,128)(2,1)} %param.13) | copy-start | bytes 786436
  7.2 31.9 %all-gather.3.cloned.1.call-start = ((), (), s32[]{:S(2)}) async-start(), calls=%async_computation.4 | async-start | bytes 1179648 | tf_op jit(solution)/shard_map/all_gather | solution.py:108
  12.0 52.7 %all-gather.5.cloned.1.call-start = ((), (), s32[]{:S(2)}) async-start(), calls=%async_computation.5 | async-start | bytes 1179648 | tf_op jit(solution)/shard_map/all_gather | solution.py:109
  16.3 3.3 %copy-start.6 = (s32[384]{0:T(512)}, s32[384]{0:T(512)S(1)}, u32[]{:S(2)}) copy-start(s32[384]{0:T(512)S(1)} %eq.15) | copy-start | bytes 4612
  16.3 2.7 %copy-start.8 = (s32[1024]{0:T(1024)}, s32[1024]{0:T(1024)S(1)}, u32[]{:S(2)}) copy-start(s32[1024]{0:T(1024)S(1)} %pad_clamp_fusion) | copy-start | bytes 12292
  41.4 4.1 %copy-start.11 = (pred[1024]{0:T(1024)(128)(4,1)S(1)}, pred[1024]{0:T(1024)(128)(4,1)}, u32[]{:S(2)}) copy-start(pred[1024]{0:T(1024)(128)(4,1)} %iota_compare_fusion.2) | copy-start | bytes 3076
  43.5 2.0 copy-start.3
  45.5 21.4 %copy-start.12 = (pred[1024]{0:T(1024)(128)(4,1)S(1)}, pred[1024]{0:T(1024)(128)(4,1)}, u32[]{:S(2)}) copy-start(pred[1024]{0:T(1024)(128)(4,1)} %iota_compare_fusion.2) | copy-start | bytes 3076
  66.9 3.7 %copy-start.4 = (bf16[1,128,1024]{2,1,0:T(8,128)(2,1)S(1)}, bf16[1,128,1024]{2,1,0:T(8,128)(2,1)}, u32[]{:S(2)}) copy-start(bf16[1,128,1024]{2,1,0:T(8,128)(2,1)} %param.12) | copy-start | bytes 786436
  66.9 3.7 %copy-start.5 = (bf16[512,1024]{1,0:T(8,128)(2,1)S(1)}, bf16[512,1024]{1,0:T(8,128)(2,1)}, u32[]{:S(2)}) copy-start(bf16[512,1024]{1,0:T(8,128)(2,1)} %param.16) | copy-start | bytes 3145732
  70.6 2.1 copy-start.9
  71.1 0.9 copy-start.2
  72.8 4.4 %copy-start.13 = (pred[384]{0:T(512)(128)(4,1)S(1)}, pred[384]{0:T(512)(128)(4,1)}, u32[]{:S(2)}) copy-start(pred[384]{0:T(512)(128)(4,1)} %compare_and_fusion) | copy-start | bytes 1156
  89.9 35.5 %copy-start.10 = (f32[1,1024]{1,0:T(1,128)S(1)}, f32[1,1024]{1,0:T(1,128)}, u32[]{:S(2)}) copy-start(f32[1,1024]{1,0:T(1,128)} %param.17) | copy-start | bytes 12292
  116.4 24.4 %all-to-all-start.2 = ((bf16[128,3,1024]{2,1,0:T(4,128)(2,1)}), bf16[128,3,1024]{2,1,0:T(4,128)(2,1)}, u32[]{:S(2)}, u32[]{:S(2)}) async-start(bf16[128,3,1024]{2,1,0:T(4,128)(2,1)} %get-tuple-element.13), calls=%async_computation.2 | async-start | bytes 2097152 | tf_op jit(solution)/shard_map/all_to_all | solution.py:61
  156.5 8.1 %copy-start.15 = (bf16[1,1024,2048]{2,1,0:T(8,128)(2,1)S(1)}, bf16[1,1024,2048]{2,1,0:T(8,128)(2,1)}, u32[]{:S(2)}) copy-start(bf16[1,1024,2048]{2,1,0:T(8,128)(2,1)} %param.18) | copy-start | bytes 12582916
  163.5 1.1 copy-start.16
  170.7 24.4 %all-to-all-start.3 = ((bf16[128,3,1024]{2,1,0:T(4,128)(2,1)}), bf16[128,3,1024]{2,1,0:T(4,128)(2,1)}, u32[]{:S(2)}, u32[]{:S(2)}) async-start(bf16[128,3,1024]{2,1,0:T(4,128)(2,1)} %reshape.148), calls=%async_computation.3 | async-start | bytes 2097152 | tf_op jit(solution)/shard_map/all_to_all | solution.py:61
  195.1 24.4 %all-to-all-start.1 = ((bf16[128,3,1024]{2,1,0:T(4,128)(2,1)}), bf16[128,3,1024]{2,1,0:T(4,128)(2,1)}, u32[]{:S(2)}, u32[]{:S(2)}) async-start(bf16[128,3,1024]{2,1,0:T(4,128)(2,1)} %reshape.145), calls=%async_computation.1 | async-start | bytes 2097152 | tf_op jit(solution)/shard_map/all_to_all | solution.py:61
  200.8 10.2 %copy-start.7 = (s32[384]{0:T(512)S(1)}, s32[384]{0:T(512)}, u32[]{:S(2)}) copy-start(s32[384]{0:T(512)} %copy-done.6) | copy-start | bytes 4612
Sparse Core Ops, SparseCore 0:
  12.1 26.9 all-gather.2
  41.4 23.1 all-gather.4
where the time goes:
time: 235 us; the launch traced here: 234 us
  waiting for transfers between devices  57.4 us (24%)
  matrix products  51.7 us (22%)
  local copies, waits for them, and re-layouts  48.6 us (21%)
  blocking collectives  26.5 us (11%)
  other arithmetic  17.5 us (7%)
  starting transfers between devices  17.4 us (7%)
  between operations  15 us (6%)
    all_to_all x1, blocking collectives, deliver(): lax.all_to_all(payload, ('seq', 'exp'), split_axis=0, concat_axis=0, tile...  26.5 us
    all_to_all x3, waiting for transfers between devices, deliver(): lax.all_to_all(payload, ('seq', 'exp'), split_axis=0, concat_axis=0, tile...  20.3 us
    all_gather x1, waiting for transfers between devices, local(): key_block = lax.all_gather(key_rows, 'seq', axis=0, tiled=True)  18.3 us
    all_gather x1, waiting for transfers between devices, local(): value_block = lax.all_gather(value_rows, 'seq', axis=0, tiled=True)  18 us
    all_to_all x3, starting transfers between devices, deliver(): lax.all_to_all(payload, ('seq', 'exp'), split_axis=0, concat_axis=0, tile...  17.3 us
    gather x2, local copies, waits for them, and re-layouts, select(): jnp.take(table, flat_chosen, axis=0)  7.05 us
    dot_general x1, matrix products, expert_backward(): jnp.dot(activated.T, out_grad, preferred_element_type=jnp.float32)  7.05 us
    dot_general x1, matrix products, expert_backward(): act_grad = jnp.dot(out_grad, w_second.T, preferred_element_type=jnp.float32)  6.94 us
  transfers between devices with their start and end apart: 5, of which 5 were waited for; matrix products, arithmetic and copies ran while one was open for 21% of the time, Pallas kernels for 0%

commit v1 on v0

v1 whole, which is shorter than its diff:
```python
import jax
import jax.numpy as jnp
from jax import lax
from jax.experimental import pallas as pl
from jax.experimental.pallas import tpu as pltpu
from jax.sharding import PartitionSpec as P

HEADS = 8
HD = 64
D = 1024
FF = 2048
FR = 128
DEVS = 128
SLOT = 3
KEYS = 1024
LIVE = 256
TILES = D // 128
ROWS = SLOT * TILES
PAIR = 2 * HD

epsilon = 1e-05
masked_score = -1e30
empty_mark = 2.0**100
empty_bound = 2.0**99

F32 = jnp.float32
BF16 = jnp.bfloat16
MB = 1024 * 1024


def params(mib, semantics=None):
    return pltpu.CompilerParams(vmem_limit_bytes=mib * MB, dimension_semantics=semantics)


def whole(shape):
    return pl.BlockSpec(shape, lambda *_: (0,) * len(shape))


def dot(a, b, dims=((1,), (0,))):
    return lax.dot_general(a, b, (dims, ((), ())), preferred_element_type=F32)


def normalize(values):
    center = jnp.mean(values, axis=-1, keepdims=True)
    shifted = values - center
    spread = jnp.mean(jnp.square(shifted), axis=-1, keepdims=True)
    inverse = lax.rsqrt(spread + epsilon)
    return shifted * inverse, inverse


def spread_matrix(index_ref, count_ref, slot):
    frame = lax.broadcasted_iota(jnp.int32, (FR, DEVS), 0)
    named = jnp.broadcast_to(index_ref[slot : slot + 1, :], (FR, DEVS)) == frame
    used = jnp.broadcast_to(count_ref[...], (FR, DEVS)) > slot
    return jnp.where(named & used, 1.0, 0.0)


def pack_rows(stage, rows, per, first):
    for tile in range(TILES):
        stage[pl.ds(first + tile, DEVS, stride=per), :] = rows[:, tile * 128 : (tile + 1) * 128]


def unpack_rows(stage, per, first):
    return jnp.concatenate(
        [stage[pl.ds(first + tile, DEVS, stride=per), :] for tile in range(TILES)], axis=1
    )


def project_kernel(frames_ref, weight_ref, kv_ref, q_ref, normed):
    step = pl.program_id(0)

    @pl.when(step == 0)
    def _():
        normed[...] = normalize(frames_ref[...].astype(F32))[0].astype(BF16)

    block = dot(normed[...], weight_ref[...]).astype(BF16)

    @pl.when(step < 2)
    def _():
        kv_ref[...] = block

    @pl.when(step == 2)
    def _():
        q_ref[...] = block


def project(frames, weight):
    half = HEADS * HD
    return pl.pallas_call(
        project_kernel,
        grid=(3,),
        in_specs=[
            whole((FR, D)),
            pl.BlockSpec((D, half), lambda n: (0, lax.rem(n + 1, 3))),
        ],
        out_specs=[
            pl.BlockSpec((FR, half), lambda n: (0, jnp.minimum(n, 1))),
            whole((FR, half)),
        ],
        out_shape=[
            jax.ShapeDtypeStruct((FR, 2 * half), BF16),
            jax.ShapeDtypeStruct((FR, half), BF16),
        ],
        scratch_shapes=[pltpu.VMEM((FR, D), BF16)],
        compiler_params=params(32),
        cost_estimate=pl.CostEstimate(
            flops=2 * FR * D * 3 * half, bytes_accessed=4 * MB, transcendentals=0
        ),
    )(frames, weight)


def gather_kernel(table_ref, index_ref, count_ref, out_ref, stage):
    count_column = jnp.broadcast_to(count_ref[...].astype(F32), (DEVS, DEVS)).T
    for slot in range(SLOT):
        pick = spread_matrix(index_ref, count_ref, slot).T.astype(BF16)
        rows = dot(pick, table_ref[...])
        mark = jnp.where(count_column[:, 0:1] > slot, 0.0, empty_mark)
        pack_rows(stage, rows + mark, ROWS, slot * TILES)
    out_ref[...] = stage[...].astype(BF16)


def gather_rows(table, index, count):
    return pl.pallas_call(
        gather_kernel,
        out_shape=jax.ShapeDtypeStruct((DEVS * ROWS, 128), BF16),
        scratch_shapes=[pltpu.VMEM((DEVS * ROWS, 128), F32)],
        compiler_params=params(32),
        cost_estimate=pl.CostEstimate(
            flops=2 * DEVS * SLOT * FR * D, bytes_accessed=2 * MB, transcendentals=0
        ),
    )(table, index, count)


def attend_kernel(
    length_ref, q_ref, k_ref, v_ref, frames_ref, weight_ref, index_ref, count_ref,
    resid_ref, rows_ref, attended, stage,
):
    step = pl.program_id(0)
    low = lax.broadcasted_iota(jnp.int32, (FR, PAIR), 1) < HD
    q = q_ref[...].astype(F32) * HD ** (-0.5)
    both = jnp.concatenate([jnp.where(low, q, 0.0), jnp.where(low, 0.0, q)], axis=0).astype(BF16)
    scores = dot(both, k_ref[...], ((1,), (1,)))
    live = lax.broadcasted_iota(jnp.int32, (1, KEYS), 1) < length_ref[0]
    scores = jnp.where(live, scores, masked_score)
    top = jnp.max(scores, axis=-1, keepdims=True)
    weights = jnp.exp(scores - top)
    total = jnp.sum(weights, axis=-1, keepdims=True)
    mixed = dot(weights.astype(BF16), v_ref[...]) / total
    attended[:, pl.ds(pl.multiple_of(step * PAIR, PAIR), PAIR)] = jnp.where(
        low, mixed[:FR], mixed[FR:]
    ).astype(BF16)

    @pl.when(step == HEADS // 2 - 1)
    def _():
        resid = (frames_ref[...].astype(F32) + dot(attended[...], weight_ref[...])).astype(BF16)
        resid_ref[...] = resid
        mid = normalize(resid.astype(F32))[0].astype(BF16)
        for slot in range(SLOT):
            pick = spread_matrix(index_ref, count_ref, slot).T.astype(BF16)
            pack_rows(stage, dot(pick, mid), ROWS, slot * TILES)
        rows_ref[...] = stage[...].astype(BF16)


def attend(length, q, kv, frames, weight, index, count):
    pairs = HEADS // 2
    return pl.pallas_call(
        attend_kernel,
        grid_spec=pltpu.PrefetchScalarGridSpec(
            num_scalar_prefetch=1,
            grid=(pairs,),
            in_specs=[
                pl.BlockSpec((FR, PAIR), lambda n, _: (0, n)),
                pl.BlockSpec((KEYS, PAIR), lambda n, _: (0, n)),
                pl.BlockSpec((KEYS, PAIR), lambda n, _: (0, n + pairs)),
                whole((FR, D)),
                whole((HEADS * HD, D)),
                whole((SLOT, DEVS)),
                whole((1, DEVS)),
            ],
            out_specs=[whole((FR, D)), whole((DEVS * ROWS, 128))],
            scratch_shapes=[
                pltpu.VMEM((FR, HEADS * HD), BF16),
                pltpu.VMEM((DEVS * ROWS, 128), F32),
            ],
        ),
        out_shape=[
            jax.ShapeDtypeStruct((FR, D), BF16),
            jax.ShapeDtypeStruct((DEVS * ROWS, 128), BF16),
        ],
        compiler_params=params(40),
        cost_estimate=pl.CostEstimate(
            flops=8 * FR * KEYS * HEADS * HD, bytes_accessed=5 * MB,
            transcendentals=FR * KEYS * HEADS,
        ),
    )(length, q, kv, kv, frames, weight, index, count)


FF_TILE = 512


def prepare_kernel(rows_ref, second_ref, grads_ref, place_ref, take_ref, pulled_ref, stage):
    @pl.when(pl.program_id(0) == 0)
    def _():
        stage[...] = rows_ref[...].astype(F32)
        rows = [unpack_rows(stage, ROWS, slot * TILES) for slot in range(SLOT)]
        rows = jnp.concatenate(rows, axis=0)
        total = SLOT * DEVS
        live = rows[:, 0:128] < empty_bound
        before = lax.broadcasted_iota(jnp.int32, (total, total), 0) >= lax.broadcasted_iota(
            jnp.int32, (total, total), 1
        )
        ranks = dot(
            jnp.where(before, 1.0, 0.0).astype(BF16), jnp.where(live, 1.0, 0.0).astype(BF16)
        )
        seat = jnp.where(live, ranks - 1.0, -1.0)[:, 0:1].astype(jnp.int32)
        place = jnp.where(
            seat == lax.broadcasted_iota(jnp.int32, (total, LIVE), 1), 1.0, 0.0
        )
        take = place.T.astype(BF16)
        place_ref[...] = place.astype(BF16)
        take_ref[...] = take
        grads_ref[...] = dot(take, rows.astype(BF16)).astype(BF16)

    pulled_ref[...] = dot(grads_ref[...], second_ref[...], ((1,), (1,)))


def prepare(rows, second):
    total = SLOT * DEVS
    return pl.pallas_call(
        prepare_kernel,
        grid=(FF // FF_TILE,),
        in_specs=[whole((DEVS * ROWS, 128)), pl.BlockSpec((FF_TILE, D), lambda n: (n, 0))],
        out_specs=[
            whole((LIVE, D)),
            whole((total, LIVE)),
            whole((LIVE, total)),
            pl.BlockSpec((LIVE, FF_TILE), lambda n: (0, n)),
        ],
        out_shape=[
            jax.ShapeDtypeStruct((LIVE, D), BF16),
            jax.ShapeDtypeStruct((total, LIVE), BF16),
            jax.ShapeDtypeStruct((LIVE, total), BF16),
            jax.ShapeDtypeStruct((LIVE, FF), F32),
        ],
        scratch_shapes=[pltpu.VMEM((DEVS * ROWS, 128), F32)],
        compiler_params=params(32),
        cost_estimate=pl.CostEstimate(
            flops=2 * LIVE * D * FF, bytes_accessed=8 * MB, transcendentals=0
        ),
    )(rows, second)


gelu_scale = (2.0 / jnp.pi) ** 0.5
gelu_cubic = 0.044715


def expert_kernel(
    rows_ref, take_ref, place_ref, grads_ref, pulled_ref, first_ref, second_ref, router_ref,
    back_ref, picked_ref, active_ref, before_grad_ref, out_grad_ref, route_grad_ref,
    stage, gates, result, row_grad, logit,
):
    step = pl.program_id(0)
    steps = pl.num_programs(0)

    @pl.when(step == 0)
    def _():
        stage[pl.ds(0, DEVS * ROWS), :] = rows_ref[...].astype(F32)
        rows = [
            unpack_rows(stage, ROWS, slot * TILES).astype(BF16) for slot in range(SLOT)
        ]
        picked = dot(take_ref[...], jnp.concatenate(rows, axis=0))
        picked_ref[...] = picked.astype(BF16)
        logits = jnp.sum(picked * router_ref[...], axis=-1, keepdims=True)
        gate = 1.0 / (1.0 + jnp.exp(-logits))
        gates[...] = jnp.broadcast_to(gate, gates.shape)
        out_grad_ref[...] = (gate * grads_ref[...].astype(F32)).astype(BF16)
        result[...] = jnp.zeros_like(result)
        row_grad[...] = jnp.zeros_like(row_grad)
        logit[...] = jnp.zeros_like(logit)

    first = first_ref[...]
    before = dot(picked_ref[...], first)
    square = before * before
    bend = jnp.tanh(gelu_scale * before * (1.0 + gelu_cubic * square))
    half = 0.5 * (1.0 + bend)
    active = (before * half).astype(BF16)
    slope = half + 0.5 * before * (1.0 - bend * bend) * (
        gelu_scale * (1.0 + 3.0 * gelu_cubic * square)
    )
    pulled = pulled_ref[...]
    gate = gates[:, 0:1]
    before_grad = (gate * pulled * slope).astype(BF16)
    active_ref[...] = active
    before_grad_ref[...] = before_grad
    logit[...] += jnp.sum(active.astype(F32) * pulled, axis=-1, keepdims=True)
    result[...] += dot(active, second_ref[...])
    row_grad[...] += dot(before_grad, first, ((1,), (1,)))

    @pl.when(step == steps - 1)
    def _():
        gate = gates[:, 0:1]
        logit_grad = logit[:, 0:1] * gate * (1.0 - gate)
        route_grad_ref[...] = jnp.sum(
            logit_grad * picked_ref[...].astype(F32), axis=0, keepdims=True
        )
        returned = (gate * result[...]).astype(BF16)
        back = (row_grad[...] + logit_grad * router_ref[...]).astype(BF16)
        for slot in range(SLOT):
            place = place_ref[pl.ds(slot * DEVS, DEVS), :]
            pack_rows(stage, dot(place, returned), 2 * ROWS, slot * TILES)
            pack_rows(stage, dot(place, back), 2 * ROWS, ROWS + slot * TILES)
        back_ref[...] = stage[...].astype(BF16)


def expert(rows, take, place, grads, pulled, first, second, router):
    total = SLOT * DEVS
    tile = FF_TILE
    return pl.pallas_call(
        expert_kernel,
        grid=(FF // tile,),
        in_specs=[
            whole((DEVS * ROWS, 128)),
            whole((LIVE, total)),
            whole((total, LIVE)),
            whole((LIVE, D)),
            pl.BlockSpec((LIVE, tile), lambda n: (0, n)),
            pl.BlockSpec((D, tile), lambda n: (0, n)),
            pl.BlockSpec((tile, D), lambda n: (n, 0)),
            whole((1, D)),
        ],
        out_specs=[
            whole((DEVS * ROWS * 2, 128)),
            whole((LIVE, D)),
            pl.BlockSpec((LIVE, tile), lambda n: (0, n)),
            pl.BlockSpec((LIVE, tile), lambda n: (0, n)),
            whole((LIVE, D)),
            whole((1, D)),
        ],
        out_shape=[
            jax.ShapeDtypeStruct((DEVS * ROWS * 2, 128), BF16),
            jax.ShapeDtypeStruct((LIVE, D), BF16),
            jax.ShapeDtypeStruct((LIVE, FF), BF16),
            jax.ShapeDtypeStruct((LIVE, FF), BF16),
            jax.ShapeDtypeStruct((LIVE, D), BF16),
            jax.ShapeDtypeStruct((1, D), F32),
        ],
        scratch_shapes=[
            pltpu.VMEM((DEVS * ROWS * 2, 128), F32),
            pltpu.VMEM((LIVE, 128), F32),
            pltpu.VMEM((LIVE, D), F32),
            pltpu.VMEM((LIVE, D), F32),
            pltpu.VMEM((LIVE, 128), F32),
        ],
        compiler_params=params(48),
        cost_estimate=pl.CostEstimate(
            flops=6 * LIVE * D * FF, bytes_accessed=14 * MB, transcendentals=LIVE * FF
        ),
    )(rows, take, place, grads, pulled, first, second, router)


def weight_grad_kernel(picked_ref, before_grad_ref, active_ref, out_grad_ref, first_ref, second_ref):
    first_ref[...] = dot(picked_ref[...], before_grad_ref[...], ((0,), (0,))).astype(BF16)
    second_ref[...] = dot(active_ref[...], out_grad_ref[...], ((0,), (0,))).astype(BF16)


def weight_grads(picked, before_grad, active, out_grad):
    tile = FF_TILE
    return pl.pallas_call(
        weight_grad_kernel,
        grid=(FF // tile,),
        in_specs=[
            whole((LIVE, D)),
            pl.BlockSpec((LIVE, tile), lambda n: (0, n)),
            pl.BlockSpec((LIVE, tile), lambda n: (0, n)),
            whole((LIVE, D)),
        ],
        out_specs=[
            pl.BlockSpec((D, tile), lambda n: (0, n)),
            pl.BlockSpec((tile, D), lambda n: (n, 0)),
        ],
        out_shape=[
            jax.ShapeDtypeStruct((D, FF), BF16),
            jax.ShapeDtypeStruct((FF, D), BF16),
        ],
        compiler_params=params(32),
        cost_estimate=pl.CostEstimate(
            flops=4 * LIVE * D * FF, bytes_accessed=11 * MB, transcendentals=0
        ),
    )(picked, before_grad, active, out_grad)


def combine_kernel(
    rows_ref, index_ref, count_ref, resid_ref, upstream_ref, output_ref, grad_ref, stage
):
    stage[...] = rows_ref[...].astype(F32)
    mixture = jnp.zeros((FR, D), F32)
    normed_grad = jnp.zeros((FR, D), F32)
    for slot in range(SLOT):
        spread = spread_matrix(index_ref, count_ref, slot).astype(BF16)
        rows = unpack_rows(stage, 2 * ROWS, slot * TILES).astype(BF16)
        mixture += dot(spread, rows)
        rows = unpack_rows(stage, 2 * ROWS, ROWS + slot * TILES).astype(BF16)
        normed_grad += dot(spread, rows)
    resid = resid_ref[...].astype(F32)
    output_ref[...] = (resid + mixture).astype(BF16)
    unit, inverse = normalize(resid)
    first_mean = jnp.mean(normed_grad, axis=-1, keepdims=True)
    second_mean = jnp.mean(normed_grad * unit, axis=-1, keepdims=True)
    grad = inverse * (normed_grad - first_mean - unit * second_mean)
    grad_ref[...] = (upstream_ref[...].astype(F32) + grad).astype(BF16)


def combine(rows, index, count, resid, upstream):
    return pl.pallas_call(
        combine_kernel,
        out_shape=[jax.ShapeDtypeStruct((FR, D), BF16)] * 2,
        scratch_shapes=[pltpu.VMEM((DEVS * ROWS * 2, 128), F32)],
        compiler_params=params(32),
        cost_estimate=pl.CostEstimate(
            flops=4 * DEVS * SLOT * FR * D, bytes_accessed=3 * MB, transcendentals=0
        ),
    )(rows, index, count, resid, upstream)


def deliver(rows, per):
    moved = lax.all_to_all(
        rows.reshape(DEVS, per, 128), ("seq", "exp"), split_axis=0, concat_axis=0, tiled=True
    )
    return moved.reshape(DEVS * per, 128)


def local(
    frames,
    cotangent,
    lengths,
    qkv_weight,
    out_weight,
    router,
    expert_in,
    expert_out,
    send_index,
    send_count,
):
    own_frames = frames[0]
    upstream = cotangent[0]
    first = expert_in[0]
    second = expert_out[0]
    index = send_index[0].T

    kv, q = project(own_frames, qkv_weight)
    all_kv = lax.all_gather(kv, "seq", axis=0, tiled=True)
    arrived_g = deliver(gather_rows(upstream, index, send_count), ROWS)
    resid, rows_x = attend(lengths, q, all_kv, own_frames, out_weight, index, send_count)
    arrived_x = deliver(rows_x, ROWS)
    grads, place, take, pulled = prepare(arrived_g, second)
    back, picked, active, before_grad, out_grad, grad_route = expert(
        arrived_x, take, place, grads, pulled, first, second, router
    )
    arrived_back = deliver(back, 2 * ROWS)
    grad_first, grad_second = weight_grads(picked, before_grad, active, out_grad)
    output, grad_resid = combine(arrived_back, index, send_count, resid, upstream)
    return (output[None], grad_resid[None], grad_first[None], grad_second[None], grad_route)


def solution(mesh):
    in_specs = (
        P("exp", "seq", None),
        P("exp", "seq", None),
        P("exp"),
        P(),
        P(),
        P(("seq", "exp"), None),
        P(("seq", "exp"), None, None),
        P(("seq", "exp"), None, None),
        P(("seq", "exp"), None, None),
        P(("seq", "exp"), None),
    )
    out_specs = (
        P("exp", "seq", None),
        P("exp", "seq", None),
        P(("seq", "exp"), None, None),
        P(("seq", "exp"), None, None),
        P(("seq", "exp"), None),
    )
    return jax.shard_map(local, mesh=mesh, in_specs=in_specs, out_specs=out_specs, check_vma=False)
```

time: 235 us -> 131 us (0.56)
  matrix products: 51.7 us -> 0 us
  local copies, waits for them, and re-layouts: 48.6 us -> 13.1 us
  Pallas kernels: 0 us -> 30.2 us
  blocking collectives: 26.5 us -> 0 us
  other arithmetic: 17.5 us -> 0 us
  waiting for transfers between devices: 57.4 us -> 48.5 us
  starting transfers between devices: 17.4 us -> 24.2 us
    dot_general x14 -> x0, matrix products: 51.7 us -> none  [the longest x1 7.05 us: expert_backward(): jnp.dot(activated.T, out_grad, preferred_element_type=jnp.float32)]
    pallas_call x0 -> x7, Pallas kernels: none -> 30.2 us  [the longest x1 11.4 us: expert(): pl.pallas_call(expert_kernel, grid=(FF // tile,), in_specs=[whole((DEVS *...]
    all_to_all x1 -> x0, blocking collectives: 26.5 us -> none  [deliver(): lax.all_to_all(payload, ('seq', 'exp'), split_axis=0, concat_axis=0, tile...]
    reshape x7 -> x0, local copies, waits for them, and re-layouts: 22.7 us -> none  [the longest x2 6.57 us: restore_rows(): return block.reshape(experts, slot_count, model_width)]
    all_gather x2 -> x1, waiting for transfers between devices: 36.4 us -> 21.1 us  [local(): all_kv = lax.all_gather(kv, 'seq', axis=0, tiled=True)]
    unnamed x35, local copies, waits for them, and re-layouts: 4.59 us -> 13.1 us
    all_to_all x3, waiting for transfers between devices: 20.3 us -> 27.4 us  [deliver(): lax.all_to_all(rows.reshape(DEVS, per, 128), ('seq', 'exp'), split_axis=0...]
    gather x2 -> x0, local copies, waits for them, and re-layouts: 7.05 us -> none  [select(): jnp.take(table, flat_chosen, axis=0)]
  transfers between devices with their start and end apart: 5 -> 4, of which waited for: 5 -> 3; matrix products, arithmetic and copies ran while one was open for 21% -> 0% of each run, Pallas kernels for 0% -> 11%
where the time goes in v1:
time: 131 us
  waiting for transfers between devices  48.5 us (37%)
  Pallas kernels  30.2 us (23%)
  starting transfers between devices  24.2 us (18%)
  between operations  14.8 us (11%)
  local copies, waits for them, and re-layouts  13.1 us (10%)
    all_to_all x3, waiting for transfers between devices, deliver(): lax.all_to_all(rows.reshape(DEVS, per, 128), ('seq', 'exp'), split_axis=0...  27.4 us
    all_to_all x3, starting transfers between devices, deliver(): lax.all_to_all(rows.reshape(DEVS, per, 128), ('seq', 'exp'), split_axis=0...  24.1 us
    all_gather x1, waiting for transfers between devices, local(): all_kv = lax.all_gather(kv, 'seq', axis=0, tiled=True)  21.1 us
    unnamed x35, local copies, waits for them, and re-layouts  13.1 us
    pallas_call x1, Pallas kernels, expert(): pl.pallas_call(expert_kernel, grid=(FF // tile,), in_specs=[whole((DEVS *...  11.4 us
    pallas_call x1, Pallas kernels, attend(): pl.pallas_call(attend_kernel, grid_spec=pltpu.PrefetchScalarGridSpec(num_...  5.16 us
    pallas_call x1, Pallas kernels, weight_grads(): pl.pallas_call(weight_grad_kernel, grid=(FF // tile,), in_specs=[whole((L...  4.51 us
    pallas_call x1, Pallas kernels, prepare(): pl.pallas_call(prepare_kernel, grid=(FF // FF_TILE,), in_specs=[whole((DE...  2.97 us
  transfers between devices with their start and end apart: 4, of which 3 were waited for; matrix products, arithmetic and copies ran while one was open for 0% of the time, Pallas kernels for 11%

profile of v1, /device:TPU:1, one launch (start us, length us, event | category | flops | bytes accessed | tf_op | source)
XLA Modules:
  0.0 130.8 jit_solution(6452931960239748597)
XLA Ops:
  7.2 0.0 copy-start.8
  7.2 0.0 all-gather.2.cloned.1.call-start
  7.2 0.0 copy-start.2
  7.2 1.9 %copy-done.2 = bf16[1024,1536]{1,0:T(8,128)(2,1)S(1)} copy-done((bf16[1024,1536]{1,0:T(8,128)(2,1)S(1)}, bf16[1024,1536]{1,0:T(8,128)(2,1)}, u32[]{:S(2)}) %copy-start.2) | copy-done | bytes 3145752
  9.1 0.0 copy-start.5
  9.1 0.9 copy-done.5
  10.1 0.0 copy-start.16
  10.1 0.0 copy-start.7
  10.1 0.0 copy-start.4
  10.1 0.0 copy-start.6
  10.1 2.4 %shard_map.137 = (bf16[128,1024]{1,0:T(8,128)(2,1)}, bf16[128,512]{1,0:T(8,128)(2,1)S(1)}) custom-call(bf16[128,1024]{1,0:T(8,128)(2,1)S(1)} %bitcast.24, bf16[1024,1536]{1,0:T(8,128)(2,1)S(1)} %copy-done.2), custom_call_target="tpu_custom_call" | custom-call | flops 402653184 | bytes 4194304 | tf_op jit(solution)/shard_map/pallas_call | solution.py:89
  12.5 0.0 all-gather.2.cloned.1.call-update
  12.5 0.0 copy-done.16
  12.5 0.0 copy-done.8
  12.5 0.0 copy-done.7
  12.5 1.4 %shard_map.139 = bf16[3072,128]{1,0:T(8,128)(2,1)} custom-call(bf16[128,1024]{1,0:T(8,128)(2,1)S(1)} %bitcast.26, s32[3,128]{1,0:T(4,128)S(1)} %bitcast.28, s32[1,128]{1,0:T(1,128)S(1)} %copy-done.8), custom_call_target="tpu_custom_call" | custom-call | flops 100663296 | bytes 2097152 | tf_op jit(solution)/shard_map/pallas_call | solution.py:123
  14.0 11.5 %all-to-all-start.1 = ((bf16[128,24,128]{2,1,0:T(8,128)(2,1)}), bf16[128,24,128]{2,1,0:T(8,128)(2,1)S(1)}, u32[]{:S(2)}, u32[]{:S(2)}) async-start(bf16[128,24,128]{2,1,0:T(8,128)(2,1)} %bitcast.5), calls=%async_computation.1 | async-start | bytes 1572864 | tf_op jit(solution)/shard_map/all_to_all | solution.py:426
  26.1 21.1 %all-gather.2.cloned.1.call-done.k_ref.v_ref = bf16[1024,1024]{1,0:T(8,128)(2,1)} async-done(((bf16[128,1024]{1,0:T(8,128)(2,1)}), bf16[1024,1024]{1,0:T(8,128)(2,1)}) %all-gather.2.cloned.1.call-update) | async-done | bytes 2097168 | tf_op jit(solution)/shard_map/all_gather | solution.py:451
  47.2 0.0 copy-done.4
  47.2 0.0 copy-done.6
  47.2 0.0 copy-start.1
  47.2 1.6 %copy-done.1 = bf16[1024,1024]{1,0:T(8,128)(2,1)S(1)} copy-done((bf16[1024,1024]{1,0:T(8,128)(2,1)S(1)}, bf16[1024,1024]{1,0:T(8,128)(2,1)}, u32[]{:S(2)}) %copy-start.1) | copy-done | bytes 2097176
  48.8 5.2 %shard_map.138 = (bf16[128,1024]{1,0:T(8,128)(2,1)S(1)}, bf16[3072,128]{1,0:T(8,128)(2,1)}) custom-call(s32[1]{0:T(128)S(6)} %copy.18.length_ref, bf16[128,512]{1,0:T(8,128)(2,1)S(1)} %get-tuple-element.23.q_ref, bf16[1024,1024]{1,0:T(8,128)(2,1)S(1)} %copy-done.1, bf16[1024,1024]{1,0:T(8,128)(2,1)S(1)} %copy-done.1, bf16[128,1024]{1,0:T(8,128)(2,1)S(1)} %bitcast.25, ...), custom_call_target="tpu_custom_call" | custom-call | flops 536870912 | bytes 5242880 | tf_op jit(solution)/shard_map/pallas_call | solution.py:166
  54.0 0.0 all-to-all-done.1
  54.0 0.0 copy-start.9
  54.0 8.4 %all-to-all-start = ((bf16[128,24,128]{2,1,0:T(8,128)(2,1)}), bf16[128,24,128]{2,1,0:T(8,128)(2,1)S(1)}, u32[]{:S(2)}, u32[]{:S(2)}) async-start(bf16[128,24,128]{2,1,0:T(8,128)(2,1)} %bitcast.2), calls=%async_computation | async-start | bytes 1572864 | tf_op jit(solution)/shard_map/all_to_all | solution.py:426
  62.4 0.0 copy-start
  62.4 2.2 %copy-done = bf16[1,2048,1024]{2,1,0:T(8,128)(2,1)S(1)} copy-done((bf16[1,2048,1024]{2,1,0:T(8,128)(2,1)S(1)}, bf16[1,2048,1024]{2,1,0:T(8,128)(2,1)}, u32[]{:S(2)}) %copy-start) | copy-done | bytes 4194328
  64.5 3.0 %shard_map.140 = (bf16[256,1024]{1,0:T(8,128)(2,1)S(1)}, bf16[384,256]{1,0:T(8,128)(2,1)S(1)}, bf16[256,384]{1,0:T(8,128)(2,1)S(1)}, f32[256,2048]{1,0:T(8,128)S(1)}) custom-call(bf16[3072,128]{1,0:T(8,128)(2,1)S(1)} %bitcast.22, bf16[2048,1024]{1,0:T(8,128)(2,1)S(1)} %bitcast.20), custom_call_target="tpu_custom_call" | custom-call | flops 1073741824 | bytes 8388608 | tf_op jit(solution)/shard_map/pallas_call | solution.py:229
  67.5 0.0 copy-start.3
  67.5 1.3 %copy-done.3 = f32[256,2048]{1,0:T(8,128)} copy-done((f32[256,2048]{1,0:T(8,128)}, f32[256,2048]{1,0:T(8,128)S(1)}, u32[]{:S(2)}) %copy-start.3) | copy-done | bytes 2097176
  68.8 10.2 %all-to-all-done = bf16[128,24,128]{2,1,0:T(8,128)(2,1)S(1)} async-done(((bf16[128,24,128]{2,1,0:T(8,128)(2,1)}), bf16[128,24,128]{2,1,0:T(8,128)(2,1)S(1)}, u32[]{:S(2)}, u32[]{:S(2)}) %all-to-all-start) | async-done | bytes 786464 | tf_op jit(solution)/shard_map/all_to_all | solution.py:426
  79.0 0.0 copy-done.9
  79.0 11.4 %shard_map.141 = (bf16[6144,128]{1,0:T(8,128)(2,1)}, bf16[256,1024]{1,0:T(8,128)(2,1)S(1)}, bf16[256,2048]{1,0:T(8,128)(2,1)S(1)}, bf16[256,2048]{1,0:T(8,128)(2...) custom-call(bf16[3072,128]{1,0:T(8,128)(2,1)S(1)} %bitcast.23, ...), custom_call_target="tpu_custom_call" | custom-call | flops 3221225472 | bytes 14680064 | tf_op jit(solution)/shard_map/pallas_call | solution.py:318
  90.4 0.0 copy-start.10
  90.4 1.0 copy-done.10
  91.4 0.0 copy-start.12
  91.4 1.0 copy-done.12
  92.3 0.0 copy-start.14
  92.3 0.8 copy-done.14
  93.1 4.3 %all-to-all-start.2 = ((bf16[128,48,128]{2,1,0:T(8,128)(2,1)}), bf16[128,48,128]{2,1,0:T(8,128)(2,1)S(1)}, u32[]{:S(2)}, u32[]{:S(2)}) async-start(bf16[128,48,128]{2,1,0:T(8,128)(2,1)} %bitcast.32), calls=%async_computation.2 | async-start | bytes 3145728 | tf_op jit(solution)/shard_map/all_to_all | solution.py:426
  97.4 0.0 copy-done.15
  97.4 0.0 copy-start.11
  97.5 1.2 copy-done.11
  98.7 1.2 copy-done.13
  99.9 4.5 %shard_map.143 = (bf16[1024,2048]{1,0:T(8,128)(2,1)}, bf16[2048,1024]{1,0:T(8,128)(2,1)}) custom-call(bf16[256,1024]{1,0:T(8,128)(2,1)S(1)} %get-tuple-element.34.picked_ref, bf16[256,2048]{1,0:T(8,128)(2,1)S(1)} %copy-done.13, bf16[256,2048]{1,0:T(8,128)(2,1)S(1)} %copy-done.11, bf16[256,1024]{1,0:T(8,128)(2,1)S(1)} %copy-done.15), custom_call_target="tpu_custom_call" | custom-call | flops 2147483648 | bytes 11534336 | tf_op jit(solution)/shard_map/pallas_call | solution.py:368
  104.4 17.3 %all-to-all-done.2 = bf16[128,48,128]{2,1,0:T(8,128)(2,1)S(1)} async-done(((bf16[128,48,128]{2,1,0:T(8,128)(2,1)}), bf16[128,48,128]{2,1,0:T(8,128)(2,1)S(1)}, u32[]{:S(2)}, u32[]{:S(2)}) %all-to-all-start.2) | async-done | bytes 1572896 | tf_op jit(solution)/shard_map/all_to_all | solution.py:426
  121.7 2.3 %shard_map.142 = (bf16[128,1024]{1,0:T(8,128)(2,1)}, bf16[128,1024]{1,0:T(8,128)(2,1)}) custom-call(bf16[6144,128]{1,0:T(8,128)(2,1)S(1)} %bitcast.21, s32[3,128]{1,0:T(4,128)S(1)} %bitcast.30, s32[1,128]{1,0:T(1,128)S(1)} %copy-done.8, bf16[128,1024]{1,0:T(8,128)(2,1)S(1)} %get-tuple-element.31.resid_ref, bf16[128,1024]{1,0:T(8,128)(2,1)S(1)} %bitcast.27), custom_call_target="tpu_custom_call" | custom-call | flops 201326592 | bytes 3145728 | tf_op jit(solution)/shard_map/pallas_call | solution.py:414
  (3 shorter events, 0.0 us)
Async XLA Ops:
  7.2 5.4 %copy-start.8 = (s32[1,128]{1,0:T(1,128)S(1)}, s32[1,128]{1,0:T(1,128)}, u32[]{:S(2)}) copy-start(s32[1,128]{1,0:T(1,128)} %count_ref.5) | copy-start | bytes 1540
  7.2 40.0 %all-gather.2.cloned.1.call-start = ((), (), s32[]{:S(2)}) async-start(), calls=%async_computation.3 | async-start | bytes 2359296 | tf_op jit(solution)/shard_map/all_gather | solution.py:451
  7.2 1.9 %copy-start.2 = (bf16[1024,1536]{1,0:T(8,128)(2,1)S(1)}, bf16[1024,1536]{1,0:T(8,128)(2,1)}, u32[]{:S(2)}) copy-start(bf16[1024,1536]{1,0:T(8,128)(2,1)} %weight_ref.2) | copy-start | bytes 9437188
  9.1 0.9 copy-start.5
  10.1 2.4 %copy-start.16 = (s32[1,128,3]{1,0,2:T(1,128)S(1)}, s32[1,128,3]{1,0,2:T(1,128)}, u32[]{:S(2)}) copy-start(s32[1,128,3]{1,0,2:T(1,128)} %param.18) | copy-start | bytes 4612
  10.1 2.5 %copy-start.7 = (bf16[1,128,1024]{2,1,0:T(8,128)(2,1)S(1)}, bf16[1,128,1024]{2,1,0:T(8,128)(2,1)}, u32[]{:S(2)}) copy-start(bf16[1,128,1024]{2,1,0:T(8,128)(2,1)} %param.11) | copy-start | bytes 786436
  10.1 37.2 %copy-start.4 = (bf16[512,1024]{1,0:T(8,128)(2,1)S(1)}, bf16[512,1024]{1,0:T(8,128)(2,1)}, u32[]{:S(2)}) copy-start(bf16[512,1024]{1,0:T(8,128)(2,1)} %weight_ref.3) | copy-start | bytes 3145732
  10.1 37.2 %copy-start.6 = (bf16[1,128,1024]{2,1,0:T(8,128)(2,1)S(1)}, bf16[1,128,1024]{2,1,0:T(8,128)(2,1)}, u32[]{:S(2)}) copy-start(bf16[1,128,1024]{2,1,0:T(8,128)(2,1)} %param.10) | copy-start | bytes 786436
  14.0 40.0 %all-to-all-start.1 = ((bf16[128,24,128]{2,1,0:T(8,128)(2,1)}), bf16[128,24,128]{2,1,0:T(8,128)(2,1)S(1)}, u32[]{:S(2)}, u32[]{:S(2)}) async-start(bf16[128,24,128]{2,1,0:T(8,128)(2,1)} %bitcast.5), calls=%async_computation.1 | async-start | bytes 1572864 | tf_op jit(solution)/shard_map/all_to_all | solution.py:426
  47.2 1.6 %copy-start.1 = (bf16[1024,1024]{1,0:T(8,128)(2,1)S(1)}, bf16[1024,1024]{1,0:T(8,128)(2,1)}, u32[]{:S(2)}) copy-start(bf16[1024,1024]{1,0:T(8,128)(2,1)} %all-gather.2.cloned.1.call-done.k_ref.v_ref) | copy-start | bytes 6291460
  54.0 25.0 %copy-start.9 = (f32[1,1024]{1,0:T(1,128)S(1)}, f32[1,1024]{1,0:T(1,128)}, u32[]{:S(2)}) copy-start(f32[1,1024]{1,0:T(1,128)} %router_ref.1) | copy-start | bytes 12292
  54.0 25.0 %all-to-all-start = ((bf16[128,24,128]{2,1,0:T(8,128)(2,1)}), bf16[128,24,128]{2,1,0:T(8,128)(2,1)S(1)}, u32[]{:S(2)}, u32[]{:S(2)}) async-start(bf16[128,24,128]{2,1,0:T(8,128)(2,1)} %bitcast.2), calls=%async_computation | async-start | bytes 1572864 | tf_op jit(solution)/shard_map/all_to_all | solution.py:426
  62.4 2.2 %copy-start = (bf16[1,2048,1024]{2,1,0:T(8,128)(2,1)S(1)}, bf16[1,2048,1024]{2,1,0:T(8,128)(2,1)}, u32[]{:S(2)}) copy-start(bf16[1,2048,1024]{2,1,0:T(8,128)(2,1)} %param.17) | copy-start | bytes 12582916
  67.5 1.3 %copy-start.3 = (f32[256,2048]{1,0:T(8,128)}, f32[256,2048]{1,0:T(8,128)S(1)}, u32[]{:S(2)}) copy-start(f32[256,2048]{1,0:T(8,128)S(1)} %get-tuple-element.29.pulled_ref) | copy-start | bytes 6291460
  90.4 1.0 copy-start.10
  91.4 1.0 copy-start.12
  92.3 0.8 copy-start.14
  93.1 4.3 %copy-start.15 = (bf16[256,1024]{1,0:T(8,128)(2,1)S(1)}, bf16[256,1024]{1,0:T(8,128)(2,1)}, u32[]{:S(2)}) copy-start(bf16[256,1024]{1,0:T(8,128)(2,1)} %copy-done.14) | copy-start | bytes 1572868
  93.1 28.5 %all-to-all-start.2 = ((bf16[128,48,128]{2,1,0:T(8,128)(2,1)}), bf16[128,48,128]{2,1,0:T(8,128)(2,1)S(1)}, u32[]{:S(2)}, u32[]{:S(2)}) async-start(bf16[128,48,128]{2,1,0:T(8,128)(2,1)} %bitcast.32), calls=%async_computation.2 | async-start | bytes 3145728 | tf_op jit(solution)/shard_map/all_to_all | solution.py:426
  97.4 1.2 copy-start.11
  98.7 1.2 copy-start.13
Sparse Core Ops, SparseCore 0:
  12.6 34.5 all-gather.1

commit v2 on v1

v2 whole, which is shorter than its diff:
```python
import jax
import jax.numpy as jnp
from jax import lax
from jax.experimental import pallas as pl
from jax.experimental.pallas import tpu as pltpu
from jax.sharding import PartitionSpec as P

HEADS = 8
HD = 64
D = 1024
FF = 2048
FR = 128
DEVS = 128
SLOT = 3
KEYS = 1024
LIVE = 256
TILES = D // 128
ROWS = SLOT * TILES

epsilon = 1e-05
masked_score = -1e30
empty_mark = 2.0**100
empty_bound = 2.0**99

F32 = jnp.float32
BF16 = jnp.bfloat16
MB = 1024 * 1024


def params(mib):
    return pltpu.CompilerParams(vmem_limit_bytes=mib * MB)


def whole(shape):
    return pl.BlockSpec(shape, lambda *_: (0,) * len(shape))


def dot(a, b, dims=((1,), (0,))):
    return lax.dot_general(a, b, (dims, ((), ())), preferred_element_type=F32)


def normalize(values):
    center = jnp.mean(values, axis=-1, keepdims=True)
    shifted = values - center
    spread = jnp.mean(jnp.square(shifted), axis=-1, keepdims=True)
    inverse = lax.rsqrt(spread + epsilon)
    return shifted * inverse, inverse


def spread_matrix(index_ref, count_ref, slot):
    frame = lax.broadcasted_iota(jnp.int32, (FR, DEVS), 0)
    named = jnp.broadcast_to(index_ref[slot : slot + 1, :], (FR, DEVS)) == frame
    used = jnp.broadcast_to(count_ref[...], (FR, DEVS)) > slot
    return jnp.where(named & used, 1.0, 0.0)


def pack_rows(stage, rows, per, first):
    for tile in range(TILES):
        stage[pl.ds(first + tile, DEVS, stride=per), :] = rows[:, tile * 128 : (tile + 1) * 128]


def unpack_rows(stage, per, first):
    return jnp.concatenate(
        [stage[pl.ds(first + tile, DEVS, stride=per), :] for tile in range(TILES)], axis=1
    )


PART = HD * 3
HALF = HEADS * HD


def project_kernel(frames_ref, weight_ref, out_ref, normed):
    step = pl.program_id(0)

    @pl.when(step == 0)
    def _():
        normed[...] = normalize(frames_ref[...].astype(F32))[0].astype(BF16)

    block = dot(normed[...], weight_ref[...]).T.astype(BF16)
    for head in range(HEADS):
        start = pl.multiple_of(head * PART + step * HD, HD)
        out_ref[pl.ds(start, HD), :] = block[head * HD : (head + 1) * HD]


def project(frames, weight):
    return pl.pallas_call(
        project_kernel,
        grid=(3,),
        in_specs=[whole((FR, D)), pl.BlockSpec((D, HALF), lambda n: (0, n))],
        out_specs=whole((HEADS * PART, FR)),
        out_shape=jax.ShapeDtypeStruct((HEADS * PART, FR), BF16),
        scratch_shapes=[pltpu.VMEM((FR, D), BF16)],
        compiler_params=params(56),
        cost_estimate=pl.CostEstimate(
            flops=2 * FR * D * 3 * HALF, bytes_accessed=4 * MB, transcendentals=0
        ),
    )(frames, weight)


def staged(stage):
    return stage[...].reshape(DEVS, 1, ROWS, 128).astype(BF16)


def gather_kernel(table_ref, index_ref, count_ref, out_ref, stage):
    count_column = jnp.broadcast_to(count_ref[...].astype(F32), (DEVS, DEVS)).T
    for slot in range(SLOT):
        pick = spread_matrix(index_ref, count_ref, slot).T.astype(BF16)
        rows = dot(pick, table_ref[...])
        mark = jnp.where(count_column[:, 0:1] > slot, 0.0, empty_mark)
        pack_rows(stage, rows + mark, ROWS, slot * TILES)
    out_ref[...] = staged(stage)


def gather_rows(table, index, count):
    return pl.pallas_call(
        gather_kernel,
        grid=(1,),
        in_specs=[whole((FR, D)), whole((SLOT, DEVS)), whole((1, DEVS))],
        out_specs=pl.BlockSpec((DEVS, 1, ROWS, 128), lambda n: (0, 1, 0, 0)),
        out_shape=jax.ShapeDtypeStruct((DEVS, 2, ROWS, 128), BF16),
        scratch_shapes=[pltpu.VMEM((DEVS * ROWS, 128), F32)],
        compiler_params=params(20),
        cost_estimate=pl.CostEstimate(
            flops=2 * DEVS * SLOT * FR * D, bytes_accessed=2 * MB, transcendentals=0
        ),
    )(table, index, count)


QUERIES = 256


def attend_kernel(length_ref, parts_ref, out_ref):
    parts = [parts_ref[s * PART : (s + 1) * PART, :] for s in range(HEADS)]
    q = jnp.concatenate([part[:HD] for part in parts], axis=1)
    k = jnp.concatenate([part[HD : 2 * HD] for part in parts], axis=1).astype(F32)
    k = (k * HD ** (-0.5)).T.astype(BF16)
    v = jnp.concatenate([part[2 * HD :] for part in parts], axis=1)
    live = lax.broadcasted_iota(jnp.int32, (KEYS, QUERIES), 0) < length_ref[0]
    for first in range(0, KEYS, QUERIES):
        scores = dot(k, q[:, first : first + QUERIES])
        scores = jnp.where(live, scores, masked_score)
        top = jnp.max(scores, axis=0, keepdims=True)
        weights = jnp.exp(scores - top)
        total = jnp.sum(weights, axis=0, keepdims=True)
        mixed = (dot(v, weights.astype(BF16)) / total).astype(BF16)
        for piece in range(QUERIES // FR):
            source = first // FR + piece
            out_ref[source * HD : (source + 1) * HD, :] = mixed[:, piece * FR : (piece + 1) * FR]


def attend(length, parts):
    return pl.pallas_call(
        attend_kernel,
        in_specs=[
            pl.BlockSpec(memory_space=pltpu.SMEM),
            pl.BlockSpec(memory_space=pltpu.VMEM),
        ],
        out_shape=jax.ShapeDtypeStruct((HALF, FR), BF16),
        compiler_params=params(24),
        cost_estimate=pl.CostEstimate(
            flops=4 * KEYS * KEYS * HD, bytes_accessed=MB // 2, transcendentals=KEYS * KEYS
        ),
    )(length, parts)


def residual_kernel(
    attended_ref, frames_ref, weight_ref, index_ref, count_ref, packed_ref,
    resid_ref, out_ref, stage,
):
    attended = attended_ref[...].astype(F32).T.astype(BF16)
    resid = (frames_ref[...].astype(F32) + dot(attended, weight_ref[...])).astype(BF16)
    resid_ref[...] = resid
    mid = normalize(resid.astype(F32))[0].astype(BF16)
    for slot in range(SLOT):
        pick = spread_matrix(index_ref, count_ref, slot).T.astype(BF16)
        pack_rows(stage, dot(pick, mid), ROWS, slot * TILES)
    out_ref[...] = staged(stage)


def residual(attended, frames, weight, index, count, packed):
    return pl.pallas_call(
        residual_kernel,
        grid=(1,),
        in_specs=[
            whole((HALF, FR)),
            whole((FR, D)),
            whole((HALF, D)),
            whole((SLOT, DEVS)),
            whole((1, DEVS)),
            pl.BlockSpec(memory_space=pl.ANY),
        ],
        out_specs=[
            whole((FR, D)),
            pl.BlockSpec((DEVS, 1, ROWS, 128), lambda n: (0, 0, 0, 0)),
        ],
        out_shape=[
            jax.ShapeDtypeStruct((FR, D), BF16),
            jax.ShapeDtypeStruct((DEVS, 2, ROWS, 128), BF16),
        ],
        input_output_aliases={5: 1},
        scratch_shapes=[pltpu.VMEM((DEVS * ROWS, 128), F32)],
        compiler_params=params(24),
        cost_estimate=pl.CostEstimate(
            flops=2 * FR * HALF * D + 2 * DEVS * SLOT * FR * D,
            bytes_accessed=3 * MB, transcendentals=0,
        ),
    )(attended, frames, weight, index, count, packed)


FF_TILE = 512
D_TILE = 256
FF_STEPS = FF // FF_TILE
gelu_scale = (2.0 / jnp.pi) ** 0.5
gelu_cubic = 0.044715


def seats(first_column):
    total = SLOT * DEVS
    live = first_column < empty_bound
    ahead = lax.broadcasted_iota(jnp.int32, (total, total), 0) >= lax.broadcasted_iota(
        jnp.int32, (total, total), 1
    )
    ranks = dot(jnp.where(ahead, 1.0, 0.0).astype(BF16), jnp.where(live, 1.0, 0.0).astype(BF16))
    seat = jnp.where(live, ranks - 1.0, -1.0)[:, 0:1].astype(jnp.int32)
    return jnp.where(seat == lax.broadcasted_iota(jnp.int32, (total, LIVE), 1), 1.0, 0.0)


def expert_kernel(
    rows_ref, first_hbm, second_hbm, router_ref,
    back_ref, picked_ref, active_ref, before_grad_ref, out_grad_ref, route_grad_ref,
    stage, first_ref, second_ref, first_sem, second_sem,
):
    loads = []
    for step in range(FF_STEPS):
        columns = pl.ds(step * FF_TILE, FF_TILE)
        loads.append((
            pltpu.make_async_copy(
                first_hbm.at[:, columns], first_ref.at[:, columns], first_sem.at[step]
            ),
            pltpu.make_async_copy(
                second_hbm.at[columns, :], second_ref.at[columns, :], second_sem.at[step]
            ),
        ))
    for pair in loads:
        for load in pair:
            load.start()

    stage[...] = rows_ref[...].astype(F32).reshape(DEVS * 2 * ROWS, 128)
    grads = [unpack_rows(stage, 2 * ROWS, ROWS + slot * TILES) for slot in range(SLOT)]
    grads = jnp.concatenate(grads, axis=0)
    place = seats(grads[:, 0:128])
    take = place.T.astype(BF16)
    place = place.astype(BF16)
    grads = dot(take, grads.astype(BF16)).astype(BF16)
    rows = [unpack_rows(stage, 2 * ROWS, slot * TILES).astype(BF16) for slot in range(SLOT)]
    picked_wide = dot(take, jnp.concatenate(rows, axis=0))
    picked = picked_wide.astype(BF16)
    picked_ref[...] = picked
    logits = jnp.sum(picked_wide * router_ref[...], axis=-1, keepdims=True)
    gate = 1.0 / (1.0 + jnp.exp(-logits))
    out_grad_ref[...] = (gate * grads.astype(F32)).astype(BF16)

    logit = jnp.zeros((LIVE, 1), F32)
    for step in range(FF_STEPS):
        columns = pl.ds(step * FF_TILE, FF_TILE)
        loads[step][0].wait()
        before = dot(picked, first_ref[:, columns])
        loads[step][1].wait()
        pulled = dot(grads, second_ref[columns, :], ((1,), (1,)))
        square = before * before
        bend = jnp.tanh(before * (gelu_scale + (gelu_scale * gelu_cubic) * square))
        half = 0.5 + 0.5 * bend
        active = (before * half).astype(BF16)
        slope = half + (before * (1.0 - bend * bend)) * (
            0.5 * gelu_scale + (1.5 * gelu_scale * gelu_cubic) * square
        )
        active_ref[:, columns] = active
        before_grad_ref[:, columns] = (gate * pulled * slope).astype(BF16)
        logit += jnp.sum(active.astype(F32) * pulled, axis=-1, keepdims=True)

    logit_grad = logit * gate * (1.0 - gate)
    route_grad_ref[...] = jnp.sum(logit_grad * picked_ref[...].astype(F32), axis=0, keepdims=True)
    for start in range(0, D, D_TILE):
        columns = pl.ds(start, D_TILE)
        result = dot(active_ref[...], second_ref[:, columns])
        returned = dot(place, (gate * result).astype(BF16))
        row_grad = dot(before_grad_ref[...], first_ref[columns, :], ((1,), (1,)))
        row_grad = row_grad + logit_grad * router_ref[:, columns]
        row_grad = dot(place, row_grad.astype(BF16))
        for slot in range(SLOT):
            sources = slice(slot * DEVS, (slot + 1) * DEVS)
            for tile in range(D_TILE // 128):
                lanes = slice(tile * 128, (tile + 1) * 128)
                at = slot * TILES + start // 128 + tile
                stage[pl.ds(at, DEVS, stride=2 * ROWS), :] = returned[sources, lanes]
                stage[pl.ds(ROWS + at, DEVS, stride=2 * ROWS), :] = row_grad[sources, lanes]
    back_ref[...] = stage[...].reshape(DEVS, 2, ROWS, 128).astype(BF16)


def expert(rows, first, second, router):
    vmem = pl.BlockSpec(memory_space=pltpu.VMEM)
    hbm = pl.BlockSpec(memory_space=pl.ANY)
    return pl.pallas_call(
        expert_kernel,
        in_specs=[vmem, hbm, hbm, vmem],
        out_specs=[vmem] * 6,
        out_shape=[
            jax.ShapeDtypeStruct((DEVS, 2, ROWS, 128), BF16),
            jax.ShapeDtypeStruct((LIVE, D), BF16),
            jax.ShapeDtypeStruct((LIVE, FF), BF16),
            jax.ShapeDtypeStruct((LIVE, FF), BF16),
            jax.ShapeDtypeStruct((LIVE, D), BF16),
            jax.ShapeDtypeStruct((1, D), F32),
        ],
        scratch_shapes=[
            pltpu.VMEM((DEVS * ROWS * 2, 128), F32),
            pltpu.VMEM((D, FF), BF16),
            pltpu.VMEM((FF, D), BF16),
            pltpu.SemaphoreType.DMA((FF_STEPS,)),
            pltpu.SemaphoreType.DMA((FF_STEPS,)),
        ],
        compiler_params=params(56),
        cost_estimate=pl.CostEstimate(
            flops=8 * LIVE * D * FF, bytes_accessed=14 * MB, transcendentals=LIVE * FF
        ),
    )(rows, first, second, router)


def weight_grad_kernel(picked_ref, before_grad_ref, active_ref, out_grad_ref, first_ref, second_ref):
    first_ref[...] = dot(picked_ref[...], before_grad_ref[...], ((0,), (0,))).astype(BF16)
    second_ref[...] = dot(active_ref[...], out_grad_ref[...], ((0,), (0,))).astype(BF16)


def weight_grads(picked, before_grad, active, out_grad):
    tile = FF_TILE
    return pl.pallas_call(
        weight_grad_kernel,
        grid=(FF // tile,),
        in_specs=[
            whole((LIVE, D)),
            pl.BlockSpec((LIVE, tile), lambda n: (0, n)),
            pl.BlockSpec((LIVE, tile), lambda n: (0, n)),
            whole((LIVE, D)),
        ],
        out_specs=[
            pl.BlockSpec((D, tile), lambda n: (0, n)),
            pl.BlockSpec((tile, D), lambda n: (n, 0)),
        ],
        out_shape=[
            jax.ShapeDtypeStruct((D, FF), BF16),
            jax.ShapeDtypeStruct((FF, D), BF16),
        ],
        compiler_params=params(24),
        cost_estimate=pl.CostEstimate(
            flops=4 * LIVE * D * FF, bytes_accessed=11 * MB, transcendentals=0
        ),
    )(picked, before_grad, active, out_grad)


def combine_kernel(
    rows_ref, index_ref, count_ref, resid_ref, upstream_ref, output_ref, grad_ref, stage
):
    stage[...] = rows_ref[...].astype(F32).reshape(DEVS * 2 * ROWS, 128)
    mixture = jnp.zeros((FR, D), F32)
    normed_grad = jnp.zeros((FR, D), F32)
    for slot in range(SLOT):
        spread = spread_matrix(index_ref, count_ref, slot).astype(BF16)
        rows = unpack_rows(stage, 2 * ROWS, slot * TILES).astype(BF16)
        mixture += dot(spread, rows)
        rows = unpack_rows(stage, 2 * ROWS, ROWS + slot * TILES).astype(BF16)
        normed_grad += dot(spread, rows)
    resid = resid_ref[...].astype(F32)
    output_ref[...] = (resid + mixture).astype(BF16)
    unit, inverse = normalize(resid)
    first_mean = jnp.mean(normed_grad, axis=-1, keepdims=True)
    second_mean = jnp.mean(normed_grad * unit, axis=-1, keepdims=True)
    grad = inverse * (normed_grad - first_mean - unit * second_mean)
    grad_ref[...] = (upstream_ref[...].astype(F32) + grad).astype(BF16)


def combine(rows, index, count, resid, upstream):
    return pl.pallas_call(
        combine_kernel,
        out_shape=[jax.ShapeDtypeStruct((FR, D), BF16)] * 2,
        scratch_shapes=[pltpu.VMEM((DEVS * ROWS * 2, 128), F32)],
        compiler_params=params(28),
        cost_estimate=pl.CostEstimate(
            flops=4 * DEVS * SLOT * FR * D, bytes_accessed=3 * MB, transcendentals=0
        ),
    )(rows, index, count, resid, upstream)


def exchange(rows, axes):
    return lax.all_to_all(rows, axes, split_axis=0, concat_axis=0, tiled=True)


def local(
    frames,
    cotangent,
    lengths,
    qkv_weight,
    out_weight,
    router,
    expert_in,
    expert_out,
    send_index,
    send_count,
):
    own_frames = frames[0]
    upstream = cotangent[0]
    index = send_index[0].T
    everywhere = ("seq", "exp")

    parts = project(own_frames, qkv_weight).reshape(HEADS, PART, FR)
    parts = exchange(parts, "seq").reshape(HEADS * PART, FR)
    packed = gather_rows(upstream, index, send_count)
    attended = attend(lengths, parts).reshape(HEADS, HD, FR)
    attended = exchange(attended, "seq").reshape(HALF, FR)
    resid, packed = residual(attended, own_frames, out_weight, index, send_count, packed)
    arrived = exchange(packed, everywhere)
    back, picked, active, before_grad, out_grad, grad_route = expert(
        arrived, expert_in[0], expert_out[0], router
    )
    arrived_back = exchange(back, everywhere)
    grad_first, grad_second = weight_grads(picked, before_grad, active, out_grad)
    output, grad_resid = combine(arrived_back, index, send_count, resid, upstream)
    return (output[None], grad_resid[None], grad_first[None], grad_second[None], grad_route)


def solution(mesh):
    in_specs = (
        P("exp", "seq", None),
        P("exp", "seq", None),
        P("exp"),
        P(),
        P(),
        P(("seq", "exp"), None),
        P(("seq", "exp"), None, None),
        P(("seq", "exp"), None, None),
        P(("seq", "exp"), None, None),
        P(("seq", "exp"), None),
    )
    out_specs = (
        P("exp", "seq", None),
        P("exp", "seq", None),
        P(("seq", "exp"), None, None),
        P(("seq", "exp"), None, None),
        P(("seq", "exp"), None),
    )
    return jax.shard_map(local, mesh=mesh, in_specs=in_specs, out_specs=out_specs, check_vma=False)
```

time: 131 us -> 114 us (0.87)
  blocking collectives: 0 us -> 33 us
  waiting for transfers between devices: 48.5 us -> 28.5 us
  between operations: 14.8 us -> 1.38 us
  local copies, waits for them, and re-layouts: 13.1 us -> 3.33 us
  starting transfers between devices: 24.2 us -> 15.1 us
  Pallas kernels: 30.2 us -> 32.2 us
    all_to_all x0 -> x1, blocking collectives: none -> 33 us  [exchange(): return lax.all_to_all(rows, axes, split_axis=0, concat_axis=0, tiled=True)]
    all_gather x1 -> x0, waiting for transfers between devices: 21.1 us -> none  [local(): all_kv = lax.all_gather(kv, 'seq', axis=0, tiled=True)]
    unnamed x35 -> x19, local copies, waits for them, and re-layouts: 13.1 us -> 3.33 us
    all_to_all x3, starting transfers between devices: 24.1 us -> 15.1 us  [exchange(): return lax.all_to_all(rows, axes, split_axis=0, concat_axis=0, tiled=True)]
    pallas_call x1, Pallas kernels: 2.4 us -> 4.34 us  [project(): pl.pallas_call(project_kernel, grid=(3,), in_specs=[whole((FR, D)), pl.Bl...]
  transfers between devices with their start and end apart: 4 -> 3, of which waited for: 3 -> 3; matrix products, arithmetic and copies ran while one was open for 0% -> 0% of each run, Pallas kernels for 11% -> 5%
where the time goes in v2:
time: 114 us; the launch traced here: 113 us
  blocking collectives  33 us (29%)
  Pallas kernels  32.2 us (28%)
  waiting for transfers between devices  28.5 us (25%)
  starting transfers between devices  15.1 us (13%)
  local copies, waits for them, and re-layouts  3.33 us (3%)
  between operations  1.38 us (1%)
    all_to_all x1, blocking collectives, exchange(): return lax.all_to_all(rows, axes, split_axis=0, concat_axis=0, tiled=True)  33 us
    all_to_all x3, waiting for transfers between devices, exchange(): return lax.all_to_all(rows, axes, split_axis=0, concat_axis=0, tiled=True)  28.5 us
    pallas_call x1, Pallas kernels, expert(): pl.pallas_call(expert_kernel, in_specs=[vmem, hbm, hbm, vmem], out_specs=...  15.7 us
    all_to_all x3, starting transfers between devices, exchange(): return lax.all_to_all(rows, axes, split_axis=0, concat_axis=0, tiled=True)  15.1 us
    pallas_call x1, Pallas kernels, weight_grads(): pl.pallas_call(weight_grad_kernel, grid=(FF // tile,), in_specs=[whole((L...  4.49 us
    pallas_call x1, Pallas kernels, project(): pl.pallas_call(project_kernel, grid=(3,), in_specs=[whole((FR, D)), pl.Bl...  4.34 us
    pallas_call x1, Pallas kernels, attend(): pl.pallas_call(attend_kernel, in_specs=[pl.BlockSpec(memory_space=pltpu.S...  3.57 us
    unnamed x19, local copies, waits for them, and re-layouts  3.33 us
  transfers between devices with their start and end apart: 3, of which 3 were waited for; matrix products, arithmetic and copies ran while one was open for 0% of the time, Pallas kernels for 5%

profile of v2, /device:TPU:1, one launch (start us, length us, event | category | flops | bytes accessed | tf_op | source)
XLA Modules:
  0.0 113.4 jit_solution(3401108052560017518)
XLA Ops:
  0.6 0.0 copy-start.8
  0.6 0.0 copy-start.1
  0.7 0.0 copy-start.3
  0.7 4.3 %shard_map.137 = bf16[1536,128]{1,0:T(8,128)(2,1)} custom-call(bf16[128,1024]{1,0:T(8,128)(2,1)} %bitcast.19, bf16[1024,1536]{1,0:T(8,128)(2,1)} %weight_ref.2), custom_call_target="tpu_custom_call" | custom-call | flops 402653184 | bytes 4194304 | tf_op jit(solution)/shard_map/pallas_call | solution.py:86
  5.0 0.0 copy-start
  5.0 0.0 copy-start.2
  5.0 5.9 %all-to-all-start = ((bf16[8,192,128]{2,1,0:T(8,128)(2,1)}), bf16[8,192,128]{2,1,0:T(8,128)(2,1)S(1)}, u32[]{:S(2)}, u32[]{:S(2)}) async-start(bf16[8,192,128]{2,1,0:T(8,128)(2,1)} %bitcast.26), calls=%async_computation | async-start | bytes 786432 | tf_op jit(solution)/shard_map/all_to_all | solution.py:394
  11.6 7.4 %all-to-all-done = bf16[8,192,128]{2,1,0:T(8,128)(2,1)S(1)} async-done(((bf16[8,192,128]{2,1,0:T(8,128)(2,1)}), bf16[8,192,128]{2,1,0:T(8,128)(2,1)S(1)}, u32[]{:S(2)}, u32[]{:S(2)}) %all-to-all-start) | async-done | bytes 393248 | tf_op jit(solution)/shard_map/all_to_all | solution.py:394
  19.0 3.6 %shard_map.138 = bf16[512,128]{1,0:T(8,128)(2,1)} custom-call(s32[1]{0:T(128)S(6)} %copy.20.length_ref, bf16[1536,128]{1,0:T(8,128)(2,1)S(1)} %bitcast.22), custom_call_target="tpu_custom_call" | custom-call | flops 268435456 | bytes 524288 | tf_op jit(solution)/shard_map/pallas_call | solution.py:152
  22.6 4.1 %all-to-all-start.1 = ((bf16[8,64,128]{2,1,0:T(8,128)(2,1)}), bf16[8,64,128]{2,1,0:T(8,128)(2,1)S(1)}, u32[]{:S(2)}, u32[]{:S(2)}) async-start(bf16[8,64,128]{2,1,0:T(8,128)(2,1)} %bitcast.3), calls=%async_computation.1 | async-start | bytes 262144 | tf_op jit(solution)/shard_map/all_to_all | solution.py:394
  26.7 0.0 copy-done.8
  26.7 0.0 copy-done.1
  26.7 0.0 copy-done.3
  26.8 0.6 shard_map.139.packed_ref
  27.4 4.7 %all-to-all-done.1 = bf16[8,64,128]{2,1,0:T(8,128)(2,1)S(1)} async-done(((bf16[8,64,128]{2,1,0:T(8,128)(2,1)}), bf16[8,64,128]{2,1,0:T(8,128)(2,1)S(1)}, u32[]{:S(2)}, u32[]{:S(2)}) %all-to-all-start.1) | async-done | bytes 131104 | tf_op jit(solution)/shard_map/all_to_all | solution.py:394
  32.0 0.0 copy-done
  32.0 0.0 copy-done.2
  32.0 1.1 shard_map.140
  33.2 33.0 %all_to_all.20.rows_ref = bf16[128,2,24,128]{3,2,1,0:T(8,128)(2,1)} all-to-all(bf16[128,2,24,128]{3,2,1,0:T(8,128)(2,1)S(1)} %get-tuple-element.17), channel_id=1, replica_groups=mesh['seq'=8,'exp'=16] {'seq','exp'}, dimensions={0} | all-to-all | bytes 3145728 | tf_op jit(solution)/shard_map/all_to_all | solution.py:394
  66.2 15.7 %shard_map.141 = (bf16[128,2,24,128]{3,2,1,0:T(8,128)(2,1)}, bf16[256,1024]{1,0:T(8,128)(2,1)}, bf16[256,2048]{1,0:T(8,128)(2,1)}, bf16[256,2048]{1,0:T(8,128)(2...) custom-call(bf16[128,2,24,128]{3,2,1,0:T(8,128)(2,1)} %all_to_all.20.rows_ref, bf16[1024,2048]{1,0:T(8,128)(2,1)} %bitcast.27, ...), custom_call_target="tpu_custom_call" | custom-call | flops 4294967296 | bytes 14680064 | tf_op jit(solution)/shard_map/pallas_call | solution.py:303
  81.9 0.0 copy-start.4
  81.9 5.0 %all-to-all-start.3 = ((bf16[128,2,24,128]{3,2,1,0:T(8,128)(2,1)}), bf16[128,2,24,128]{3,2,1,0:T(8,128)(2,1)S(1)}, u32[]{:S(2)}, u32[]{:S(2)}) async-start(bf16[128,2,24,128]{3,2,1,0:T(8,128)(2,1)} %get-tuple-element.18), calls=%async_computation.3 | async-start | bytes 3145728 | tf_op jit(solution)/shard_map/all_to_all | solution.py:394
  86.9 0.0 copy-done.4
  86.9 0.0 copy-start.5
  86.9 1.2 %copy-done.5 = bf16[256,2048]{1,0:T(8,128)(2,1)S(1)} copy-done((bf16[256,2048]{1,0:T(8,128)(2,1)S(1)}, bf16[256,2048]{1,0:T(8,128)(2,1)}, u32[]{:S(2)}) %copy-start.5) | copy-done | bytes 1048600
  88.1 0.0 copy-start.6
  88.1 1.0 copy-done.6
  89.2 0.0 copy-start.7
  89.2 1.0 copy-done.7
  90.2 4.5 %shard_map.143 = (bf16[1024,2048]{1,0:T(8,128)(2,1)}, bf16[2048,1024]{1,0:T(8,128)(2,1)}) custom-call(bf16[256,1024]{1,0:T(8,128)(2,1)S(1)} %copy-done.6, bf16[256,2048]{1,0:T(8,128)(2,1)S(1)} %copy-done.5, bf16[256,2048]{1,0:T(8,128)(2,1)S(1)} %copy-done.4, bf16[256,1024]{1,0:T(8,128)(2,1)S(1)} %copy-done.7), custom_call_target="tpu_custom_call" | custom-call | flops 2147483648 | bytes 11534336 | tf_op jit(solution)/shard_map/pallas_call | solution.py:336
  94.7 16.4 %all-to-all-done.3.rows_ref = bf16[128,2,24,128]{3,2,1,0:T(8,128)(2,1)S(1)} async-done(((bf16[128,2,24,128]{3,2,1,0:T(8,128)(2,1)}), bf16[128,2,24,128]{3,2,1,0:T(8,128)(2,1)S(1)}, u32[]{:S(2)}, u32[]{:S(2)}) %all-to-all-start.3) | async-done | bytes 1572896 | tf_op jit(solution)/shard_map/all_to_all | solution.py:394
  111.1 2.3 %shard_map.142 = (bf16[128,1024]{1,0:T(8,128)(2,1)}, bf16[128,1024]{1,0:T(8,128)(2,1)}) custom-call(bf16[128,2,24,128]{3,2,1,0:T(8,128)(2,1)S(1)} %all-to-all-done.3.rows_ref, s32[3,128]{1,0:T(4,128)S(1)} %bitcast.25, s32[1,128]{1,0:T(1,128)S(1)} %copy-done.3, bf16[128,1024]{1,0:T(8,128)(2,1)S(1)} %get-tuple-element.19.resid_ref, bf16[128,1024]{1,0:T(8,128)(2,1)S(1)} %bitcast.18), custom_call_target="tpu_custom_call" | custom-call | flops 201326592 | bytes 3145728 | tf_op jit(solution)/shard_map/pallas_call | solution.py:382
  (1 shorter events, 0.0 us)
Async XLA Ops:
  0.6 26.1 %copy-start.8 = (s32[1,128,3]{1,0,2:T(1,128)S(1)}, s32[1,128,3]{1,0,2:T(1,128)}, u32[]{:S(2)}) copy-start(s32[1,128,3]{1,0,2:T(1,128)} %param.18) | copy-start | bytes 4612
  0.6 26.1 %copy-start.1 = (bf16[1,128,1024]{2,1,0:T(8,128)(2,1)S(1)}, bf16[1,128,1024]{2,1,0:T(8,128)(2,1)}, u32[]{:S(2)}) copy-start(bf16[1,128,1024]{2,1,0:T(8,128)(2,1)} %param.11) | copy-start | bytes 786436
  0.7 26.1 %copy-start.3 = (s32[1,128]{1,0:T(1,128)S(1)}, s32[1,128]{1,0:T(1,128)}, u32[]{:S(2)}) copy-start(s32[1,128]{1,0:T(1,128)} %count_ref.5) | copy-start | bytes 1540
  5.0 27.0 %copy-start = (bf16[512,1024]{1,0:T(8,128)(2,1)S(1)}, bf16[512,1024]{1,0:T(8,128)(2,1)}, u32[]{:S(2)}) copy-start(bf16[512,1024]{1,0:T(8,128)(2,1)} %weight_ref.3) | copy-start | bytes 3145732
  5.0 27.0 %copy-start.2 = (bf16[1,128,1024]{2,1,0:T(8,128)(2,1)S(1)}, bf16[1,128,1024]{2,1,0:T(8,128)(2,1)}, u32[]{:S(2)}) copy-start(bf16[1,128,1024]{2,1,0:T(8,128)(2,1)} %param.10) | copy-start | bytes 786436
  5.0 14.0 %all-to-all-start = ((bf16[8,192,128]{2,1,0:T(8,128)(2,1)}), bf16[8,192,128]{2,1,0:T(8,128)(2,1)S(1)}, u32[]{:S(2)}, u32[]{:S(2)}) async-start(bf16[8,192,128]{2,1,0:T(8,128)(2,1)} %bitcast.26), calls=%async_computation | async-start | bytes 786432 | tf_op jit(solution)/shard_map/all_to_all | solution.py:394
  22.6 9.4 %all-to-all-start.1 = ((bf16[8,64,128]{2,1,0:T(8,128)(2,1)}), bf16[8,64,128]{2,1,0:T(8,128)(2,1)S(1)}, u32[]{:S(2)}, u32[]{:S(2)}) async-start(bf16[8,64,128]{2,1,0:T(8,128)(2,1)} %bitcast.3), calls=%async_computation.1 | async-start | bytes 262144 | tf_op jit(solution)/shard_map/all_to_all | solution.py:394
  81.9 5.0 %copy-start.4 = (bf16[256,2048]{1,0:T(8,128)(2,1)S(1)}, bf16[256,2048]{1,0:T(8,128)(2,1)}, u32[]{:S(2)}) copy-start(bf16[256,2048]{1,0:T(8,128)(2,1)} %get-tuple-element.24.active_ref) | copy-start | bytes 3145732
  81.9 29.2 %all-to-all-start.3 = ((bf16[128,2,24,128]{3,2,1,0:T(8,128)(2,1)}), bf16[128,2,24,128]{3,2,1,0:T(8,128)(2,1)S(1)}, u32[]{:S(2)}, u32[]{:S(2)}) async-start(bf16[128,2,24,128]{3,2,1,0:T(8,128)(2,1)} %get-tuple-element.18), calls=%async_computation.3 | async-start | bytes 3145728 | tf_op jit(solution)/shard_map/all_to_all | solution.py:394
  86.9 1.2 %copy-start.5 = (bf16[256,2048]{1,0:T(8,128)(2,1)S(1)}, bf16[256,2048]{1,0:T(8,128)(2,1)}, u32[]{:S(2)}) copy-start(bf16[256,2048]{1,0:T(8,128)(2,1)} %get-tuple-element.23.before_grad_ref) | copy-start | bytes 3145732
  88.1 1.0 copy-start.6
  89.2 1.0 copy-start.7

commit v3 on v2

--- a/solution.py
+++ b/solution.py
@@ -54,15 +54,19 @@
     return jnp.where(named & used, 1.0, 0.0)
 
 
-def pack_rows(stage, rows, per, first):
+def pack_rows(stage, rows, slot):
     for tile in range(TILES):
-        stage[pl.ds(first + tile, DEVS, stride=per), :] = rows[:, tile * 128 : (tile + 1) * 128]
-
-
-def unpack_rows(stage, per, first):
-    return jnp.concatenate(
-        [stage[pl.ds(first + tile, DEVS, stride=per), :] for tile in range(TILES)], axis=1
-    )
+        at = pl.ds(slot * TILES + tile, DEVS, stride=ROWS)
+        stage[at, :] = rows[:, tile * 128 : (tile + 1) * 128]
+
+
+def stage_rows(stage, rows_ref, half):
+    stage[...] = rows_ref[:, half].astype(F32).reshape(DEVS * ROWS, 128)
+
+
+def unpack_rows(stage, slot):
+    tiles = [stage[pl.ds(slot * TILES + tile, DEVS, stride=ROWS), :] for tile in range(TILES)]
+    return jnp.concatenate(tiles, axis=1)
 
 
 PART = HD * 3
@@ -107,7 +111,7 @@
         pick = spread_matrix(index_ref, count_ref, slot).T.astype(BF16)
         rows = dot(pick, table_ref[...])
         mark = jnp.where(count_column[:, 0:1] > slot, 0.0, empty_mark)
-        pack_rows(stage, rows + mark, ROWS, slot * TILES)
+        pack_rows(stage, rows + mark, slot)
     out_ref[...] = staged(stage)
 
 
@@ -173,7 +177,7 @@
     mid = normalize(resid.astype(F32))[0].astype(BF16)
     for slot in range(SLOT):
         pick = spread_matrix(index_ref, count_ref, slot).T.astype(BF16)
-        pack_rows(stage, dot(pick, mid), ROWS, slot * TILES)
+        pack_rows(stage, dot(pick, mid), slot)
     out_ref[...] = staged(stage)
 
 
@@ -207,9 +211,9 @@
     )(attended, frames, weight, index, count, packed)
 
 
-FF_TILE = 512
-D_TILE = 256
+FF_TILE = 1024
 FF_STEPS = FF // FF_TILE
+WG_TILE = 512
 gelu_scale = (2.0 / jnp.pi) ** 0.5
 gelu_cubic = 0.044715
 
@@ -227,32 +231,40 @@
 
 def expert_kernel(
     rows_ref, first_hbm, second_hbm, router_ref,
-    back_ref, picked_ref, active_ref, before_grad_ref, out_grad_ref, route_grad_ref,
-    stage, first_ref, second_ref, first_sem, second_sem,
+    back_ref, route_grad_ref, saved_ref,
+    stage_x, stage_g, pulled_ref, first_ref, second_ref, first_sem, second_sem,
 ):
-    loads = []
+    picked_ref = saved_ref.at[:, :D]
+    out_grad_ref = saved_ref.at[:, D : 2 * D]
+    active_ref = saved_ref.at[:, 2 * D : 2 * D + FF]
+    before_grad_ref = saved_ref.at[:, 2 * D + FF :]
+
+    def tiles(step):
+        return pl.ds(step * FF_TILE, FF_TILE)
+
+    first_loads, second_loads = [], []
     for step in range(FF_STEPS):
-        columns = pl.ds(step * FF_TILE, FF_TILE)
-        loads.append((
-            pltpu.make_async_copy(
-                first_hbm.at[:, columns], first_ref.at[:, columns], first_sem.at[step]
-            ),
-            pltpu.make_async_copy(
-                second_hbm.at[columns, :], second_ref.at[columns, :], second_sem.at[step]
-            ),
+        columns = tiles(step)
+        first_loads.append(pltpu.make_async_copy(
+            first_hbm.at[:, columns], first_ref.at[:, columns], first_sem.at[step]
         ))
-    for pair in loads:
-        for load in pair:
-            load.start()
-
-    stage[...] = rows_ref[...].astype(F32).reshape(DEVS * 2 * ROWS, 128)
-    grads = [unpack_rows(stage, 2 * ROWS, ROWS + slot * TILES) for slot in range(SLOT)]
-    grads = jnp.concatenate(grads, axis=0)
+        second_loads.append(pltpu.make_async_copy(
+            second_hbm.at[columns, :], second_ref.at[columns, :], second_sem.at[step]
+        ))
+        second_loads[-1].start()
+        first_loads[-1].start()
+
+    stage_rows(stage_g, rows_ref, 1)
+    grads = jnp.concatenate([unpack_rows(stage_g, slot) for slot in range(SLOT)], axis=0)
     place = seats(grads[:, 0:128])
     take = place.T.astype(BF16)
     place = place.astype(BF16)
     grads = dot(take, grads.astype(BF16)).astype(BF16)
-    rows = [unpack_rows(stage, 2 * ROWS, slot * TILES).astype(BF16) for slot in range(SLOT)]
+    for step in range(FF_STEPS):
+        second_loads[step].wait()
+        pulled_ref[:, tiles(step)] = dot(grads, second_ref[tiles(step), :], ((1,), (1,)))
+    stage_rows(stage_x, rows_ref, 0)
+    rows = [unpack_rows(stage_x, slot).astype(BF16) for slot in range(SLOT)]
     picked_wide = dot(take, jnp.concatenate(rows, axis=0))
     picked = picked_wide.astype(BF16)
     picked_ref[...] = picked
@@ -262,11 +274,10 @@
 
     logit = jnp.zeros((LIVE, 1), F32)
     for step in range(FF_STEPS):
-        columns = pl.ds(step * FF_TILE, FF_TILE)
-        loads[step][0].wait()
+        columns = tiles(step)
+        pulled = pulled_ref[:, columns]
+        first_loads[step].wait()
         before = dot(picked, first_ref[:, columns])
-        loads[step][1].wait()
-        pulled = dot(grads, second_ref[columns, :], ((1,), (1,)))
         square = before * before
         bend = jnp.tanh(before * (gelu_scale + (gelu_scale * gelu_cubic) * square))
         half = 0.5 + 0.5 * bend
@@ -280,21 +291,17 @@
 
     logit_grad = logit * gate * (1.0 - gate)
     route_grad_ref[...] = jnp.sum(logit_grad * picked_ref[...].astype(F32), axis=0, keepdims=True)
-    for start in range(0, D, D_TILE):
-        columns = pl.ds(start, D_TILE)
-        result = dot(active_ref[...], second_ref[:, columns])
-        returned = dot(place, (gate * result).astype(BF16))
-        row_grad = dot(before_grad_ref[...], first_ref[columns, :], ((1,), (1,)))
-        row_grad = row_grad + logit_grad * router_ref[:, columns]
-        row_grad = dot(place, row_grad.astype(BF16))
-        for slot in range(SLOT):
-            sources = slice(slot * DEVS, (slot + 1) * DEVS)
-            for tile in range(D_TILE // 128):
-                lanes = slice(tile * 128, (tile + 1) * 128)
-                at = slot * TILES + start // 128 + tile
-                stage[pl.ds(at, DEVS, stride=2 * ROWS), :] = returned[sources, lanes]
-                stage[pl.ds(ROWS + at, DEVS, stride=2 * ROWS), :] = row_grad[sources, lanes]
-    back_ref[...] = stage[...].reshape(DEVS, 2, ROWS, 128).astype(BF16)
+    result = dot(active_ref[...], second_ref[...])
+    returned = dot(place, (gate * result).astype(BF16))
+    for slot in range(SLOT):
+        pack_rows(stage_x, returned[slot * DEVS : (slot + 1) * DEVS], slot)
+    back_ref[:, 0:1] = staged(stage_x)
+    row_grad = dot(before_grad_ref[...], first_ref[...], ((1,), (1,)))
+    row_grad = row_grad + logit_grad * router_ref[...]
+    row_grad = dot(place, row_grad.astype(BF16))
+    for slot in range(SLOT):
+        pack_rows(stage_g, row_grad[slot * DEVS : (slot + 1) * DEVS], slot)
+    back_ref[:, 1:2] = staged(stage_g)
 
 
 def expert(rows, first, second, router):
@@ -303,23 +310,22 @@
     return pl.pallas_call(
         expert_kernel,
         in_specs=[vmem, hbm, hbm, vmem],
-        out_specs=[vmem] * 6,
+        out_specs=[vmem, vmem, vmem],
         out_shape=[
             jax.ShapeDtypeStruct((DEVS, 2, ROWS, 128), BF16),
-            jax.ShapeDtypeStruct((LIVE, D), BF16),
-            jax.ShapeDtypeStruct((LIVE, FF), BF16),
-            jax.ShapeDtypeStruct((LIVE, FF), BF16),
-            jax.ShapeDtypeStruct((LIVE, D), BF16),
             jax.ShapeDtypeStruct((1, D), F32),
+            jax.ShapeDtypeStruct((LIVE, 2 * D + 2 * FF), BF16),
         ],
         scratch_shapes=[
-            pltpu.VMEM((DEVS * ROWS * 2, 128), F32),
+            pltpu.VMEM((DEVS * ROWS, 128), F32),
+            pltpu.VMEM((DEVS * ROWS, 128), F32),
+            pltpu.VMEM((LIVE, FF), F32),
             pltpu.VMEM((D, FF), BF16),
             pltpu.VMEM((FF, D), BF16),
             pltpu.SemaphoreType.DMA((FF_STEPS,)),
             pltpu.SemaphoreType.DMA((FF_STEPS,)),
         ],
-        compiler_params=params(56),
+        compiler_params=params(44),
         cost_estimate=pl.CostEstimate(
             flops=8 * LIVE * D * FF, bytes_accessed=14 * MB, transcendentals=LIVE * FF
         ),
@@ -331,16 +337,16 @@
     second_ref[...] = dot(active_ref[...], out_grad_ref[...], ((0,), (0,))).astype(BF16)
 
 
-def weight_grads(picked, before_grad, active, out_grad):
-    tile = FF_TILE
+def weight_grads(saved):
+    tile = WG_TILE
     return pl.pallas_call(
         weight_grad_kernel,
         grid=(FF // tile,),
         in_specs=[
-            whole((LIVE, D)),
-            pl.BlockSpec((LIVE, tile), lambda n: (0, n)),
-            pl.BlockSpec((LIVE, tile), lambda n: (0, n)),
-            whole((LIVE, D)),
+            pl.BlockSpec((LIVE, D), lambda n: (0, 0)),
+            pl.BlockSpec((LIVE, tile), lambda n: (0, (2 * D + FF) // tile + n)),
+            pl.BlockSpec((LIVE, tile), lambda n: (0, 2 * D // tile + n)),
+            pl.BlockSpec((LIVE, D), lambda n: (0, 1)),
         ],
         out_specs=[
             pl.BlockSpec((D, tile), lambda n: (0, n)),
@@ -354,21 +360,20 @@
         cost_estimate=pl.CostEstimate(
             flops=4 * LIVE * D * FF, bytes_accessed=11 * MB, transcendentals=0
         ),
-    )(picked, before_grad, active, out_grad)
+    )(saved, saved, saved, saved)
 
 
 def combine_kernel(
-    rows_ref, index_ref, count_ref, resid_ref, upstream_ref, output_ref, grad_ref, stage
+    rows_ref, index_ref, count_ref, resid_ref, upstream_ref, output_ref, grad_ref, stage, stage_g
 ):
-    stage[...] = rows_ref[...].astype(F32).reshape(DEVS * 2 * ROWS, 128)
+    stage_rows(stage, rows_ref, 0)
+    stage_rows(stage_g, rows_ref, 1)
     mixture = jnp.zeros((FR, D), F32)
     normed_grad = jnp.zeros((FR, D), F32)
     for slot in range(SLOT):
         spread = spread_matrix(index_ref, count_ref, slot).astype(BF16)
-        rows = unpack_rows(stage, 2 * ROWS, slot * TILES).astype(BF16)
-        mixture += dot(spread, rows)
-        rows = unpack_rows(stage, 2 * ROWS, ROWS + slot * TILES).astype(BF16)
-        normed_grad += dot(spread, rows)
+        mixture += dot(spread, unpack_rows(stage, slot).astype(BF16))
+        normed_grad += dot(spread, unpack_rows(stage_g, slot).astype(BF16))
     resid = resid_ref[...].astype(F32)
     output_ref[...] = (resid + mixture).astype(BF16)
     unit, inverse = normalize(resid)
@@ -382,7 +387,7 @@
     return pl.pallas_call(
         combine_kernel,
         out_shape=[jax.ShapeDtypeStruct((FR, D), BF16)] * 2,
-        scratch_shapes=[pltpu.VMEM((DEVS * ROWS * 2, 128), F32)],
+        scratch_shapes=[pltpu.VMEM((DEVS * ROWS, 128), F32)] * 2,
         compiler_params=params(28),
         cost_estimate=pl.CostEstimate(
             flops=4 * DEVS * SLOT * FR * D, bytes_accessed=3 * MB, transcendentals=0
@@ -418,11 +423,11 @@
     attended = exchange(attended, "seq").reshape(HALF, FR)
     resid, packed = residual(attended, own_frames, out_weight, index, send_count, packed)
     arrived = exchange(packed, everywhere)
-    back, picked, active, before_grad, out_grad, grad_route = expert(
+    back, grad_route, saved = expert(
         arrived, expert_in[0], expert_out[0], router
     )
     arrived_back = exchange(back, everywhere)
-    grad_first, grad_second = weight_grads(picked, before_grad, active, out_grad)
+    grad_first, grad_second = weight_grads(saved)
     output, grad_resid = combine(arrived_back, index, send_count, resid, upstream)
     return (output[None], grad_resid[None], grad_first[None], grad_second[None], grad_route)
 

time: 114 us -> 111 us (0.974)
  Pallas kernels: 32.2 us -> 27 us
  waiting for transfers between devices: 28.5 us -> 31.4 us
  local copies, waits for them, and re-layouts: 3.33 us -> 2.11 us
    pallas_call x1, Pallas kernels: 15.7 us -> 9.51 us  [expert(): pl.pallas_call(expert_kernel, in_specs=[vmem, hbm, hbm, vmem], out_specs=...]
    all_to_all x3, waiting for transfers between devices: 28.5 us -> 31.4 us  [exchange(): return lax.all_to_all(rows, axes, split_axis=0, concat_axis=0, tiled=True)]
    unnamed x19, local copies, waits for them, and re-layouts: 3.33 us -> 2.11 us
where the time goes in v3:
time: 111 us
  blocking collectives  32.9 us (30%)
  waiting for transfers between devices  31.4 us (28%)
  Pallas kernels  27 us (24%)
  starting transfers between devices  15.9 us (14%)
  local copies, waits for them, and re-layouts  2.11 us (2%)
  between operations  1.38 us (1%)
    all_to_all x1, blocking collectives, exchange(): return lax.all_to_all(rows, axes, split_axis=0, concat_axis=0, tiled=True)  32.9 us
    all_to_all x3, waiting for transfers between devices, exchange(): return lax.all_to_all(rows, axes, split_axis=0, concat_axis=0, tiled=True)  31.4 us
    all_to_all x3, starting transfers between devices, exchange(): return lax.all_to_all(rows, axes, split_axis=0, concat_axis=0, tiled=True)  15.9 us
    pallas_call x1, Pallas kernels, expert(): pl.pallas_call(expert_kernel, in_specs=[vmem, hbm, hbm, vmem], out_specs=...  9.51 us
    pallas_call x1, Pallas kernels, weight_grads(): pl.pallas_call(weight_grad_kernel, grid=(FF // tile,), in_specs=[pl.Block...  4.58 us
    pallas_call x1, Pallas kernels, project(): pl.pallas_call(project_kernel, grid=(3,), in_specs=[whole((FR, D)), pl.Bl...  4.34 us
    pallas_call x1, Pallas kernels, attend(): pl.pallas_call(attend_kernel, in_specs=[pl.BlockSpec(memory_space=pltpu.S...  3.57 us
    pallas_call x1, Pallas kernels, combine(): pl.pallas_call(combine_kernel, out_shape=[jax.ShapeDtypeStruct((FR, D), B...  3.23 us
  transfers between devices with their start and end apart: 3, of which 3 were waited for; matrix products, arithmetic and copies ran while one was open for 0% of the time, Pallas kernels for 5%

profile of v3, /device:TPU:1, one launch (start us, length us, event | category | flops | bytes accessed | tf_op | source)
XLA Modules:
  0.0 110.7 jit_solution(6851054573791390711)
XLA Ops:
  0.6 0.0 copy-start.8
  0.6 0.0 copy-start.2
  0.7 0.0 copy-start.6
  0.7 4.3 %shard_map.137 = bf16[1536,128]{1,0:T(8,128)(2,1)} custom-call(bf16[128,1024]{1,0:T(8,128)(2,1)} %bitcast.19, bf16[1024,1536]{1,0:T(8,128)(2,1)} %weight_ref.2), custom_call_target="tpu_custom_call" | custom-call | flops 402653184 | bytes 4194304 | tf_op jit(solution)/shard_map/pallas_call | solution.py:90
  5.0 0.0 copy-start.1
  5.0 0.0 copy-start.3
  5.0 5.9 %all-to-all-start = ((bf16[8,192,128]{2,1,0:T(8,128)(2,1)}), bf16[8,192,128]{2,1,0:T(8,128)(2,1)S(1)}, u32[]{:S(2)}, u32[]{:S(2)}) async-start(bf16[8,192,128]{2,1,0:T(8,128)(2,1)} %bitcast.26), calls=%async_computation | async-start | bytes 786432 | tf_op jit(solution)/shard_map/all_to_all | solution.py:399
  11.6 7.4 %all-to-all-done = bf16[8,192,128]{2,1,0:T(8,128)(2,1)S(1)} async-done(((bf16[8,192,128]{2,1,0:T(8,128)(2,1)}), bf16[8,192,128]{2,1,0:T(8,128)(2,1)S(1)}, u32[]{:S(2)}, u32[]{:S(2)}) %all-to-all-start) | async-done | bytes 393248 | tf_op jit(solution)/shard_map/all_to_all | solution.py:399
  19.0 3.6 %shard_map.138 = bf16[512,128]{1,0:T(8,128)(2,1)} custom-call(s32[1]{0:T(128)S(6)} %copy.20.length_ref, bf16[1536,128]{1,0:T(8,128)(2,1)S(1)} %bitcast.22), custom_call_target="tpu_custom_call" | custom-call | flops 268435456 | bytes 524288 | tf_op jit(solution)/shard_map/pallas_call | solution.py:156
  22.6 4.1 %all-to-all-start.1 = ((bf16[8,64,128]{2,1,0:T(8,128)(2,1)}), bf16[8,64,128]{2,1,0:T(8,128)(2,1)S(1)}, u32[]{:S(2)}, u32[]{:S(2)}) async-start(bf16[8,64,128]{2,1,0:T(8,128)(2,1)} %bitcast.3), calls=%async_computation.1 | async-start | bytes 262144 | tf_op jit(solution)/shard_map/all_to_all | solution.py:399
  26.7 0.0 copy-done.8
  26.7 0.0 copy-done.2
  26.7 0.0 copy-done.6
  26.8 0.6 shard_map.139.packed_ref
  27.4 0.0 copy-start.7
  27.4 4.6 %all-to-all-done.1 = bf16[8,64,128]{2,1,0:T(8,128)(2,1)S(1)} async-done(((bf16[8,64,128]{2,1,0:T(8,128)(2,1)}), bf16[8,64,128]{2,1,0:T(8,128)(2,1)S(1)}, u32[]{:S(2)}, u32[]{:S(2)}) %all-to-all-start.1) | async-done | bytes 131104 | tf_op jit(solution)/shard_map/all_to_all | solution.py:399
  32.0 0.0 copy-done.1
  32.0 0.0 copy-done.3
  32.0 1.1 %shard_map.140 = (bf16[128,1024]{1,0:T(8,128)(2,1)S(1)}, bf16[128,2,24,128]{3,2,1,0:T(8,128)(2,1)S(1)}) custom-call(bf16[512,128]{1,0:T(8,128)(2,1)S(1)} %bitcast.21, bf16[128,1024]{1,0:T(8,128)(2,1)S(1)} %bitcast.20, bf16[512,1024]{1,0:T(8,128)(2,1)S(1)} %copy-done.1, s32[3,128]{1,0:T(4,128)S(1)} %bitcast.24, ...), custom_call_target="tpu_custom_call", output_to_operand_aliasing={{1}: (5, {})} | custom-call | flops 234881024 | bytes 3145728 | tf_op jit(solution)/shard_map/pallas_call | solution.py:185
  33.2 0.0 copy-start.4
  33.2 32.9 %all_to_all.20.rows_ref = bf16[128,2,24,128]{3,2,1,0:T(8,128)(2,1)S(1)} all-to-all(bf16[128,2,24,128]{3,2,1,0:T(8,128)(2,1)S(1)} %get-tuple-element.14), channel_id=1, replica_groups=mesh['seq'=8,'exp'=16] {'seq','exp'}, dimensions={0} | all-to-all | bytes 3145728 | tf_op jit(solution)/shard_map/all_to_all | solution.py:399
  66.1 0.0 copy-done.4
  66.1 0.0 copy-done.7
  66.1 9.5 %shard_map.141 = (bf16[128,2,24,128]{3,2,1,0:T(8,128)(2,1)S(1)}, f32[1,1024]{1,0:T(1,128)}, bf16[256,6144]{1,0:T(8,128)(2,1)S(1)}) custom-call(bf16[128,2,24,128]{3,2,1,0:T(8,128)(2,1)S(1)} %all_to_all.20.rows_ref, bf16[1024,2048]{1,0:T(8,128)(2,1)} %bitcast.27, bf16[2048,1024]{1,0:T(8,128)(2,1)} %bitcast.28, f32[1,1024]{1,0:T(1,128)S(1)} %copy-done.7), custom_call_target="tpu_custom_call" | custom-call | flops 4294967296 | bytes 14680064 | tf_op jit(solution)/shard_map/pallas_call | solution.py:310
  75.6 0.0 copy-start
  75.6 1.1 %copy-done = bf16[128,2,24,128]{3,2,1,0:T(8,128)(2,1)} copy-done((bf16[128,2,24,128]{3,2,1,0:T(8,128)(2,1)}, bf16[128,2,24,128]{3,2,1,0:T(8,128)(2,1)S(1)}, u32[]{:S(2)}) %copy-start) | copy-done | bytes 1572888
  76.7 5.9 %all-to-all-start.3 = ((bf16[128,2,24,128]{3,2,1,0:T(8,128)(2,1)}), bf16[128,2,24,128]{3,2,1,0:T(8,128)(2,1)}, u32[]{:S(2)}, u32[]{:S(2)}) async-start(bf16[128,2,24,128]{3,2,1,0:T(8,128)(2,1)} %copy-done), calls=%async_computation.3 | async-start | bytes 3145728 | tf_op jit(solution)/shard_map/all_to_all | solution.py:399
  82.6 4.6 %shard_map.143 = (bf16[1024,2048]{1,0:T(8,128)(2,1)}, bf16[2048,1024]{1,0:T(8,128)(2,1)}) custom-call(bf16[256,6144]{1,0:T(8,128)(2,1)S(1)} %get-tuple-element.19.picked_ref.before_grad_ref.active_ref.out_grad_ref, bf16[256,6144]{1,0:T(8,128)(2,1)S(1)} %get-tuple-element.19.picked_ref.before_grad_ref.active_ref.out_grad_ref, ...), custom_call_target="tpu_custom_call" | custom-call | flops 2147483648 | bytes 11534336 | tf_op jit(solution)/shard_map/pallas_call | solution.py:342
  87.2 19.4 %all-to-all-done.3.rows_ref = bf16[128,2,24,128]{3,2,1,0:T(8,128)(2,1)} async-done(((bf16[128,2,24,128]{3,2,1,0:T(8,128)(2,1)}), bf16[128,2,24,128]{3,2,1,0:T(8,128)(2,1)}, u32[]{:S(2)}, u32[]{:S(2)}) %all-to-all-start.3) | async-done | bytes 1572896 | tf_op jit(solution)/shard_map/all_to_all | solution.py:399
  106.5 0.0 copy-start.5
  106.5 0.9 copy-done.5
  107.5 3.2 %shard_map.142 = (bf16[128,1024]{1,0:T(8,128)(2,1)}, bf16[128,1024]{1,0:T(8,128)(2,1)}) custom-call(bf16[128,2,24,128]{3,2,1,0:T(8,128)(2,1)} %all-to-all-done.3.rows_ref, s32[3,128]{1,0:T(4,128)S(1)} %bitcast.25, s32[1,128]{1,0:T(1,128)S(1)} %copy-done.6, bf16[128,1024]{1,0:T(8,128)(2,1)S(1)} %copy-done.5, bf16[128,1024]{1,0:T(8,128)(2,1)S(1)} %bitcast.18), custom_call_target="tpu_custom_call" | custom-call | flops 201326592 | bytes 3145728 | tf_op jit(solution)/shard_map/pallas_call | solution.py:387
  (1 shorter events, 0.0 us)
Async XLA Ops:
  0.6 26.1 %copy-start.8 = (s32[1,128,3]{1,0,2:T(1,128)S(1)}, s32[1,128,3]{1,0,2:T(1,128)}, u32[]{:S(2)}) copy-start(s32[1,128,3]{1,0,2:T(1,128)} %param.18) | copy-start | bytes 4612
  0.6 26.1 %copy-start.2 = (bf16[1,128,1024]{2,1,0:T(8,128)(2,1)S(1)}, bf16[1,128,1024]{2,1,0:T(8,128)(2,1)}, u32[]{:S(2)}) copy-start(bf16[1,128,1024]{2,1,0:T(8,128)(2,1)} %param.11) | copy-start | bytes 786436
  0.7 26.1 %copy-start.6 = (s32[1,128]{1,0:T(1,128)S(1)}, s32[1,128]{1,0:T(1,128)}, u32[]{:S(2)}) copy-start(s32[1,128]{1,0:T(1,128)} %count_ref.5) | copy-start | bytes 1540
  5.0 27.0 %copy-start.1 = (bf16[512,1024]{1,0:T(8,128)(2,1)S(1)}, bf16[512,1024]{1,0:T(8,128)(2,1)}, u32[]{:S(2)}) copy-start(bf16[512,1024]{1,0:T(8,128)(2,1)} %weight_ref.3) | copy-start | bytes 3145732
  5.0 27.0 %copy-start.3 = (bf16[1,128,1024]{2,1,0:T(8,128)(2,1)S(1)}, bf16[1,128,1024]{2,1,0:T(8,128)(2,1)}, u32[]{:S(2)}) copy-start(bf16[1,128,1024]{2,1,0:T(8,128)(2,1)} %param.10) | copy-start | bytes 786436
  5.0 14.0 %all-to-all-start = ((bf16[8,192,128]{2,1,0:T(8,128)(2,1)}), bf16[8,192,128]{2,1,0:T(8,128)(2,1)S(1)}, u32[]{:S(2)}, u32[]{:S(2)}) async-start(bf16[8,192,128]{2,1,0:T(8,128)(2,1)} %bitcast.26), calls=%async_computation | async-start | bytes 786432 | tf_op jit(solution)/shard_map/all_to_all | solution.py:399
  22.6 9.4 %all-to-all-start.1 = ((bf16[8,64,128]{2,1,0:T(8,128)(2,1)}), bf16[8,64,128]{2,1,0:T(8,128)(2,1)S(1)}, u32[]{:S(2)}, u32[]{:S(2)}) async-start(bf16[8,64,128]{2,1,0:T(8,128)(2,1)} %bitcast.3), calls=%async_computation.1 | async-start | bytes 262144 | tf_op jit(solution)/shard_map/all_to_all | solution.py:399
  27.4 38.7 %copy-start.7 = (f32[1,1024]{1,0:T(1,128)S(1)}, f32[1,1024]{1,0:T(1,128)}, u32[]{:S(2)}) copy-start(f32[1,1024]{1,0:T(1,128)} %router_ref.1) | copy-start | bytes 12292
  33.2 32.9 %copy-start.4 = (bf16[128,1024]{1,0:T(8,128)(2,1)}, bf16[128,1024]{1,0:T(8,128)(2,1)S(1)}, u32[]{:S(2)}) copy-start(bf16[128,1024]{1,0:T(8,128)(2,1)S(1)} %get-tuple-element.16.resid_ref) | copy-start | bytes 786436
  75.6 1.1 %copy-start = (bf16[128,2,24,128]{3,2,1,0:T(8,128)(2,1)}, bf16[128,2,24,128]{3,2,1,0:T(8,128)(2,1)S(1)}, u32[]{:S(2)}) copy-start(bf16[128,2,24,128]{3,2,1,0:T(8,128)(2,1)S(1)} %get-tuple-element.15) | copy-start | bytes 4718596
  76.7 29.8 %all-to-all-start.3 = ((bf16[128,2,24,128]{3,2,1,0:T(8,128)(2,1)}), bf16[128,2,24,128]{3,2,1,0:T(8,128)(2,1)}, u32[]{:S(2)}, u32[]{:S(2)}) async-start(bf16[128,2,24,128]{3,2,1,0:T(8,128)(2,1)} %copy-done), calls=%async_computation.3 | async-start | bytes 3145728 | tf_op jit(solution)/shard_map/all_to_all | solution.py:399
  106.5 1.0 copy-start.5

commit v4 on v3

--- a/solution.py
+++ b/solution.py
@@ -12,6 +12,7 @@
 FR = 128
 DEVS = 128
 SLOT = 3
+UTTS = 16
 KEYS = 1024
 LIVE = 256
 TILES = D // 128
@@ -69,146 +70,181 @@
     return jnp.concatenate(tiles, axis=1)
 
 
-PART = HD * 3
+INFO = 16
+PART = HD * 3 + INFO
 HALF = HEADS * HD
 
 
-def project_kernel(frames_ref, weight_ref, out_ref, normed):
+def project_kernel(frames_ref, index_ref, count_ref, weight_ref, out_ref, normed):
     step = pl.program_id(0)
 
     @pl.when(step == 0)
     def _():
         normed[...] = normalize(frames_ref[...].astype(F32))[0].astype(BF16)
+        info = jnp.concatenate(
+            [
+                index_ref[...].astype(F32),
+                count_ref[...].astype(F32),
+                jnp.zeros((INFO - SLOT - 1, DEVS), F32),
+            ],
+            axis=0,
+        ).astype(BF16)
+        for head in range(HEADS):
+            out_ref[head, 3 * HD :, :] = info
 
     block = dot(normed[...], weight_ref[...]).T.astype(BF16)
     for head in range(HEADS):
-        start = pl.multiple_of(head * PART + step * HD, HD)
-        out_ref[pl.ds(start, HD), :] = block[head * HD : (head + 1) * HD]
-
-
-def project(frames, weight):
+        start = pl.multiple_of(step * HD, HD)
+        out_ref[head, pl.ds(start, HD), :] = block[head * HD : (head + 1) * HD]
+
+
+def project(frames, index, count, weight):
     return pl.pallas_call(
         project_kernel,
         grid=(3,),
-        in_specs=[whole((FR, D)), pl.BlockSpec((D, HALF), lambda n: (0, n))],
-        out_specs=whole((HEADS * PART, FR)),
-        out_shape=jax.ShapeDtypeStruct((HEADS * PART, FR), BF16),
+        in_specs=[
+            whole((FR, D)),
+            whole((SLOT, DEVS)),
+            whole((1, DEVS)),
+            pl.BlockSpec((D, HALF), lambda n: (0, n)),
+        ],
+        out_specs=whole((HEADS, PART, FR)),
+        out_shape=jax.ShapeDtypeStruct((HEADS, PART, FR), BF16),
         scratch_shapes=[pltpu.VMEM((FR, D), BF16)],
         compiler_params=params(56),
         cost_estimate=pl.CostEstimate(
             flops=2 * FR * D * 3 * HALF, bytes_accessed=4 * MB, transcendentals=0
         ),
-    )(frames, weight)
+    )(frames, index, count, weight)
+
+
+SENT = 64
+ATTENDED = 16
+ATTENDED_ROWS = slice(SENT - ATTENDED, SENT)
 
 
 def staged(stage):
-    return stage[...].reshape(DEVS, 1, ROWS, 128).astype(BF16)
-
-
-def gather_kernel(table_ref, index_ref, count_ref, out_ref, stage):
+    return stage[...].reshape(DEVS, ROWS, 128)
+
+
+def gather_kernel(grads_ref, frames_ref, index_ref, count_ref, out_ref, stage_g, stage_f):
     count_column = jnp.broadcast_to(count_ref[...].astype(F32), (DEVS, DEVS)).T
     for slot in range(SLOT):
         pick = spread_matrix(index_ref, count_ref, slot).T.astype(BF16)
-        rows = dot(pick, table_ref[...])
         mark = jnp.where(count_column[:, 0:1] > slot, 0.0, empty_mark)
-        pack_rows(stage, rows + mark, slot)
-    out_ref[...] = staged(stage)
-
-
-def gather_rows(table, index, count):
+        pack_rows(stage_g, dot(pick, grads_ref[...]) + mark, slot)
+        pack_rows(stage_f, dot(pick, frames_ref[...]), slot)
+    rows = jnp.concatenate([staged(stage_g), staged(stage_f)], axis=1)
+    out_ref[...] = rows.astype(BF16)
+
+
+def gather_rows(grads, frames, index, count):
     return pl.pallas_call(
         gather_kernel,
         grid=(1,),
-        in_specs=[whole((FR, D)), whole((SLOT, DEVS)), whole((1, DEVS))],
-        out_specs=pl.BlockSpec((DEVS, 1, ROWS, 128), lambda n: (0, 1, 0, 0)),
-        out_shape=jax.ShapeDtypeStruct((DEVS, 2, ROWS, 128), BF16),
-        scratch_shapes=[pltpu.VMEM((DEVS * ROWS, 128), F32)],
-        compiler_params=params(20),
-        cost_estimate=pl.CostEstimate(
-            flops=2 * DEVS * SLOT * FR * D, bytes_accessed=2 * MB, transcendentals=0
-        ),
-    )(table, index, count)
+        in_specs=[whole((FR, D)), whole((FR, D)), whole((SLOT, DEVS)), whole((1, DEVS))],
+        out_specs=pl.BlockSpec((DEVS, 2 * ROWS, 128), lambda n: (0, 0, 0)),
+        out_shape=jax.ShapeDtypeStruct((DEVS, SENT, 128), BF16),
+        scratch_shapes=[pltpu.VMEM((DEVS * ROWS, 128), F32)] * 2,
+        compiler_params=params(24),
+        cost_estimate=pl.CostEstimate(
+            flops=4 * DEVS * SLOT * FR * D, bytes_accessed=3 * MB, transcendentals=0
+        ),
+    )(grads, frames, index, count)
 
 
 QUERIES = 256
 
 
-def attend_kernel(length_ref, parts_ref, out_ref):
-    parts = [parts_ref[s * PART : (s + 1) * PART, :] for s in range(HEADS)]
+def attend_kernel(scalar_ref, parts_ref, packed_ref, out_ref, sent_ref, stage):
+    parts = [parts_ref[s] for s in range(HEADS)]
     q = jnp.concatenate([part[:HD] for part in parts], axis=1)
     k = jnp.concatenate([part[HD : 2 * HD] for part in parts], axis=1).astype(F32)
     k = (k * HD ** (-0.5)).T.astype(BF16)
-    v = jnp.concatenate([part[2 * HD :] for part in parts], axis=1)
-    live = lax.broadcasted_iota(jnp.int32, (KEYS, QUERIES), 0) < length_ref[0]
-    for first in range(0, KEYS, QUERIES):
-        scores = dot(k, q[:, first : first + QUERIES])
+    v = jnp.concatenate([part[2 * HD : 3 * HD] for part in parts], axis=1)
+    infos = [part[3 * HD :].astype(F32) for part in parts]
+    live = lax.broadcasted_iota(jnp.int32, (KEYS, QUERIES), 0) < scalar_ref[0]
+    head = scalar_ref[1]
+    frame = lax.broadcasted_iota(jnp.int32, (FR, DEVS), 0).astype(F32)
+    upper = lax.broadcasted_iota(jnp.int32, (2 * HD, QUERIES), 0) < HD
+    own = upper == (lax.broadcasted_iota(jnp.int32, (2 * HD, QUERIES), 1) < FR)
+    stage[...] = jnp.zeros_like(stage)
+
+    def spread(source, slot):
+        info = infos[source]
+        named = jnp.broadcast_to(info[slot : slot + 1], (FR, DEVS)) == frame
+        used = jnp.broadcast_to(info[SLOT : SLOT + 1], (FR, DEVS)) > slot
+        return jnp.where(named & used, 1.0, 0.0)
+
+    for pair in range(KEYS // QUERIES):
+        scores = dot(k, q[:, pair * QUERIES : (pair + 1) * QUERIES])
         scores = jnp.where(live, scores, masked_score)
         top = jnp.max(scores, axis=0, keepdims=True)
         weights = jnp.exp(scores - top)
         total = jnp.sum(weights, axis=0, keepdims=True)
         mixed = (dot(v, weights.astype(BF16)) / total).astype(BF16)
-        for piece in range(QUERIES // FR):
-            source = first // FR + piece
-            out_ref[source * HD : (source + 1) * HD, :] = mixed[:, piece * FR : (piece + 1) * FR]
-
-
-def attend(length, parts):
+        for half in range(2):
+            source = 2 * pair + half
+            piece = lax.rem(source - head + HEADS, HEADS)
+            out_ref[piece] = mixed[:, half * FR : (half + 1) * FR]
+        mixed = mixed.astype(F32)
+        twice = jnp.where(own, jnp.concatenate([mixed, mixed], axis=0), 0.0).astype(BF16)
+        for slot in range(SLOT):
+            spreads = [spread(2 * pair, slot), spread(2 * pair + 1, slot)]
+            spreads = jnp.concatenate(spreads, axis=0).astype(BF16)
+            at = pl.ds(slot * (KEYS // QUERIES) + pair, DEVS, stride=ATTENDED)
+            stage[at, :] = dot(twice, spreads).T
+    sent_ref[...] = stage[...].reshape(DEVS, ATTENDED, 128).astype(BF16)
+
+
+def attend(scalars, parts, packed):
     return pl.pallas_call(
         attend_kernel,
+        grid=(1,),
         in_specs=[
             pl.BlockSpec(memory_space=pltpu.SMEM),
-            pl.BlockSpec(memory_space=pltpu.VMEM),
-        ],
-        out_shape=jax.ShapeDtypeStruct((HALF, FR), BF16),
-        compiler_params=params(24),
-        cost_estimate=pl.CostEstimate(
-            flops=4 * KEYS * KEYS * HD, bytes_accessed=MB // 2, transcendentals=KEYS * KEYS
-        ),
-    )(length, parts)
-
-
-def residual_kernel(
-    attended_ref, frames_ref, weight_ref, index_ref, count_ref, packed_ref,
-    resid_ref, out_ref, stage,
-):
-    attended = attended_ref[...].astype(F32).T.astype(BF16)
-    resid = (frames_ref[...].astype(F32) + dot(attended, weight_ref[...])).astype(BF16)
-    resid_ref[...] = resid
-    mid = normalize(resid.astype(F32))[0].astype(BF16)
-    for slot in range(SLOT):
-        pick = spread_matrix(index_ref, count_ref, slot).T.astype(BF16)
-        pack_rows(stage, dot(pick, mid), slot)
-    out_ref[...] = staged(stage)
-
-
-def residual(attended, frames, weight, index, count, packed):
+            whole((HEADS, PART, FR)),
+            pl.BlockSpec(memory_space=pl.ANY),
+        ],
+        out_specs=[
+            whole((HEADS, HD, FR)),
+            pl.BlockSpec((DEVS, ATTENDED, 128), lambda n: (0, SENT // ATTENDED - 1, 0)),
+        ],
+        out_shape=[
+            jax.ShapeDtypeStruct((HEADS, HD, FR), BF16),
+            jax.ShapeDtypeStruct((DEVS, SENT, 128), BF16),
+        ],
+        input_output_aliases={2: 1},
+        scratch_shapes=[pltpu.VMEM((DEVS * ATTENDED, 128), F32)],
+        compiler_params=params(28),
+        cost_estimate=pl.CostEstimate(
+            flops=4 * KEYS * KEYS * HD, bytes_accessed=MB, transcendentals=KEYS * KEYS
+        ),
+    )(scalars, parts, packed)
+
+
+def residual_kernel(scalar_ref, *refs):
+    pieces, (frames_ref, weight_ref, resid_ref, attended) = refs[:HEADS], refs[HEADS:]
+    for step in range(HEADS):
+        head = lax.rem(scalar_ref[1] - step + HEADS, HEADS)
+        attended[pl.ds(pl.multiple_of(head * HD, HD), HD), :] = pieces[step][...]
+    mixed = dot(attended[...].astype(F32).T.astype(BF16), weight_ref[...])
+    resid_ref[...] = (frames_ref[...].astype(F32) + mixed).astype(BF16)
+
+
+def residual(scalars, pieces, frames, weight):
+    vmem = pl.BlockSpec(memory_space=pltpu.VMEM)
     return pl.pallas_call(
         residual_kernel,
-        grid=(1,),
-        in_specs=[
-            whole((HALF, FR)),
-            whole((FR, D)),
-            whole((HALF, D)),
-            whole((SLOT, DEVS)),
-            whole((1, DEVS)),
-            pl.BlockSpec(memory_space=pl.ANY),
-        ],
-        out_specs=[
-            whole((FR, D)),
-            pl.BlockSpec((DEVS, 1, ROWS, 128), lambda n: (0, 0, 0, 0)),
-        ],
-        out_shape=[
-            jax.ShapeDtypeStruct((FR, D), BF16),
-            jax.ShapeDtypeStruct((DEVS, 2, ROWS, 128), BF16),
-        ],
-        input_output_aliases={5: 1},
-        scratch_shapes=[pltpu.VMEM((DEVS * ROWS, 128), F32)],
-        compiler_params=params(24),
-        cost_estimate=pl.CostEstimate(
-            flops=2 * FR * HALF * D + 2 * DEVS * SLOT * FR * D,
-            bytes_accessed=3 * MB, transcendentals=0,
-        ),
-    )(attended, frames, weight, index, count, packed)
+        in_specs=[pl.BlockSpec(memory_space=pltpu.SMEM)] + [vmem] * (HEADS + 2),
+        out_specs=vmem,
+        out_shape=jax.ShapeDtypeStruct((FR, D), BF16),
+        scratch_shapes=[pltpu.VMEM((HALF, FR), BF16)],
+        compiler_params=params(16),
+        cost_estimate=pl.CostEstimate(
+            flops=2 * FR * HALF * D, bytes_accessed=2 * MB, transcendentals=0
+        ),
+    )(scalars, *pieces, frames, weight)
 
 
 FF_TILE = 1024
@@ -229,10 +265,26 @@
     return jnp.where(seat == lax.broadcasted_iota(jnp.int32, (total, LIVE), 1), 1.0, 0.0)
 
 
+def unpack_attended(stage):
+    low = lax.broadcasted_iota(jnp.int32, (UTTS, 128), 1) < HD
+    rows = []
+    for slot in range(SLOT):
+        for pair in range(HEADS // 2):
+            at = pl.ds(slot * (HEADS // 2) + pair, DEVS, stride=ATTENDED)
+            values = stage[at, :]
+            heads = [values[head * UTTS : (head + 1) * UTTS] for head in range(HEADS)]
+            for half in range(2):
+                own = low if half == 0 else jnp.logical_not(low)
+                kept = [jnp.where(own, part, 0.0) for part in heads]
+                rows.append(jnp.concatenate(kept, axis=1))
+    return jnp.concatenate(rows, axis=0).astype(BF16)
+
+
 def expert_kernel(
-    rows_ref, first_hbm, second_hbm, router_ref,
+    rows_ref, first_hbm, second_hbm, mix_hbm, router_ref,
     back_ref, route_grad_ref, saved_ref,
-    stage_x, stage_g, pulled_ref, first_ref, second_ref, first_sem, second_sem,
+    stage_x, stage_g, stage_a, pulled_ref, first_ref, second_ref, mix_ref,
+    first_sem, second_sem, mix_sem,
 ):
     picked_ref = saved_ref.at[:, :D]
     out_grad_ref = saved_ref.at[:, D : 2 * D]
@@ -242,6 +294,8 @@
     def tiles(step):
         return pl.ds(step * FF_TILE, FF_TILE)
 
+    mix_load = pltpu.make_async_copy(mix_hbm, mix_ref, mix_sem)
+    mix_load.start()
     first_loads, second_loads = [], []
     for step in range(FF_STEPS):
         columns = tiles(step)
@@ -254,7 +308,10 @@
         second_loads[-1].start()
         first_loads[-1].start()
 
-    stage_rows(stage_g, rows_ref, 1)
+    sent = rows_ref[...].astype(F32)
+    stage_g[...] = sent[:, :ROWS].reshape(DEVS * ROWS, 128)
+    stage_x[...] = sent[:, ROWS : 2 * ROWS].reshape(DEVS * ROWS, 128)
+    stage_a[...] = sent[:, ATTENDED_ROWS].reshape(DEVS * ATTENDED, 128)
     grads = jnp.concatenate([unpack_rows(stage_g, slot) for slot in range(SLOT)], axis=0)
     place = seats(grads[:, 0:128])
     take = place.T.astype(BF16)
@@ -263,10 +320,20 @@
     for step in range(FF_STEPS):
         second_loads[step].wait()
         pulled_ref[:, tiles(step)] = dot(grads, second_ref[tiles(step), :], ((1,), (1,)))
-    stage_rows(stage_x, rows_ref, 0)
     rows = [unpack_rows(stage_x, slot).astype(BF16) for slot in range(SLOT)]
-    picked_wide = dot(take, jnp.concatenate(rows, axis=0))
-    picked = picked_wide.astype(BF16)
+    taken = dot(take, jnp.concatenate(rows, axis=0))
+    attended = dot(take, unpack_attended(stage_a))
+    attended = [attended[:, head * 128 : (head + 1) * 128] for head in range(HEADS)]
+    attended = [values + pltpu.roll(values, HD, 1) for values in attended]
+    low = lax.broadcasted_iota(jnp.int32, (LIVE, 128), 1) < HD
+    attended = [
+        jnp.where(low, attended[head], attended[head + 1]) for head in range(0, HEADS, 2)
+    ]
+    attended = jnp.concatenate(attended, axis=1).astype(BF16)
+    mix_load.wait()
+    resid = (taken + dot(attended, mix_ref[...])).astype(BF16)
+    picked = normalize(resid.astype(F32))[0].astype(BF16)
+    picked_wide = picked.astype(F32)
     picked_ref[...] = picked
     logits = jnp.sum(picked_wide * router_ref[...], axis=-1, keepdims=True)
     gate = 1.0 / (1.0 + jnp.exp(-logits))
@@ -295,21 +362,21 @@
     returned = dot(place, (gate * result).astype(BF16))
     for slot in range(SLOT):
         pack_rows(stage_x, returned[slot * DEVS : (slot + 1) * DEVS], slot)
-    back_ref[:, 0:1] = staged(stage_x)
+    back_ref[:, 0] = staged(stage_x).astype(BF16)
     row_grad = dot(before_grad_ref[...], first_ref[...], ((1,), (1,)))
     row_grad = row_grad + logit_grad * router_ref[...]
     row_grad = dot(place, row_grad.astype(BF16))
     for slot in range(SLOT):
         pack_rows(stage_g, row_grad[slot * DEVS : (slot + 1) * DEVS], slot)
-    back_ref[:, 1:2] = staged(stage_g)
-
-
-def expert(rows, first, second, router):
+    back_ref[:, 1] = staged(stage_g).astype(BF16)
+
+
+def expert(rows, first, second, mix, router):
     vmem = pl.BlockSpec(memory_space=pltpu.VMEM)
     hbm = pl.BlockSpec(memory_space=pl.ANY)
     return pl.pallas_call(
         expert_kernel,
-        in_specs=[vmem, hbm, hbm, vmem],
+        in_specs=[vmem, hbm, hbm, hbm, vmem],
         out_specs=[vmem, vmem, vmem],
         out_shape=[
             jax.ShapeDtypeStruct((DEVS, 2, ROWS, 128), BF16),
@@ -319,17 +386,20 @@
         scratch_shapes=[
             pltpu.VMEM((DEVS * ROWS, 128), F32),
             pltpu.VMEM((DEVS * ROWS, 128), F32),
+            pltpu.VMEM((DEVS * ATTENDED, 128), F32),
             pltpu.VMEM((LIVE, FF), F32),
             pltpu.VMEM((D, FF), BF16),
             pltpu.VMEM((FF, D), BF16),
+            pltpu.VMEM((HALF, D), BF16),
             pltpu.SemaphoreType.DMA((FF_STEPS,)),
             pltpu.SemaphoreType.DMA((FF_STEPS,)),
+            pltpu.SemaphoreType.DMA,
         ],
         compiler_params=params(44),
         cost_estimate=pl.CostEstimate(
             flops=8 * LIVE * D * FF, bytes_accessed=14 * MB, transcendentals=LIVE * FF
         ),
-    )(rows, first, second, router)
+    )(rows, first, second, mix, router)
 
 
 def weight_grad_kernel(picked_ref, before_grad_ref, active_ref, out_grad_ref, first_ref, second_ref):
@@ -388,7 +458,7 @@
         combine_kernel,
         out_shape=[jax.ShapeDtypeStruct((FR, D), BF16)] * 2,
         scratch_shapes=[pltpu.VMEM((DEVS * ROWS, 128), F32)] * 2,
-        compiler_params=params(28),
+        compiler_params=params(56),
         cost_estimate=pl.CostEstimate(
             flops=4 * DEVS * SLOT * FR * D, bytes_accessed=3 * MB, transcendentals=0
         ),
@@ -416,16 +486,19 @@
     index = send_index[0].T
     everywhere = ("seq", "exp")
 
-    parts = project(own_frames, qkv_weight).reshape(HEADS, PART, FR)
-    parts = exchange(parts, "seq").reshape(HEADS * PART, FR)
-    packed = gather_rows(upstream, index, send_count)
-    attended = attend(lengths, parts).reshape(HEADS, HD, FR)
-    attended = exchange(attended, "seq").reshape(HALF, FR)
-    resid, packed = residual(attended, own_frames, out_weight, index, send_count, packed)
+    own = lax.axis_index("seq").astype(jnp.int32)
+    scalars = jnp.concatenate([lengths, own[None]])
+
+    parts = exchange(project(own_frames, index, send_count, qkv_weight), "seq")
+    packed = gather_rows(upstream, own_frames, index, send_count)
+    attended, packed = attend(scalars, parts, packed)
     arrived = exchange(packed, everywhere)
-    back, grad_route, saved = expert(
-        arrived, expert_in[0], expert_out[0], router
-    )
+    pieces = [attended[0]]
+    for step in range(1, HEADS):
+        ring = [(source, (source + step) % HEADS) for source in range(HEADS)]
+        pieces.append(lax.ppermute(attended[step], "seq", ring))
+    resid = residual(scalars, pieces, own_frames, out_weight)
+    back, grad_route, saved = expert(arrived, expert_in[0], expert_out[0], out_weight, router)
     arrived_back = exchange(back, everywhere)
     grad_first, grad_second = weight_grads(saved)
     output, grad_resid = combine(arrived_back, index, send_count, resid, upstream)

time: 111 us -> 118 us (1.063)
  waiting for transfers between devices: 31.4 us -> 21.8 us
  blocking collectives: 32.9 us -> 38.1 us
  Pallas kernels: 27 us -> 31.2 us
  starting transfers between devices: 15.9 us -> 20 us
  local copies, waits for them, and re-layouts: 2.11 us -> 4.44 us
    all_to_all x3 -> x2, waiting for transfers between devices: 31.4 us -> 6.54 us  [exchange(): return lax.all_to_all(rows, axes, split_axis=0, concat_axis=0, tiled=True)]
    ppermute x0 -> x7, waiting for transfers between devices: none -> 15.3 us  [local(): pieces.append(lax.ppermute(attended[step], 'seq', ring))]
    ppermute x0 -> x7, starting transfers between devices: none -> 8.22 us  [local(): pieces.append(lax.ppermute(attended[step], 'seq', ring))]
    all_to_all x1, blocking collectives: 32.9 us -> 38.1 us  [exchange(): return lax.all_to_all(rows, axes, split_axis=0, concat_axis=0, tiled=True)]
    all_to_all x3 -> x2, starting transfers between devices: 15.9 us -> 11.8 us  [exchange(): return lax.all_to_all(rows, axes, split_axis=0, concat_axis=0, tiled=True)]
    pallas_call x4, Pallas kernels: 18.5 us -> 22.2 us  [the longest x1 12.4 us: expert(): pl.pallas_call(expert_kernel, in_specs=[vmem, hbm, hbm, hbm, vmem], out_s...]
    unnamed x19, local copies, waits for them, and re-layouts: 2.11 us -> 4.42 us
  transfers between devices with their start and end apart: 3 -> 9, of which waited for: 3 -> 4; matrix products, arithmetic and copies ran while one was open for 0% -> 0% of each run, Pallas kernels for 5% -> 6%
where the time goes in v4:
time: 118 us; the launch traced here: 117 us
  blocking collectives  38.1 us (32%)
  Pallas kernels  31.2 us (26%)
  waiting for transfers between devices  21.8 us (18%)
  starting transfers between devices  20 us (17%)
  local copies, waits for them, and re-layouts  4.44 us (4%)
  between operations  1.42 us (1%)
    all_to_all x1, blocking collectives, exchange(): return lax.all_to_all(rows, axes, split_axis=0, concat_axis=0, tiled=True)  38.1 us
    ppermute x7, waiting for transfers between devices, local(): pieces.append(lax.ppermute(attended[step], 'seq', ring))  15.3 us
    pallas_call x1, Pallas kernels, expert(): pl.pallas_call(expert_kernel, in_specs=[vmem, hbm, hbm, hbm, vmem], out_s...  12.4 us
    all_to_all x2, starting transfers between devices, exchange(): return lax.all_to_all(rows, axes, split_axis=0, concat_axis=0, tiled=True)  11.8 us
    ppermute x7, starting transfers between devices, local(): pieces.append(lax.ppermute(attended[step], 'seq', ring))  8.22 us
    all_to_all x2, waiting for transfers between devices, exchange(): return lax.all_to_all(rows, axes, split_axis=0, concat_axis=0, tiled=True)  6.54 us
    pallas_call x1, Pallas kernels, weight_grads(): pl.pallas_call(weight_grad_kernel, grid=(FF // tile,), in_specs=[pl.Block...  4.54 us
    pallas_call x1, Pallas kernels, attend(): pl.pallas_call(attend_kernel, grid=(1,), in_specs=[pl.BlockSpec(memory_sp...  4.53 us
  transfers between devices with their start and end apart: 9, of which 4 were waited for; matrix products, arithmetic and copies ran while one was open for 0% of the time, Pallas kernels for 6%

profile of v4, /device:TPU:1, one launch (start us, length us, event | category | flops | bytes accessed | tf_op | source)
XLA Modules:
  0.0 117.1 jit_solution(11384650882911650128)
XLA Ops:
  0.6 0.0 copy-start.7
  0.6 0.0 copy-start
  0.7 0.0 copy-start.4
  0.7 1.3 %copy.18 = s32[1,128,3]{1,2,0:T(4,128)} copy(s32[1,128,3]{1,0,2:T(1,128)} %param.18) | data formatting | bytes 3072
  2.0 0.0 copy-start.6
  2.0 4.4 %shard_map.137 = bf16[8,208,128]{2,1,0:T(8,128)(2,1)} custom-call(bf16[128,1024]{1,0:T(8,128)(2,1)} %bitcast.30, s32[3,128]{1,0:T(4,128)} %bitcast.35, s32[1,128]{1,0:T(1,128)} %count_ref.5, bf16[1024,1536]{1,0:T(8,128)(2,1)} %weight_ref.1), custom_call_target="tpu_custom_call" | custom-call | flops 402653184 | bytes 4194304 | tf_op jit(solution)/shard_map/pallas_call | solution.py:102
  6.4 5.8 %all-to-all-start = ((bf16[8,208,128]{2,1,0:T(8,128)(2,1)}), bf16[8,208,128]{2,1,0:T(8,128)(2,1)S(1)}, u32[]{:S(2)}, u32[]{:S(2)}) async-start(bf16[8,208,128]{2,1,0:T(8,128)(2,1)} %shard_map.137), calls=%async_computation | async-start | bytes 851968 | tf_op jit(solution)/shard_map/all_to_all | solution.py:469
  12.8 0.0 copy-done.7
  12.9 0.0 copy-done
  12.9 0.0 copy-done.4
  12.9 0.0 copy-done.6
  12.9 1.1 shard_map.138.packed_ref
  14.0 0.1 pad_add_fusion.scalar_ref
  14.1 0.0 copy-start.8
  14.1 6.5 %all-to-all-done.parts_ref = bf16[8,208,128]{2,1,0:T(8,128)(2,1)S(1)} async-done(((bf16[8,208,128]{2,1,0:T(8,128)(2,1)}), bf16[8,208,128]{2,1,0:T(8,128)(2,1)S(1)}, u32[]{:S(2)}, u32[]{:S(2)}) %all-to-all-start) | async-done | bytes 426016 | tf_op jit(solution)/shard_map/all_to_all | solution.py:469
  20.6 0.0 copy-start.2
  20.6 4.5 %shard_map.139 = (bf16[8,64,128]{2,1,0:T(8,128)(2,1)S(1)}, bf16[128,64,128]{2,1,0:T(8,128)(2,1)S(1)}) custom-call(s32[2]{0:T(128)S(1)} %pad_add_fusion.scalar_ref, bf16[8,208,128]{2,1,0:T(8,128)(2,1)S(1)} %all-to-all-done.parts_ref, bf16[128,64,128]{2,1,0:T(8,128)(2,1)S(1)} %shard_map.138.packed_ref), custom_call_target="tpu_custom_call", output_to_operand_aliasing={{1}: (2, {})} | custom-call | flops 268435456 | bytes 1048576 | tf_op jit(solution)/shard_map/pallas_call | solution.py:201
  25.2 38.1 %all_to_all.15.rows_ref = bf16[128,64,128]{2,1,0:T(8,128)(2,1)S(1)} all-to-all(bf16[128,64,128]{2,1,0:T(8,128)(2,1)S(1)} %get-tuple-element.14), channel_id=1, replica_groups=mesh['seq'=8,'exp'=16] {'seq','exp'}, dimensions={0} | all-to-all | bytes 4194304 | tf_op jit(solution)/shard_map/all_to_all | solution.py:469
  63.2 0.0 copy-done.8
  63.2 0.0 copy-done.2
  63.2 12.4 %shard_map.140 = (bf16[128,2,24,128]{3,2,1,0:T(8,128)(2,1)S(1)}, f32[1,1024]{1,0:T(1,128)}, bf16[256,6144]{1,0:T(8,128)(2,1)S(1)}) custom-call(bf16[128,64,128]{2,1,0:T(8,128)(2,1)S(1)} %all_to_all.15.rows_ref, bf16[1024,2048]{1,0:T(8,128)(2,1)} %bitcast.38, bf16[2048,1024]{1,0:T(8,128)(2,1)} %bitcast.39, bf16[512,1024]{1,0:T(8,128)(2,1)S(1)} %copy-done.2, ...), custom_call_target="tpu_custom_call" | custom-call | flops 4294967296 | bytes 14680064 | tf_op jit(solution)/shard_map/pallas_call | solution.py:377
  75.6 0.0 copy-start.1
  75.6 1.1 copy-done.1
  76.8 6.0 %all-to-all-start.2 = ((bf16[128,2,24,128]{3,2,1,0:T(8,128)(2,1)}), bf16[128,2,24,128]{3,2,1,0:T(8,128)(2,1)}, u32[]{:S(2)}, u32[]{:S(2)}) async-start(bf16[128,2,24,128]{3,2,1,0:T(8,128)(2,1)} %copy-done.1), calls=%async_computation.2 | async-start | bytes 3145728 | tf_op jit(solution)/shard_map/all_to_all | solution.py:469
  82.8 1.3 %collective-permute-start.6 = (bf16[64,128]{1,0:T(8,128)(2,1)S(1)}, bf16[64,128]{1,0:T(8,128)(2,1)S(1)}, u32[]{:S(2)}, u32[]{:S(2)}) collective-permute-start(bf16[64,128]{1,0:T(8,128)(2,1)S(1)} %get-tuple-element.23), channel_id=1, source_target_pairs={{0,112},{16,0},{32,16},{48,32},{64,48},{80,64},{96,80},{112,96},{1... | collective-permute-start | bytes 49160 | tf_op jit(solution)/shard_map/ppermute | solution.py:499
  84.0 1.7 %collective-permute-start.5 = (bf16[64,128]{1,0:T(8,128)(2,1)S(1)}, bf16[64,128]{1,0:T(8,128)(2,1)S(1)}, u32[]{:S(2)}, u32[]{:S(2)}) collective-permute-start(bf16[64,128]{1,0:T(8,128)(2,1)S(1)} %get-tuple-element.24), channel_id=1, source_target_pairs={{0,96},{16,112},{32,0},{48,16},{64,32},{80,48},{96,64},{112,80},{1... | collective-permute-start | bytes 49160 | tf_op jit(solution)/shard_map/ppermute | solution.py:499
  85.8 1.0 collective-permute-start.4
  86.8 2.4 %collective-permute-start.3 = (bf16[64,128]{1,0:T(8,128)(2,1)S(1)}, bf16[64,128]{1,0:T(8,128)(2,1)S(1)}, u32[]{:S(2)}, u32[]{:S(2)}) collective-permute-start(bf16[64,128]{1,0:T(8,128)(2,1)S(1)} %get-tuple-element.26), channel_id=1, source_target_pairs={{0,64},{16,80},{32,96},{48,112},{64,0},{80,16},{96,32},{112,48},{1... | collective-permute-start | bytes 49160 | tf_op jit(solution)/shard_map/ppermute | solution.py:499
  89.2 0.6 collective-permute-start.2
  89.9 12.2 %collective-permute-done.6.refs_7_ = bf16[64,128]{1,0:T(8,128)(2,1)S(1)} collective-permute-done((bf16[64,128]{1,0:T(8,128)(2,1)S(1)}, bf16[64,128]{1,0:T(8,128)(2,1)S(1)}, u32[]{:S(2)}, u32[]{:S(2)}) %collective-permute-start.6) | collective-permute-done | bytes 16416 | tf_op jit(solution)/shard_map/ppermute | solution.py:499
  102.1 0.6 collective-permute-start.1
  102.7 0.0 collective-permute-done.5.refs_6_
  102.7 0.5 collective-permute-start
  103.2 0.1 collective-permute-done.4.refs_5_
  103.3 0.0 collective-permute-done.3.refs_4_
  103.3 0.0 collective-permute-done.2.refs_3_
  103.3 3.0 %collective-permute-done.1.refs_2_ = bf16[64,128]{1,0:T(8,128)(2,1)S(1)} collective-permute-done((bf16[64,128]{1,0:T(8,128)(2,1)S(1)}, bf16[64,128]{1,0:T(8,128)(2,1)S(1)}, u32[]{:S(2)}, u32[]{:S(2)}) %collective-permute-start.1) | collective-permute-done | bytes 16416 | tf_op jit(solution)/shard_map/ppermute | solution.py:499
  106.3 0.0 collective-permute-done.refs_1_
  106.3 0.0 copy-start.3
  106.3 1.2 %copy-done.3 = bf16[512,1024]{1,0:T(8,128)(2,1)S(1)} copy-done((bf16[512,1024]{1,0:T(8,128)(2,1)S(1)}, bf16[512,1024]{1,0:T(8,128)(2,1)}, u32[]{:S(2)}) %copy-start.3) | copy-done | bytes 1048600
  107.5 0.9 shard_map.141.resid_ref
  108.5 0.0 copy-start.5
  108.5 0.7 copy-done.5
  109.2 4.5 %shard_map.143 = (bf16[1024,2048]{1,0:T(8,128)(2,1)}, bf16[2048,1024]{1,0:T(8,128)(2,1)}) custom-call(bf16[256,6144]{1,0:T(8,128)(2,1)S(1)} %get-tuple-element.19.picked_ref.before_grad_ref.active_ref.out_grad_ref, bf16[256,6144]{1,0:T(8,128)(2,1)S(1)} %get-tuple-element.19.picked_ref.before_grad_ref.active_ref.out_grad_ref, ...), custom_call_target="tpu_custom_call" | custom-call | flops 2147483648 | bytes 11534336 | tf_op jit(solution)/shard_map/pallas_call | solution.py:412
  113.7 0.0 all-to-all-done.2.rows_ref
  113.7 3.4 %shard_map.142 = (bf16[128,1024]{1,0:T(8,128)(2,1)}, bf16[128,1024]{1,0:T(8,128)(2,1)}) custom-call(bf16[128,2,24,128]{3,2,1,0:T(8,128)(2,1)} %all-to-all-done.2.rows_ref, s32[3,128]{1,0:T(4,128)} %bitcast.36, s32[1,128]{1,0:T(1,128)} %count_ref.5, bf16[128,1024]{1,0:T(8,128)(2,1)} %copy-done.5, bf16[128,1024]{1,0:T(8,128)(2,1)} %bitcast.33), custom_call_target="tpu_custom_call" | custom-call | flops 201326592 | bytes 3145728 | tf_op jit(solution)/shard_map/pallas_call | solution.py:457
  (1 shorter events, 0.0 us)
Async XLA Ops:
  0.6 12.2 %copy-start.7 = (s32[1,128]{1,0:T(1,128)S(1)}, s32[1,128]{1,0:T(1,128)}, u32[]{:S(2)}) copy-start(s32[1,128]{1,0:T(1,128)} %count_ref.5) | copy-start | bytes 1540
  0.6 12.2 %copy-start = (bf16[1,128,1024]{2,1,0:T(8,128)(2,1)S(1)}, bf16[1,128,1024]{2,1,0:T(8,128)(2,1)}, u32[]{:S(2)}) copy-start(bf16[1,128,1024]{2,1,0:T(8,128)(2,1)} %param.10) | copy-start | bytes 786436
  0.7 12.2 %copy-start.4 = (bf16[1,128,1024]{2,1,0:T(8,128)(2,1)S(1)}, bf16[1,128,1024]{2,1,0:T(8,128)(2,1)}, u32[]{:S(2)}) copy-start(bf16[1,128,1024]{2,1,0:T(8,128)(2,1)} %param.11) | copy-start | bytes 786436
  2.0 10.9 %copy-start.6 = (s32[1,128,3]{1,2,0:T(4,128)S(1)}, s32[1,128,3]{1,2,0:T(4,128)}, u32[]{:S(2)}) copy-start(s32[1,128,3]{1,2,0:T(4,128)} %copy.18) | copy-start | bytes 4612
  6.4 14.2 %all-to-all-start = ((bf16[8,208,128]{2,1,0:T(8,128)(2,1)}), bf16[8,208,128]{2,1,0:T(8,128)(2,1)S(1)}, u32[]{:S(2)}, u32[]{:S(2)}) async-start(bf16[8,208,128]{2,1,0:T(8,128)(2,1)} %shard_map.137), calls=%async_computation | async-start | bytes 851968 | tf_op jit(solution)/shard_map/all_to_all | solution.py:469
  14.1 49.2 %copy-start.8 = (f32[1,1024]{1,0:T(1,128)S(1)}, f32[1,1024]{1,0:T(1,128)}, u32[]{:S(2)}) copy-start(f32[1,1024]{1,0:T(1,128)} %router_ref.1) | copy-start | bytes 12292
  20.6 42.6 %copy-start.2 = (bf16[512,1024]{1,0:T(8,128)(2,1)S(1)}, bf16[512,1024]{1,0:T(8,128)(2,1)}, u32[]{:S(2)}) copy-start(bf16[512,1024]{1,0:T(8,128)(2,1)} %refs_9_.1) | copy-start | bytes 3145732
  75.6 1.1 copy-start.1
  76.8 36.9 %all-to-all-start.2 = ((bf16[128,2,24,128]{3,2,1,0:T(8,128)(2,1)}), bf16[128,2,24,128]{3,2,1,0:T(8,128)(2,1)}, u32[]{:S(2)}, u32[]{:S(2)}) async-start(bf16[128,2,24,128]{3,2,1,0:T(8,128)(2,1)} %copy-done.1), calls=%async_computation.2 | async-start | bytes 3145728 | tf_op jit(solution)/shard_map/all_to_all | solution.py:469
  82.8 19.3 %collective-permute-start.6 = (bf16[64,128]{1,0:T(8,128)(2,1)S(1)}, bf16[64,128]{1,0:T(8,128)(2,1)S(1)}, u32[]{:S(2)}, u32[]{:S(2)}) collective-permute-start(bf16[64,128]{1,0:T(8,128)(2,1)S(1)} %get-tuple-element.23), channel_id=1, source_target_pairs={{0,112},{16,0},{32,16},{48,32},{64,48},{80,64},{96,80},{112,96},{1... | collective-permute-start | bytes 49160 | tf_op jit(solution)/shard_map/ppermute | solution.py:499
  84.0 18.7 %collective-permute-start.5 = (bf16[64,128]{1,0:T(8,128)(2,1)S(1)}, bf16[64,128]{1,0:T(8,128)(2,1)S(1)}, u32[]{:S(2)}, u32[]{:S(2)}) collective-permute-start(bf16[64,128]{1,0:T(8,128)(2,1)S(1)} %get-tuple-element.24), channel_id=1, source_target_pairs={{0,96},{16,112},{32,0},{48,16},{64,32},{80,48},{96,64},{112,80},{1... | collective-permute-start | bytes 49160 | tf_op jit(solution)/shard_map/ppermute | solution.py:499
  85.8 17.5 %collective-permute-start.4 = (bf16[64,128]{1,0:T(8,128)(2,1)S(1)}, bf16[64,128]{1,0:T(8,128)(2,1)S(1)}, u32[]{:S(2)}, u32[]{:S(2)}) collective-permute-start(bf16[64,128]{1,0:T(8,128)(2,1)S(1)} %get-tuple-element.25), channel_id=1, source_target_pairs={{0,80},{16,96},{32,112},{48,0},{64,16},{80,32},{96,48},{112,64},{1... | collective-permute-start | bytes 49160 | tf_op jit(solution)/shard_map/ppermute | solution.py:499
  86.8 16.5 %collective-permute-start.3 = (bf16[64,128]{1,0:T(8,128)(2,1)S(1)}, bf16[64,128]{1,0:T(8,128)(2,1)S(1)}, u32[]{:S(2)}, u32[]{:S(2)}) collective-permute-start(bf16[64,128]{1,0:T(8,128)(2,1)S(1)} %get-tuple-element.26), channel_id=1, source_target_pairs={{0,64},{16,80},{32,96},{48,112},{64,0},{80,16},{96,32},{112,48},{1... | collective-permute-start | bytes 49160 | tf_op jit(solution)/shard_map/ppermute | solution.py:499
  89.2 14.1 %collective-permute-start.2 = (bf16[64,128]{1,0:T(8,128)(2,1)S(1)}, bf16[64,128]{1,0:T(8,128)(2,1)S(1)}, u32[]{:S(2)}, u32[]{:S(2)}) collective-permute-start(bf16[64,128]{1,0:T(8,128)(2,1)S(1)} %get-tuple-element.27), channel_id=1, source_target_pairs={{0,48},{16,64},{32,80},{48,96},{64,112},{80,0},{96,16},{112,32},{1... | collective-permute-start | bytes 49160 | tf_op jit(solution)/shard_map/ppermute | solution.py:499
  102.1 4.2 %collective-permute-start.1 = (bf16[64,128]{1,0:T(8,128)(2,1)S(1)}, bf16[64,128]{1,0:T(8,128)(2,1)S(1)}, u32[]{:S(2)}, u32[]{:S(2)}) collective-permute-start(bf16[64,128]{1,0:T(8,128)(2,1)S(1)} %get-tuple-element.28), channel_id=1, source_target_pairs={{0,32},{16,48},{32,64},{48,80},{64,96},{80,112},{96,0},{112,16},{1... | collective-permute-start | bytes 49160 | tf_op jit(solution)/shard_map/ppermute | solution.py:499
  102.7 3.6 %collective-permute-start = (bf16[64,128]{1,0:T(8,128)(2,1)S(1)}, bf16[64,128]{1,0:T(8,128)(2,1)S(1)}, u32[]{:S(2)}, u32[]{:S(2)}) collective-permute-start(bf16[64,128]{1,0:T(8,128)(2,1)S(1)} %get-tuple-element.29), channel_id=1, source_target_pairs={{0,16},{16,32},{32,48},{48,64},{64,80},{80,96},{96,112},{112,0},{1... | collective-permute-start | bytes 49160 | tf_op jit(solution)/shard_map/ppermute | solution.py:499
  106.3 1.2 %copy-start.3 = (bf16[512,1024]{1,0:T(8,128)(2,1)S(1)}, bf16[512,1024]{1,0:T(8,128)(2,1)}, u32[]{:S(2)}) copy-start(bf16[512,1024]{1,0:T(8,128)(2,1)} %refs_9_.1) | copy-start | bytes 3145732
  108.5 0.7 copy-start.5

commit v5 on v4

--- a/solution.py
+++ b/solution.py
@@ -50,7 +50,7 @@
 
 def spread_matrix(index_ref, count_ref, slot):
     frame = lax.broadcasted_iota(jnp.int32, (FR, DEVS), 0)
-    named = jnp.broadcast_to(index_ref[slot : slot + 1, :], (FR, DEVS)) == frame
+    named = jnp.broadcast_to(index_ref[slot], (FR, DEVS)) == frame
     used = jnp.broadcast_to(count_ref[...], (FR, DEVS)) > slot
     return jnp.where(named & used, 1.0, 0.0)
 
@@ -83,7 +83,7 @@
         normed[...] = normalize(frames_ref[...].astype(F32))[0].astype(BF16)
         info = jnp.concatenate(
             [
-                index_ref[...].astype(F32),
+                *[index_ref[slot].astype(F32) for slot in range(SLOT)],
                 count_ref[...].astype(F32),
                 jnp.zeros((INFO - SLOT - 1, DEVS), F32),
             ],
@@ -104,7 +104,7 @@
         grid=(3,),
         in_specs=[
             whole((FR, D)),
-            whole((SLOT, DEVS)),
+            whole((SLOT, 1, DEVS)),
             whole((1, DEVS)),
             pl.BlockSpec((D, HALF), lambda n: (0, n)),
         ],
@@ -142,7 +142,7 @@
     return pl.pallas_call(
         gather_kernel,
         grid=(1,),
-        in_specs=[whole((FR, D)), whole((FR, D)), whole((SLOT, DEVS)), whole((1, DEVS))],
+        in_specs=[whole((FR, D)), whole((FR, D)), whole((SLOT, 1, DEVS)), whole((1, DEVS))],
         out_specs=pl.BlockSpec((DEVS, 2 * ROWS, 128), lambda n: (0, 0, 0)),
         out_shape=jax.ShapeDtypeStruct((DEVS, SENT, 128), BF16),
         scratch_shapes=[pltpu.VMEM((DEVS * ROWS, 128), F32)] * 2,
@@ -281,11 +281,27 @@
 
 
 def expert_kernel(
-    rows_ref, first_hbm, second_hbm, mix_hbm, router_ref,
-    back_ref, route_grad_ref, saved_ref,
-    stage_x, stage_g, stage_a, pulled_ref, first_ref, second_ref, mix_ref,
-    first_sem, second_sem, mix_sem,
+    rows_ref, first_hbm, second_hbm, mix_hbm, router_ref, after_hbm,
+    back_hbm, route_grad_ref, saved_hbm,
+    stage_x, stage_g, stage_a, pulled_ref, first_ref, second_ref, mix_ref, saved_ref, back_ref,
+    first_sem, second_sem, mix_sem, rows_sem, active_sem, before_grad_sem, back_sem,
 ):
+    stores = []
+
+    def save(start, size, sem):
+        columns = pl.ds(start, size)
+        stores.append(pltpu.make_async_copy(
+            saved_ref.at[:, columns], saved_hbm.at[:, columns], sem
+        ))
+        stores[-1].start()
+
+    def leave(stage, half):
+        back_ref[half] = staged(stage).astype(BF16)
+        stores.append(pltpu.make_async_copy(
+            back_ref.at[half], back_hbm.at[:, half], back_sem.at[half]
+        ))
+        stores[-1].start()
+
     picked_ref = saved_ref.at[:, :D]
     out_grad_ref = saved_ref.at[:, D : 2 * D]
     active_ref = saved_ref.at[:, 2 * D : 2 * D + FF]
@@ -338,6 +354,7 @@
     logits = jnp.sum(picked_wide * router_ref[...], axis=-1, keepdims=True)
     gate = 1.0 / (1.0 + jnp.exp(-logits))
     out_grad_ref[...] = (gate * grads.astype(F32)).astype(BF16)
+    save(0, 2 * D, rows_sem)
 
     logit = jnp.zeros((LIVE, 1), F32)
     for step in range(FF_STEPS):
@@ -354,6 +371,8 @@
         )
         active_ref[:, columns] = active
         before_grad_ref[:, columns] = (gate * pulled * slope).astype(BF16)
+        save(2 * D + step * FF_TILE, FF_TILE, active_sem.at[step])
+        save(2 * D + FF + step * FF_TILE, FF_TILE, before_grad_sem.at[step])
         logit += jnp.sum(active.astype(F32) * pulled, axis=-1, keepdims=True)
 
     logit_grad = logit * gate * (1.0 - gate)
@@ -362,22 +381,24 @@
     returned = dot(place, (gate * result).astype(BF16))
     for slot in range(SLOT):
         pack_rows(stage_x, returned[slot * DEVS : (slot + 1) * DEVS], slot)
-    back_ref[:, 0] = staged(stage_x).astype(BF16)
+    leave(stage_x, 0)
     row_grad = dot(before_grad_ref[...], first_ref[...], ((1,), (1,)))
     row_grad = row_grad + logit_grad * router_ref[...]
     row_grad = dot(place, row_grad.astype(BF16))
     for slot in range(SLOT):
         pack_rows(stage_g, row_grad[slot * DEVS : (slot + 1) * DEVS], slot)
-    back_ref[:, 1] = staged(stage_g).astype(BF16)
-
-
-def expert(rows, first, second, mix, router):
+    leave(stage_g, 1)
+    for copy in stores:
+        copy.wait()
+
+
+def expert(rows, first, second, mix, router, after):
     vmem = pl.BlockSpec(memory_space=pltpu.VMEM)
     hbm = pl.BlockSpec(memory_space=pl.ANY)
     return pl.pallas_call(
         expert_kernel,
-        in_specs=[vmem, hbm, hbm, hbm, vmem],
-        out_specs=[vmem, vmem, vmem],
+        in_specs=[vmem, hbm, hbm, hbm, vmem, hbm],
+        out_specs=[hbm, vmem, hbm],
         out_shape=[
             jax.ShapeDtypeStruct((DEVS, 2, ROWS, 128), BF16),
             jax.ShapeDtypeStruct((1, D), F32),
@@ -391,15 +412,21 @@
             pltpu.VMEM((D, FF), BF16),
             pltpu.VMEM((FF, D), BF16),
             pltpu.VMEM((HALF, D), BF16),
+            pltpu.VMEM((LIVE, 2 * D + 2 * FF), BF16),
+            pltpu.VMEM((2, DEVS, ROWS, 128), BF16),
             pltpu.SemaphoreType.DMA((FF_STEPS,)),
             pltpu.SemaphoreType.DMA((FF_STEPS,)),
             pltpu.SemaphoreType.DMA,
-        ],
-        compiler_params=params(44),
+            pltpu.SemaphoreType.DMA,
+            pltpu.SemaphoreType.DMA((FF_STEPS,)),
+            pltpu.SemaphoreType.DMA((FF_STEPS,)),
+            pltpu.SemaphoreType.DMA((2,)),
+        ],
+        compiler_params=params(56),
         cost_estimate=pl.CostEstimate(
             flops=8 * LIVE * D * FF, bytes_accessed=14 * MB, transcendentals=LIVE * FF
         ),
-    )(rows, first, second, mix, router)
+    )(rows, first, second, mix, router, after)
 
 
 def weight_grad_kernel(picked_ref, before_grad_ref, active_ref, out_grad_ref, first_ref, second_ref):
@@ -483,7 +510,7 @@
 ):
     own_frames = frames[0]
     upstream = cotangent[0]
-    index = send_index[0].T
+    index = jnp.transpose(send_index, (2, 0, 1))
     everywhere = ("seq", "exp")
 
     own = lax.axis_index("seq").astype(jnp.int32)
@@ -498,7 +525,9 @@
         ring = [(source, (source + step) % HEADS) for source in range(HEADS)]
         pieces.append(lax.ppermute(attended[step], "seq", ring))
     resid = residual(scalars, pieces, own_frames, out_weight)
-    back, grad_route, saved = expert(arrived, expert_in[0], expert_out[0], out_weight, router)
+    back, grad_route, saved = expert(
+        arrived, expert_in[0], expert_out[0], out_weight, router, resid
+    )
     arrived_back = exchange(back, everywhere)
     grad_first, grad_second = weight_grads(saved)
     output, grad_resid = combine(arrived_back, index, send_count, resid, upstream)

time: 118 us -> 116 us (0.983)
  blocking collectives: 38.1 us -> 0 us
  waiting for transfers between devices: 21.8 us -> 45.7 us
  starting transfers between devices: 20 us -> 32.2 us
  Pallas kernels: 31.2 us -> 35.5 us
  local copies, waits for them, and re-layouts: 4.44 us -> 0.73 us
    all_to_all x1 -> x0, blocking collectives: 38.1 us -> none  [exchange(): return lax.all_to_all(rows, axes, split_axis=0, concat_axis=0, tiled=True)]
    all_to_all x2 -> x3, waiting for transfers between devices: 6.54 us -> 24.8 us  [exchange(): return lax.all_to_all(rows, axes, split_axis=0, concat_axis=0, tiled=True)]
    all_to_all x2 -> x3, starting transfers between devices: 11.8 us -> 24.1 us  [exchange(): return lax.all_to_all(rows, axes, split_axis=0, concat_axis=0, tiled=True)]
    ppermute x7, waiting for transfers between devices: 15.3 us -> 20.9 us  [local(): pieces.append(lax.ppermute(attended[step], 'seq', ring))]
    unnamed x19 -> x14, local copies, waits for them, and re-layouts: 4.42 us -> 0.72 us
    pallas_call x1, Pallas kernels: 12.4 us -> 14.8 us  [expert(): pl.pallas_call(expert_kernel, in_specs=[vmem, hbm, hbm, hbm, vmem, hbm],...]
  transfers between devices with their start and end apart: 9 -> 10, of which waited for: 4 -> 5; matrix products, arithmetic and copies ran while one was open for 0% -> 0% of each run, Pallas kernels for 6% -> 7%
where the time goes in v5:
time: 116 us
  waiting for transfers between devices  45.7 us (39%)
  Pallas kernels  35.5 us (31%)
  starting transfers between devices  32.2 us (28%)
  between operations  1.42 us (1%)
    all_to_all x3, waiting for transfers between devices, exchange(): return lax.all_to_all(rows, axes, split_axis=0, concat_axis=0, tiled=True)  24.8 us
    all_to_all x3, starting transfers between devices, exchange(): return lax.all_to_all(rows, axes, split_axis=0, concat_axis=0, tiled=True)  24.1 us
    ppermute x7, waiting for transfers between devices, local(): pieces.append(lax.ppermute(attended[step], 'seq', ring))  20.9 us
    pallas_call x1, Pallas kernels, expert(): pl.pallas_call(expert_kernel, in_specs=[vmem, hbm, hbm, hbm, vmem, hbm],...  14.8 us
    ppermute x7, starting transfers between devices, local(): pieces.append(lax.ppermute(attended[step], 'seq', ring))  8.17 us
    pallas_call x1, Pallas kernels, attend(): pl.pallas_call(attend_kernel, grid=(1,), in_specs=[pl.BlockSpec(memory_sp...  5.26 us
    pallas_call x1, Pallas kernels, weight_grads(): pl.pallas_call(weight_grad_kernel, grid=(FF // tile,), in_specs=[pl.Block...  4.57 us
    pallas_call x1, Pallas kernels, project(): pl.pallas_call(project_kernel, grid=(3,), in_specs=[whole((FR, D)), whole...  4.56 us
  transfers between devices with their start and end apart: 10, of which 5 were waited for; matrix products, arithmetic and copies ran while one was open for 0% of the time, Pallas kernels for 7%

profile of v5, /device:TPU:1, one launch (start us, length us, event | category | flops | bytes accessed | tf_op | source)
XLA Modules:
  0.0 115.7 jit_solution(14993831554655982548)
XLA Ops:
  0.6 0.0 copy-start.6
  0.6 0.0 copy-start.5
  0.7 0.0 copy-start.1
  0.7 0.0 copy-start.2
  0.7 4.6 %shard_map.137 = bf16[8,208,128]{2,1,0:T(8,128)(2,1)} custom-call(bf16[128,1024]{1,0:T(8,128)(2,1)} %bitcast.26, s32[3,1,128]{2,1,0:T(1,128)} %bitcast.31, s32[1,128]{1,0:T(1,128)} %count_ref.5, bf16[1024,1536]{1,0:T(8,128)(2,1)} %weight_ref.1), custom_call_target="tpu_custom_call" | custom-call | flops 402653184 | bytes 4194304 | tf_op jit(solution)/shard_map/pallas_call | solution.py:102
  5.2 5.8 %all-to-all-start = ((bf16[8,208,128]{2,1,0:T(8,128)(2,1)}), bf16[8,208,128]{2,1,0:T(8,128)(2,1)S(1)}, u32[]{:S(2)}, u32[]{:S(2)}) async-start(bf16[8,208,128]{2,1,0:T(8,128)(2,1)} %shard_map.137), calls=%async_computation | async-start | bytes 851968 | tf_op jit(solution)/shard_map/all_to_all | solution.py:496
  11.7 0.0 copy-done.6
  11.7 0.0 copy-done.5
  11.7 0.0 copy-done.1
  11.7 0.0 copy-done.2
  11.7 2.0 %shard_map.138.packed_ref = bf16[128,64,128]{2,1,0:T(8,128)(2,1)} custom-call(bf16[128,1024]{1,0:T(8,128)(2,1)S(1)} %bitcast.30, bf16[128,1024]{1,0:T(8,128)(2,1)S(1)} %bitcast.27, s32[3,1,128]{2,1,0:T(1,128)S(1)} %bitcast.33, s32[1,128]{1,0:T(1,128)S(1)} %copy-done.6), custom_call_target="tpu_custom_call" | custom-call | flops 201326592 | bytes 3145728 | tf_op jit(solution)/shard_map/pallas_call | solution.py:142
  13.8 0.1 pad_add_fusion.scalar_ref
  13.8 0.0 copy-start.4
  13.8 5.6 %all-to-all-done.parts_ref = bf16[8,208,128]{2,1,0:T(8,128)(2,1)S(1)} async-done(((bf16[8,208,128]{2,1,0:T(8,128)(2,1)}), bf16[8,208,128]{2,1,0:T(8,128)(2,1)S(1)}, u32[]{:S(2)}, u32[]{:S(2)}) %all-to-all-start) | async-done | bytes 426016 | tf_op jit(solution)/shard_map/all_to_all | solution.py:496
  19.5 5.3 %shard_map.139 = (bf16[8,64,128]{2,1,0:T(8,128)(2,1)S(1)}, bf16[128,64,128]{2,1,0:T(8,128)(2,1)}) custom-call(s32[2]{0:T(128)S(1)} %pad_add_fusion.scalar_ref, bf16[8,208,128]{2,1,0:T(8,128)(2,1)S(1)} %all-to-all-done.parts_ref, bf16[128,64,128]{2,1,0:T(8,128)(2,1)} %shard_map.138.packed_ref), custom_call_target="tpu_custom_call", output_to_operand_aliasing={{1}: (2, {})} | custom-call | flops 268435456 | bytes 1048576 | tf_op jit(solution)/shard_map/pallas_call | solution.py:201
  24.7 9.5 %all-to-all-start.1 = ((bf16[128,64,128]{2,1,0:T(8,128)(2,1)}), bf16[128,64,128]{2,1,0:T(8,128)(2,1)}, u32[]{:S(2)}, u32[]{:S(2)}) async-start(bf16[128,64,128]{2,1,0:T(8,128)(2,1)} %get-tuple-element.14), calls=%async_computation.1 | async-start | bytes 4194304 | tf_op jit(solution)/shard_map/all_to_all | solution.py:496
  34.2 1.2 collective-permute-start.6
  35.4 1.8 %collective-permute-start.5 = (bf16[64,128]{1,0:T(8,128)(2,1)S(1)}, bf16[64,128]{1,0:T(8,128)(2,1)S(1)}, u32[]{:S(2)}, u32[]{:S(2)}) collective-permute-start(bf16[64,128]{1,0:T(8,128)(2,1)S(1)} %get-tuple-element.24), channel_id=1, source_target_pairs={{0,96},{16,112},{32,0},{48,16},{64,32},{80,48},{96,64},{112,80},{1... | collective-permute-start | bytes 49160 | tf_op jit(solution)/shard_map/ppermute | solution.py:526
  37.2 1.1 collective-permute-start.4
  38.2 2.4 %collective-permute-start.3 = (bf16[64,128]{1,0:T(8,128)(2,1)S(1)}, bf16[64,128]{1,0:T(8,128)(2,1)S(1)}, u32[]{:S(2)}, u32[]{:S(2)}) collective-permute-start(bf16[64,128]{1,0:T(8,128)(2,1)S(1)} %get-tuple-element.26), channel_id=1, source_target_pairs={{0,64},{16,80},{32,96},{48,112},{64,0},{80,16},{96,32},{112,48},{1... | collective-permute-start | bytes 49160 | tf_op jit(solution)/shard_map/ppermute | solution.py:526
  40.6 0.7 collective-permute-start.2
  41.3 17.8 %collective-permute-done.6.refs_7_ = bf16[64,128]{1,0:T(8,128)(2,1)S(1)} collective-permute-done((bf16[64,128]{1,0:T(8,128)(2,1)S(1)}, bf16[64,128]{1,0:T(8,128)(2,1)S(1)}, u32[]{:S(2)}, u32[]{:S(2)}) %collective-permute-start.6) | collective-permute-done | bytes 16416 | tf_op jit(solution)/shard_map/ppermute | solution.py:526
  59.1 0.7 collective-permute-start.1
  59.8 0.0 collective-permute-done.5.refs_6_
  59.8 0.4 collective-permute-start
  60.2 0.1 collective-permute-done.4.refs_5_
  60.3 0.0 collective-permute-done.3.refs_4_
  60.3 0.0 collective-permute-done.2.refs_3_
  60.3 3.0 %collective-permute-done.1.refs_2_ = bf16[64,128]{1,0:T(8,128)(2,1)S(1)} collective-permute-done((bf16[64,128]{1,0:T(8,128)(2,1)S(1)}, bf16[64,128]{1,0:T(8,128)(2,1)S(1)}, u32[]{:S(2)}, u32[]{:S(2)}) %collective-permute-start.1) | collective-permute-done | bytes 16416 | tf_op jit(solution)/shard_map/ppermute | solution.py:526
  63.3 0.0 collective-permute-done.refs_1_
  63.3 0.0 copy-done.4
  63.3 0.9 shard_map.140.after_hbm.resid_ref
  64.2 0.0 copy-start.3
  64.3 0.7 copy-done.3
  64.9 0.0 all-to-all-done.1.rows_ref
  64.9 14.8 %shard_map.141 = (bf16[128,2,24,128]{3,2,1,0:T(8,128)(2,1)}, f32[1,1024]{1,0:T(1,128)}, bf16[256,6144]{1,0:T(8,128)(2,1)}) custom-call(bf16[128,64,128]{2,1,0:T(8,128)(2,1)} %all-to-all-done.1.rows_ref, bf16[1024,2048]{1,0:T(8,128)(2,1)} %bitcast.34, bf16[2048,1024]{1,0:T(8,128)(2,1)} %bitcast.35, bf16[512,1024]{1,0:T(8,128)(2,1)} %mix_hbm.1, ...), custom_call_target="tpu_custom_call" | custom-call | flops 4294967296 | bytes 14680064 | tf_op jit(solution)/shard_map/pallas_call | solution.py:398
  79.7 0.0 copy-start
  79.7 8.8 %all-to-all-start.2 = ((bf16[128,2,24,128]{3,2,1,0:T(8,128)(2,1)}), bf16[128,2,24,128]{3,2,1,0:T(8,128)(2,1)}, u32[]{:S(2)}, u32[]{:S(2)}) async-start(bf16[128,2,24,128]{3,2,1,0:T(8,128)(2,1)} %get-tuple-element.16), calls=%async_computation.2 | async-start | bytes 3145728 | tf_op jit(solution)/shard_map/all_to_all | solution.py:496
  88.5 0.0 copy-done
  88.5 4.6 %shard_map.143 = (bf16[1024,2048]{1,0:T(8,128)(2,1)}, bf16[2048,1024]{1,0:T(8,128)(2,1)}) custom-call(bf16[256,6144]{1,0:T(8,128)(2,1)S(1)} %copy-done, bf16[256,6144]{1,0:T(8,128)(2,1)S(1)} %copy-done, bf16[256,6144]{1,0:T(8,128)(2,1)S(1)} %copy-done, bf16[256,6144]{1,0:T(8,128)(2,1)S(1)} %copy-done), custom_call_target="tpu_custom_call" | custom-call | flops 2147483648 | bytes 11534336 | tf_op jit(solution)/shard_map/pallas_call | solution.py:439
  93.1 19.2 %all-to-all-done.2.rows_ref = bf16[128,2,24,128]{3,2,1,0:T(8,128)(2,1)} async-done(((bf16[128,2,24,128]{3,2,1,0:T(8,128)(2,1)}), bf16[128,2,24,128]{3,2,1,0:T(8,128)(2,1)}, u32[]{:S(2)}, u32[]{:S(2)}) %all-to-all-start.2) | async-done | bytes 1572896 | tf_op jit(solution)/shard_map/all_to_all | solution.py:496
  112.3 3.4 %shard_map.142 = (bf16[128,1024]{1,0:T(8,128)(2,1)}, bf16[128,1024]{1,0:T(8,128)(2,1)}) custom-call(bf16[128,2,24,128]{3,2,1,0:T(8,128)(2,1)} %all-to-all-done.2.rows_ref, s32[3,1,128]{2,1,0:T(1,128)} %bitcast.32, s32[1,128]{1,0:T(1,128)} %count_ref.5, bf16[128,1024]{1,0:T(8,128)(2,1)} %copy-done.3, bf16[128,1024]{1,0:T(8,128)(2,1)} %bitcast.29), custom_call_target="tpu_custom_call" | custom-call | flops 201326592 | bytes 3145728 | tf_op jit(solution)/shard_map/pallas_call | solution.py:484
  (1 shorter events, 0.0 us)
Async XLA Ops:
  0.6 11.1 %copy-start.6 = (s32[1,128]{1,0:T(1,128)S(1)}, s32[1,128]{1,0:T(1,128)}, u32[]{:S(2)}) copy-start(s32[1,128]{1,0:T(1,128)} %count_ref.5) | copy-start | bytes 1540
  0.6 11.1 %copy-start.5 = (s32[1,128,3]{1,0,2:T(1,128)S(1)}, s32[1,128,3]{1,0,2:T(1,128)}, u32[]{:S(2)}) copy-start(s32[1,128,3]{1,0,2:T(1,128)} %param.18) | copy-start | bytes 4612
  0.7 11.1 %copy-start.1 = (bf16[1,128,1024]{2,1,0:T(8,128)(2,1)S(1)}, bf16[1,128,1024]{2,1,0:T(8,128)(2,1)}, u32[]{:S(2)}) copy-start(bf16[1,128,1024]{2,1,0:T(8,128)(2,1)} %param.10) | copy-start | bytes 786436
  0.7 11.1 %copy-start.2 = (bf16[1,128,1024]{2,1,0:T(8,128)(2,1)S(1)}, bf16[1,128,1024]{2,1,0:T(8,128)(2,1)}, u32[]{:S(2)}) copy-start(bf16[1,128,1024]{2,1,0:T(8,128)(2,1)} %param.11) | copy-start | bytes 786436
  5.2 14.2 %all-to-all-start = ((bf16[8,208,128]{2,1,0:T(8,128)(2,1)}), bf16[8,208,128]{2,1,0:T(8,128)(2,1)S(1)}, u32[]{:S(2)}, u32[]{:S(2)}) async-start(bf16[8,208,128]{2,1,0:T(8,128)(2,1)} %shard_map.137), calls=%async_computation | async-start | bytes 851968 | tf_op jit(solution)/shard_map/all_to_all | solution.py:496
  13.8 49.5 %copy-start.4 = (bf16[512,1024]{1,0:T(8,128)(2,1)S(1)}, bf16[512,1024]{1,0:T(8,128)(2,1)}, u32[]{:S(2)}) copy-start(bf16[512,1024]{1,0:T(8,128)(2,1)} %mix_hbm.1) | copy-start | bytes 3145732
  24.7 40.2 %all-to-all-start.1 = ((bf16[128,64,128]{2,1,0:T(8,128)(2,1)}), bf16[128,64,128]{2,1,0:T(8,128)(2,1)}, u32[]{:S(2)}, u32[]{:S(2)}) async-start(bf16[128,64,128]{2,1,0:T(8,128)(2,1)} %get-tuple-element.14), calls=%async_computation.1 | async-start | bytes 4194304 | tf_op jit(solution)/shard_map/all_to_all | solution.py:496
  34.2 24.9 %collective-permute-start.6 = (bf16[64,128]{1,0:T(8,128)(2,1)S(1)}, bf16[64,128]{1,0:T(8,128)(2,1)S(1)}, u32[]{:S(2)}, u32[]{:S(2)}) collective-permute-start(bf16[64,128]{1,0:T(8,128)(2,1)S(1)} %get-tuple-element.23), channel_id=1, source_target_pairs={{0,112},{16,0},{32,16},{48,32},{64,48},{80,64},{96,80},{112,96},{1... | collective-permute-start | bytes 49160 | tf_op jit(solution)/shard_map/ppermute | solution.py:526
  35.4 24.4 %collective-permute-start.5 = (bf16[64,128]{1,0:T(8,128)(2,1)S(1)}, bf16[64,128]{1,0:T(8,128)(2,1)S(1)}, u32[]{:S(2)}, u32[]{:S(2)}) collective-permute-start(bf16[64,128]{1,0:T(8,128)(2,1)S(1)} %get-tuple-element.24), channel_id=1, source_target_pairs={{0,96},{16,112},{32,0},{48,16},{64,32},{80,48},{96,64},{112,80},{1... | collective-permute-start | bytes 49160 | tf_op jit(solution)/shard_map/ppermute | solution.py:526
  37.2 23.1 %collective-permute-start.4 = (bf16[64,128]{1,0:T(8,128)(2,1)S(1)}, bf16[64,128]{1,0:T(8,128)(2,1)S(1)}, u32[]{:S(2)}, u32[]{:S(2)}) collective-permute-start(bf16[64,128]{1,0:T(8,128)(2,1)S(1)} %get-tuple-element.25), channel_id=1, source_target_pairs={{0,80},{16,96},{32,112},{48,0},{64,16},{80,32},{96,48},{112,64},{1... | collective-permute-start | bytes 49160 | tf_op jit(solution)/shard_map/ppermute | solution.py:526
  38.2 22.1 %collective-permute-start.3 = (bf16[64,128]{1,0:T(8,128)(2,1)S(1)}, bf16[64,128]{1,0:T(8,128)(2,1)S(1)}, u32[]{:S(2)}, u32[]{:S(2)}) collective-permute-start(bf16[64,128]{1,0:T(8,128)(2,1)S(1)} %get-tuple-element.26), channel_id=1, source_target_pairs={{0,64},{16,80},{32,96},{48,112},{64,0},{80,16},{96,32},{112,48},{1... | collective-permute-start | bytes 49160 | tf_op jit(solution)/shard_map/ppermute | solution.py:526
  40.6 19.7 %collective-permute-start.2 = (bf16[64,128]{1,0:T(8,128)(2,1)S(1)}, bf16[64,128]{1,0:T(8,128)(2,1)S(1)}, u32[]{:S(2)}, u32[]{:S(2)}) collective-permute-start(bf16[64,128]{1,0:T(8,128)(2,1)S(1)} %get-tuple-element.27), channel_id=1, source_target_pairs={{0,48},{16,64},{32,80},{48,96},{64,112},{80,0},{96,16},{112,32},{1... | collective-permute-start | bytes 49160 | tf_op jit(solution)/shard_map/ppermute | solution.py:526
  59.1 4.2 %collective-permute-start.1 = (bf16[64,128]{1,0:T(8,128)(2,1)S(1)}, bf16[64,128]{1,0:T(8,128)(2,1)S(1)}, u32[]{:S(2)}, u32[]{:S(2)}) collective-permute-start(bf16[64,128]{1,0:T(8,128)(2,1)S(1)} %get-tuple-element.28), channel_id=1, source_target_pairs={{0,32},{16,48},{32,64},{48,80},{64,96},{80,112},{96,0},{112,16},{1... | collective-permute-start | bytes 49160 | tf_op jit(solution)/shard_map/ppermute | solution.py:526
  59.8 3.5 %collective-permute-start = (bf16[64,128]{1,0:T(8,128)(2,1)S(1)}, bf16[64,128]{1,0:T(8,128)(2,1)S(1)}, u32[]{:S(2)}, u32[]{:S(2)}) collective-permute-start(bf16[64,128]{1,0:T(8,128)(2,1)S(1)} %get-tuple-element.29), channel_id=1, source_target_pairs={{0,16},{16,32},{32,48},{48,64},{64,80},{80,96},{96,112},{112,0},{1... | collective-permute-start | bytes 49160 | tf_op jit(solution)/shard_map/ppermute | solution.py:526
  64.2 0.7 copy-start.3
  79.7 8.8 %copy-start = (bf16[256,6144]{1,0:T(8,128)(2,1)S(1)}, bf16[256,6144]{1,0:T(8,128)(2,1)}, u32[]{:S(2)}) copy-start(bf16[256,6144]{1,0:T(8,128)(2,1)} %get-tuple-element.19.picked_ref.before_grad_ref.active_ref.out_grad_ref) | copy-start | bytes 9437188
  79.7 32.6 %all-to-all-start.2 = ((bf16[128,2,24,128]{3,2,1,0:T(8,128)(2,1)}), bf16[128,2,24,128]{3,2,1,0:T(8,128)(2,1)}, u32[]{:S(2)}, u32[]{:S(2)}) async-start(bf16[128,2,24,128]{3,2,1,0:T(8,128)(2,1)} %get-tuple-element.16), calls=%async_computation.2 | async-start | bytes 3145728 | tf_op jit(solution)/shard_map/all_to_all | solution.py:496

commit v6 on v3

--- a/solution.py
+++ b/solution.py
@@ -49,7 +49,7 @@
 
 def spread_matrix(index_ref, count_ref, slot):
     frame = lax.broadcasted_iota(jnp.int32, (FR, DEVS), 0)
-    named = jnp.broadcast_to(index_ref[slot : slot + 1, :], (FR, DEVS)) == frame
+    named = jnp.broadcast_to(index_ref[slot], (FR, DEVS)) == frame
     used = jnp.broadcast_to(count_ref[...], (FR, DEVS)) > slot
     return jnp.where(named & used, 1.0, 0.0)
 
@@ -73,27 +73,39 @@
 HALF = HEADS * HD
 
 
-def project_kernel(frames_ref, weight_ref, out_ref, normed):
-    step = pl.program_id(0)
-
-    @pl.when(step == 0)
-    def _():
-        normed[...] = normalize(frames_ref[...].astype(F32))[0].astype(BF16)
-
-    block = dot(normed[...], weight_ref[...]).T.astype(BF16)
-    for head in range(HEADS):
-        start = pl.multiple_of(head * PART + step * HD, HD)
-        out_ref[pl.ds(start, HD), :] = block[head * HD : (head + 1) * HD]
+PROJECT_STEPS = 3
+
+
+def project_kernel(frames_ref, weight_hbm, out_ref, weight_ref, sems):
+    width = 3 * HALF // PROJECT_STEPS
+    loads = []
+    for step in range(PROJECT_STEPS):
+        columns = pl.ds(step * width, width)
+        loads.append(pltpu.make_async_copy(
+            weight_hbm.at[:, columns], weight_ref.at[:, columns], sems.at[step]
+        ))
+        loads[-1].start()
+    normed = normalize(frames_ref[...].astype(F32))[0].astype(BF16)
+    for step in range(PROJECT_STEPS):
+        loads[step].wait()
+        block = dot(normed, weight_ref[:, pl.ds(step * width, width)]).astype(BF16).T
+        for piece in range(width // HD):
+            part, head = divmod(step * width // HD + piece, HEADS)
+            start = head * PART + part * HD
+            out_ref[start : start + HD, :] = block[piece * HD : (piece + 1) * HD]
 
 
 def project(frames, weight):
+    vmem = pl.BlockSpec(memory_space=pltpu.VMEM)
     return pl.pallas_call(
         project_kernel,
-        grid=(3,),
-        in_specs=[whole((FR, D)), pl.BlockSpec((D, HALF), lambda n: (0, n))],
-        out_specs=whole((HEADS * PART, FR)),
+        in_specs=[vmem, pl.BlockSpec(memory_space=pl.ANY)],
+        out_specs=vmem,
         out_shape=jax.ShapeDtypeStruct((HEADS * PART, FR), BF16),
-        scratch_shapes=[pltpu.VMEM((FR, D), BF16)],
+        scratch_shapes=[
+            pltpu.VMEM((D, 3 * HALF), BF16),
+            pltpu.SemaphoreType.DMA((PROJECT_STEPS,)),
+        ],
         compiler_params=params(56),
         cost_estimate=pl.CostEstimate(
             flops=2 * FR * D * 3 * HALF, bytes_accessed=4 * MB, transcendentals=0
@@ -119,7 +131,7 @@
     return pl.pallas_call(
         gather_kernel,
         grid=(1,),
-        in_specs=[whole((FR, D)), whole((SLOT, DEVS)), whole((1, DEVS))],
+        in_specs=[whole((FR, D)), whole((SLOT, 1, DEVS)), whole((1, DEVS))],
         out_specs=pl.BlockSpec((DEVS, 1, ROWS, 128), lambda n: (0, 1, 0, 0)),
         out_shape=jax.ShapeDtypeStruct((DEVS, 2, ROWS, 128), BF16),
         scratch_shapes=[pltpu.VMEM((DEVS * ROWS, 128), F32)],
@@ -130,7 +142,7 @@
     )(table, index, count)
 
 
-QUERIES = 256
+QUERIES = 1024
 
 
 def attend_kernel(length_ref, parts_ref, out_ref):
@@ -175,9 +187,10 @@
     resid = (frames_ref[...].astype(F32) + dot(attended, weight_ref[...])).astype(BF16)
     resid_ref[...] = resid
     mid = normalize(resid.astype(F32))[0].astype(BF16)
+    picks = [spread_matrix(index_ref, count_ref, slot).T for slot in range(SLOT)]
+    rows = dot(jnp.concatenate(picks, axis=0).astype(BF16), mid)
     for slot in range(SLOT):
-        pick = spread_matrix(index_ref, count_ref, slot).T.astype(BF16)
-        pack_rows(stage, dot(pick, mid), slot)
+        pack_rows(stage, rows[slot * DEVS : (slot + 1) * DEVS], slot)
     out_ref[...] = staged(stage)
 
 
@@ -189,7 +202,7 @@
             whole((HALF, FR)),
             whole((FR, D)),
             whole((HALF, D)),
-            whole((SLOT, DEVS)),
+            whole((SLOT, 1, DEVS)),
             whole((1, DEVS)),
             pl.BlockSpec(memory_space=pl.ANY),
         ],
@@ -211,7 +224,7 @@
     )(attended, frames, weight, index, count, packed)
 
 
-FF_TILE = 1024
+FF_TILE = 2048
 FF_STEPS = FF // FF_TILE
 WG_TILE = 512
 gelu_scale = (2.0 / jnp.pi) ** 0.5
@@ -259,13 +272,15 @@
     place = seats(grads[:, 0:128])
     take = place.T.astype(BF16)
     place = place.astype(BF16)
-    grads = dot(take, grads.astype(BF16)).astype(BF16)
+    stage_rows(stage_x, rows_ref, 0)
+    rows = [unpack_rows(stage_x, slot) for slot in range(SLOT)]
+    both = jnp.concatenate([grads, jnp.concatenate(rows, axis=0)], axis=1)
+    both = dot(take, both.astype(BF16))
+    grads = both[:, :D].astype(BF16)
+    picked_wide = both[:, D:]
     for step in range(FF_STEPS):
         second_loads[step].wait()
         pulled_ref[:, tiles(step)] = dot(grads, second_ref[tiles(step), :], ((1,), (1,)))
-    stage_rows(stage_x, rows_ref, 0)
-    rows = [unpack_rows(stage_x, slot).astype(BF16) for slot in range(SLOT)]
-    picked_wide = dot(take, jnp.concatenate(rows, axis=0))
     picked = picked_wide.astype(BF16)
     picked_ref[...] = picked
     logits = jnp.sum(picked_wide * router_ref[...], axis=-1, keepdims=True)
@@ -291,16 +306,15 @@
 
     logit_grad = logit * gate * (1.0 - gate)
     route_grad_ref[...] = jnp.sum(logit_grad * picked_ref[...].astype(F32), axis=0, keepdims=True)
-    result = dot(active_ref[...], second_ref[...])
-    returned = dot(place, (gate * result).astype(BF16))
+    returned = (gate * dot(active_ref[...], second_ref[...])).astype(BF16)
+    row_grad = dot(before_grad_ref[...], first_ref[...], ((1,), (1,)))
+    row_grad = (row_grad + logit_grad * router_ref[...]).astype(BF16)
+    back = dot(place, jnp.concatenate([returned, row_grad], axis=1))
     for slot in range(SLOT):
-        pack_rows(stage_x, returned[slot * DEVS : (slot + 1) * DEVS], slot)
+        sources = slice(slot * DEVS, (slot + 1) * DEVS)
+        pack_rows(stage_x, back[sources, :D], slot)
+        pack_rows(stage_g, back[sources, D:], slot)
     back_ref[:, 0:1] = staged(stage_x)
-    row_grad = dot(before_grad_ref[...], first_ref[...], ((1,), (1,)))
-    row_grad = row_grad + logit_grad * router_ref[...]
-    row_grad = dot(place, row_grad.astype(BF16))
-    for slot in range(SLOT):
-        pack_rows(stage_g, row_grad[slot * DEVS : (slot + 1) * DEVS], slot)
     back_ref[:, 1:2] = staged(stage_g)
 
 
@@ -368,12 +382,14 @@
 ):
     stage_rows(stage, rows_ref, 0)
     stage_rows(stage_g, rows_ref, 1)
-    mixture = jnp.zeros((FR, D), F32)
-    normed_grad = jnp.zeros((FR, D), F32)
-    for slot in range(SLOT):
-        spread = spread_matrix(index_ref, count_ref, slot).astype(BF16)
-        mixture += dot(spread, unpack_rows(stage, slot).astype(BF16))
-        normed_grad += dot(spread, unpack_rows(stage_g, slot).astype(BF16))
+    spreads = [spread_matrix(index_ref, count_ref, slot).astype(BF16) for slot in range(SLOT)]
+    rows = [
+        jnp.concatenate([unpack_rows(stage, slot), unpack_rows(stage_g, slot)], axis=1)
+        for slot in range(SLOT)
+    ]
+    sums = dot(jnp.concatenate(spreads, axis=1), jnp.concatenate(rows, axis=0).astype(BF16))
+    mixture = sums[:, :D]
+    normed_grad = sums[:, D:]
     resid = resid_ref[...].astype(F32)
     output_ref[...] = (resid + mixture).astype(BF16)
     unit, inverse = normalize(resid)
@@ -388,7 +404,7 @@
         combine_kernel,
         out_shape=[jax.ShapeDtypeStruct((FR, D), BF16)] * 2,
         scratch_shapes=[pltpu.VMEM((DEVS * ROWS, 128), F32)] * 2,
-        compiler_params=params(28),
+        compiler_params=params(56),
         cost_estimate=pl.CostEstimate(
             flops=4 * DEVS * SLOT * FR * D, bytes_accessed=3 * MB, transcendentals=0
         ),
@@ -413,7 +429,7 @@
 ):
     own_frames = frames[0]
     upstream = cotangent[0]
-    index = send_index[0].T
+    index = jnp.transpose(send_index, (2, 0, 1))
     everywhere = ("seq", "exp")
 
     parts = project(own_frames, qkv_weight).reshape(HEADS, PART, FR)

time: 111 us -> 110 us (level)
    pallas_call x1, Pallas kernels: 3.57 us -> 2.42 us  [attend(): pl.pallas_call(attend_kernel, in_specs=[pl.BlockSpec(memory_space=pltpu.S...]
where the time goes in v6:
time: 110 us; the launch traced here: 109 us
  blocking collectives  32.9 us (30%)
  waiting for transfers between devices  31.4 us (29%)
  Pallas kernels  26.6 us (24%)
  starting transfers between devices  16 us (15%)
  between operations  1.4 us (1%)
  local copies, waits for them, and re-layouts  1.18 us (1%)
    all_to_all x1, blocking collectives, exchange(): return lax.all_to_all(rows, axes, split_axis=0, concat_axis=0, tiled=True)  32.9 us
    all_to_all x3, waiting for transfers between devices, exchange(): return lax.all_to_all(rows, axes, split_axis=0, concat_axis=0, tiled=True)  31.4 us
    all_to_all x3, starting transfers between devices, exchange(): return lax.all_to_all(rows, axes, split_axis=0, concat_axis=0, tiled=True)  16 us
    pallas_call x1, Pallas kernels, expert(): pl.pallas_call(expert_kernel, in_specs=[vmem, hbm, hbm, vmem], out_specs=...  10.4 us
    pallas_call x1, Pallas kernels, weight_grads(): pl.pallas_call(weight_grad_kernel, grid=(FF // tile,), in_specs=[pl.Block...  4.57 us
    pallas_call x1, Pallas kernels, project(): pl.pallas_call(project_kernel, in_specs=[vmem, pl.BlockSpec(memory_space=...  4.13 us
    pallas_call x1, Pallas kernels, combine(): pl.pallas_call(combine_kernel, out_shape=[jax.ShapeDtypeStruct((FR, D), B...  3.34 us
    pallas_call x1, Pallas kernels, attend(): pl.pallas_call(attend_kernel, in_specs=[pl.BlockSpec(memory_space=pltpu.S...  2.42 us
  transfers between devices with their start and end apart: 3, of which 3 were waited for; matrix products, arithmetic and copies ran while one was open for 0% of the time, Pallas kernels for 5%

profile of v6, /device:TPU:1, one launch (start us, length us, event | category | flops | bytes accessed | tf_op | source)
XLA Modules:
  0.0 109.5 jit_solution(8354151238555973753)
XLA Ops:
  0.6 0.0 copy-start.2
  0.6 0.0 copy-start.5
  0.7 0.0 copy-start.6
  0.7 4.1 %shard_map.137 = bf16[1536,128]{1,0:T(8,128)(2,1)} custom-call(bf16[128,1024]{1,0:T(8,128)(2,1)} %bitcast.15, bf16[1024,1536]{1,0:T(8,128)(2,1)} %weight_hbm.1), custom_call_target="tpu_custom_call" | custom-call | flops 402653184 | bytes 4194304 | tf_op jit(solution)/shard_map/pallas_call | solution.py:100
  4.8 0.0 copy-start.1
  4.8 0.0 copy-start.3
  4.8 6.0 %all-to-all-start = ((bf16[8,192,128]{2,1,0:T(8,128)(2,1)}), bf16[8,192,128]{2,1,0:T(8,128)(2,1)S(1)}, u32[]{:S(2)}, u32[]{:S(2)}) async-start(bf16[8,192,128]{2,1,0:T(8,128)(2,1)} %bitcast.22), calls=%async_computation | async-start | bytes 786432 | tf_op jit(solution)/shard_map/all_to_all | solution.py:415
  11.4 7.4 %all-to-all-done = bf16[8,192,128]{2,1,0:T(8,128)(2,1)S(1)} async-done(((bf16[8,192,128]{2,1,0:T(8,128)(2,1)}), bf16[8,192,128]{2,1,0:T(8,128)(2,1)S(1)}, u32[]{:S(2)}, u32[]{:S(2)}) %all-to-all-start) | async-done | bytes 393248 | tf_op jit(solution)/shard_map/all_to_all | solution.py:415
  18.9 2.4 %shard_map.138 = bf16[512,128]{1,0:T(8,128)(2,1)} custom-call(s32[1]{0:T(128)S(6)} %copy.17.length_ref, bf16[1536,128]{1,0:T(8,128)(2,1)S(1)} %bitcast.18), custom_call_target="tpu_custom_call" | custom-call | flops 268435456 | bytes 524288 | tf_op jit(solution)/shard_map/pallas_call | solution.py:168
  21.3 4.2 %all-to-all-start.1 = ((bf16[8,64,128]{2,1,0:T(8,128)(2,1)}), bf16[8,64,128]{2,1,0:T(8,128)(2,1)S(1)}, u32[]{:S(2)}, u32[]{:S(2)}) async-start(bf16[8,64,128]{2,1,0:T(8,128)(2,1)} %bitcast.3), calls=%async_computation.1 | async-start | bytes 262144 | tf_op jit(solution)/shard_map/all_to_all | solution.py:415
  25.4 0.0 copy-done.2
  25.4 0.0 copy-done.5
  25.4 0.0 copy-done.6
  25.4 0.6 shard_map.139.packed_ref
  26.1 0.0 copy-start.7
  26.1 4.6 %all-to-all-done.1 = bf16[8,64,128]{2,1,0:T(8,128)(2,1)S(1)} async-done(((bf16[8,64,128]{2,1,0:T(8,128)(2,1)}), bf16[8,64,128]{2,1,0:T(8,128)(2,1)S(1)}, u32[]{:S(2)}, u32[]{:S(2)}) %all-to-all-start.1) | async-done | bytes 131104 | tf_op jit(solution)/shard_map/all_to_all | solution.py:415
  30.7 0.0 copy-done.1
  30.7 0.0 copy-done.3
  30.7 1.1 %shard_map.140 = (bf16[128,1024]{1,0:T(8,128)(2,1)S(1)}, bf16[128,2,24,128]{3,2,1,0:T(8,128)(2,1)S(1)}) custom-call(bf16[512,128]{1,0:T(8,128)(2,1)S(1)} %bitcast.17, bf16[128,1024]{1,0:T(8,128)(2,1)S(1)} %bitcast.16, bf16[512,1024]{1,0:T(8,128)(2,1)S(1)} %copy-done.1, s32[3,1,128]{2,1,0:T(1,128)S(1)} %bitcast.21, ...), custom_call_target="tpu_custom_call", output_to_operand_aliasing={{1}: (5, {})} | custom-call | flops 234881024 | bytes 3145728 | tf_op jit(solution)/shard_map/pallas_call | solution.py:198
  31.9 0.0 copy-start.4
  31.9 32.9 %all_to_all.20.rows_ref = bf16[128,2,24,128]{3,2,1,0:T(8,128)(2,1)S(1)} all-to-all(bf16[128,2,24,128]{3,2,1,0:T(8,128)(2,1)S(1)} %get-tuple-element.14), channel_id=1, replica_groups=mesh['seq'=8,'exp'=16] {'seq','exp'}, dimensions={0} | all-to-all | bytes 3145728 | tf_op jit(solution)/shard_map/all_to_all | solution.py:415
  64.8 0.0 copy-done.4
  64.8 0.0 copy-done.7
  64.8 10.4 %shard_map.141 = (bf16[128,2,24,128]{3,2,1,0:T(8,128)(2,1)S(1)}, f32[1,1024]{1,0:T(1,128)}, bf16[256,6144]{1,0:T(8,128)(2,1)S(1)}) custom-call(bf16[128,2,24,128]{3,2,1,0:T(8,128)(2,1)S(1)} %all_to_all.20.rows_ref, bf16[1024,2048]{1,0:T(8,128)(2,1)} %bitcast.23, bf16[2048,1024]{1,0:T(8,128)(2,1)} %bitcast.24, f32[1,1024]{1,0:T(1,128)S(1)} %copy-done.7), custom_call_target="tpu_custom_call" | custom-call | flops 4294967296 | bytes 14680064 | tf_op jit(solution)/shard_map/pallas_call | solution.py:324
  75.2 0.0 copy-start
  75.2 1.1 %copy-done = bf16[128,2,24,128]{3,2,1,0:T(8,128)(2,1)} copy-done((bf16[128,2,24,128]{3,2,1,0:T(8,128)(2,1)}, bf16[128,2,24,128]{3,2,1,0:T(8,128)(2,1)S(1)}, u32[]{:S(2)}) %copy-start) | copy-done | bytes 1572888
  76.3 5.9 %all-to-all-start.3 = ((bf16[128,2,24,128]{3,2,1,0:T(8,128)(2,1)}), bf16[128,2,24,128]{3,2,1,0:T(8,128)(2,1)}, u32[]{:S(2)}, u32[]{:S(2)}) async-start(bf16[128,2,24,128]{3,2,1,0:T(8,128)(2,1)} %copy-done), calls=%async_computation.3 | async-start | bytes 3145728 | tf_op jit(solution)/shard_map/all_to_all | solution.py:415
  82.2 4.6 %shard_map.143 = (bf16[1024,2048]{1,0:T(8,128)(2,1)}, bf16[2048,1024]{1,0:T(8,128)(2,1)}) custom-call(bf16[256,6144]{1,0:T(8,128)(2,1)S(1)} %get-tuple-element.19.picked_ref.before_grad_ref.active_ref.out_grad_ref, bf16[256,6144]{1,0:T(8,128)(2,1)S(1)} %get-tuple-element.19.picked_ref.before_grad_ref.active_ref.out_grad_ref, ...), custom_call_target="tpu_custom_call" | custom-call | flops 2147483648 | bytes 11534336 | tf_op jit(solution)/shard_map/pallas_call | solution.py:356
  86.8 19.4 %all-to-all-done.3.rows_ref = bf16[128,2,24,128]{3,2,1,0:T(8,128)(2,1)} async-done(((bf16[128,2,24,128]{3,2,1,0:T(8,128)(2,1)}), bf16[128,2,24,128]{3,2,1,0:T(8,128)(2,1)}, u32[]{:S(2)}, u32[]{:S(2)}) %all-to-all-start.3) | async-done | bytes 1572896 | tf_op jit(solution)/shard_map/all_to_all | solution.py:415
  106.1 3.3 %shard_map.142 = (bf16[128,1024]{1,0:T(8,128)(2,1)}, bf16[128,1024]{1,0:T(8,128)(2,1)}) custom-call(bf16[128,2,24,128]{3,2,1,0:T(8,128)(2,1)} %all-to-all-done.3.rows_ref, s32[3,1,128]{2,1,0:T(1,128)} %bitcast.19, s32[1,128]{1,0:T(1,128)} %count_ref.5, bf16[128,1024]{1,0:T(8,128)(2,1)} %copy-done.4, bf16[128,1024]{1,0:T(8,128)(2,1)} %bitcast.13), custom_call_target="tpu_custom_call" | custom-call | flops 201326592 | bytes 3145728 | tf_op jit(solution)/shard_map/pallas_call | solution.py:403
Async XLA Ops:
  0.6 24.8 %copy-start.2 = (bf16[1,128,1024]{2,1,0:T(8,128)(2,1)S(1)}, bf16[1,128,1024]{2,1,0:T(8,128)(2,1)}, u32[]{:S(2)}) copy-start(bf16[1,128,1024]{2,1,0:T(8,128)(2,1)} %param.11) | copy-start | bytes 786436
  0.6 24.8 %copy-start.5 = (s32[1,128,3]{1,0,2:T(1,128)S(1)}, s32[1,128,3]{1,0,2:T(1,128)}, u32[]{:S(2)}) copy-start(s32[1,128,3]{1,0,2:T(1,128)} %param.18) | copy-start | bytes 4612
  0.7 24.8 %copy-start.6 = (s32[1,128]{1,0:T(1,128)S(1)}, s32[1,128]{1,0:T(1,128)}, u32[]{:S(2)}) copy-start(s32[1,128]{1,0:T(1,128)} %count_ref.5) | copy-start | bytes 1540
  4.8 25.9 %copy-start.1 = (bf16[512,1024]{1,0:T(8,128)(2,1)S(1)}, bf16[512,1024]{1,0:T(8,128)(2,1)}, u32[]{:S(2)}) copy-start(bf16[512,1024]{1,0:T(8,128)(2,1)} %weight_ref.1) | copy-start | bytes 3145732
  4.8 25.9 %copy-start.3 = (bf16[1,128,1024]{2,1,0:T(8,128)(2,1)S(1)}, bf16[1,128,1024]{2,1,0:T(8,128)(2,1)}, u32[]{:S(2)}) copy-start(bf16[1,128,1024]{2,1,0:T(8,128)(2,1)} %param.10) | copy-start | bytes 786436
  4.8 14.0 %all-to-all-start = ((bf16[8,192,128]{2,1,0:T(8,128)(2,1)}), bf16[8,192,128]{2,1,0:T(8,128)(2,1)S(1)}, u32[]{:S(2)}, u32[]{:S(2)}) async-start(bf16[8,192,128]{2,1,0:T(8,128)(2,1)} %bitcast.22), calls=%async_computation | async-start | bytes 786432 | tf_op jit(solution)/shard_map/all_to_all | solution.py:415
  21.3 9.4 %all-to-all-start.1 = ((bf16[8,64,128]{2,1,0:T(8,128)(2,1)}), bf16[8,64,128]{2,1,0:T(8,128)(2,1)S(1)}, u32[]{:S(2)}, u32[]{:S(2)}) async-start(bf16[8,64,128]{2,1,0:T(8,128)(2,1)} %bitcast.3), calls=%async_computation.1 | async-start | bytes 262144 | tf_op jit(solution)/shard_map/all_to_all | solution.py:415
  26.1 38.7 %copy-start.7 = (f32[1,1024]{1,0:T(1,128)S(1)}, f32[1,1024]{1,0:T(1,128)}, u32[]{:S(2)}) copy-start(f32[1,1024]{1,0:T(1,128)} %router_ref.1) | copy-start | bytes 12292
  31.9 32.9 %copy-start.4 = (bf16[128,1024]{1,0:T(8,128)(2,1)}, bf16[128,1024]{1,0:T(8,128)(2,1)S(1)}, u32[]{:S(2)}) copy-start(bf16[128,1024]{1,0:T(8,128)(2,1)S(1)} %get-tuple-element.16.resid_ref) | copy-start | bytes 786436
  75.2 1.1 %copy-start = (bf16[128,2,24,128]{3,2,1,0:T(8,128)(2,1)}, bf16[128,2,24,128]{3,2,1,0:T(8,128)(2,1)S(1)}, u32[]{:S(2)}) copy-start(bf16[128,2,24,128]{3,2,1,0:T(8,128)(2,1)S(1)} %get-tuple-element.15) | copy-start | bytes 4718596
  76.3 29.8 %all-to-all-start.3 = ((bf16[128,2,24,128]{3,2,1,0:T(8,128)(2,1)}), bf16[128,2,24,128]{3,2,1,0:T(8,128)(2,1)}, u32[]{:S(2)}, u32[]{:S(2)}) async-start(bf16[128,2,24,128]{3,2,1,0:T(8,128)(2,1)} %copy-done), calls=%async_computation.3 | async-start | bytes 3145728 | tf_op jit(solution)/shard_map/all_to_all | solution.py:415

commit v7 on v6

--- a/solution.py
+++ b/solution.py
@@ -224,7 +224,7 @@
     )(attended, frames, weight, index, count, packed)
 
 
-FF_TILE = 2048
+FF_TILE = 1024
 FF_STEPS = FF // FF_TILE
 WG_TILE = 512
 gelu_scale = (2.0 / jnp.pi) ** 0.5
@@ -272,15 +272,13 @@
     place = seats(grads[:, 0:128])
     take = place.T.astype(BF16)
     place = place.astype(BF16)
-    stage_rows(stage_x, rows_ref, 0)
-    rows = [unpack_rows(stage_x, slot) for slot in range(SLOT)]
-    both = jnp.concatenate([grads, jnp.concatenate(rows, axis=0)], axis=1)
-    both = dot(take, both.astype(BF16))
-    grads = both[:, :D].astype(BF16)
-    picked_wide = both[:, D:]
+    grads = dot(take, grads.astype(BF16)).astype(BF16)
     for step in range(FF_STEPS):
         second_loads[step].wait()
         pulled_ref[:, tiles(step)] = dot(grads, second_ref[tiles(step), :], ((1,), (1,)))
+    stage_rows(stage_x, rows_ref, 0)
+    rows = [unpack_rows(stage_x, slot).astype(BF16) for slot in range(SLOT)]
+    picked_wide = dot(take, jnp.concatenate(rows, axis=0))
     picked = picked_wide.astype(BF16)
     picked_ref[...] = picked
     logits = jnp.sum(picked_wide * router_ref[...], axis=-1, keepdims=True)

time: 110 us -> 109 us (level)
  no operation moved by 1% of the time
where the time goes in v7:
time: 109 us; the launch traced here: 108 us
  blocking collectives  32.9 us (30%)
  waiting for transfers between devices  31.4 us (29%)
  Pallas kernels  25.6 us (23%)
  starting transfers between devices  16 us (15%)
  between operations  1.4 us (1%)
  local copies, waits for them, and re-layouts  1.18 us (1%)
    all_to_all x1, blocking collectives, exchange(): return lax.all_to_all(rows, axes, split_axis=0, concat_axis=0, tiled=True)  32.9 us
    all_to_all x3, waiting for transfers between devices, exchange(): return lax.all_to_all(rows, axes, split_axis=0, concat_axis=0, tiled=True)  31.4 us
    all_to_all x3, starting transfers between devices, exchange(): return lax.all_to_all(rows, axes, split_axis=0, concat_axis=0, tiled=True)  16 us
    pallas_call x1, Pallas kernels, expert(): pl.pallas_call(expert_kernel, in_specs=[vmem, hbm, hbm, vmem], out_specs=...  9.37 us
    pallas_call x1, Pallas kernels, weight_grads(): pl.pallas_call(weight_grad_kernel, grid=(FF // tile,), in_specs=[pl.Block...  4.57 us
    pallas_call x1, Pallas kernels, project(): pl.pallas_call(project_kernel, in_specs=[vmem, pl.BlockSpec(memory_space=...  4.13 us
    pallas_call x1, Pallas kernels, combine(): pl.pallas_call(combine_kernel, out_shape=[jax.ShapeDtypeStruct((FR, D), B...  3.34 us
    pallas_call x1, Pallas kernels, attend(): pl.pallas_call(attend_kernel, in_specs=[pl.BlockSpec(memory_space=pltpu.S...  2.42 us
  transfers between devices with their start and end apart: 3, of which 3 were waited for; matrix products, arithmetic and copies ran while one was open for 0% of the time, Pallas kernels for 5%

profile of v7, /device:TPU:1, one launch (start us, length us, event | category | flops | bytes accessed | tf_op | source)
XLA Modules:
  0.0 108.4 jit_solution(11347611679298228259)
XLA Ops:
  0.6 0.0 copy-start.2
  0.6 0.0 copy-start.5
  0.7 0.0 copy-start.6
  0.7 4.1 %shard_map.137 = bf16[1536,128]{1,0:T(8,128)(2,1)} custom-call(bf16[128,1024]{1,0:T(8,128)(2,1)} %bitcast.15, bf16[1024,1536]{1,0:T(8,128)(2,1)} %weight_hbm.1), custom_call_target="tpu_custom_call" | custom-call | flops 402653184 | bytes 4194304 | tf_op jit(solution)/shard_map/pallas_call | solution.py:100
  4.8 0.0 copy-start.1
  4.8 0.0 copy-start.3
  4.8 6.0 %all-to-all-start = ((bf16[8,192,128]{2,1,0:T(8,128)(2,1)}), bf16[8,192,128]{2,1,0:T(8,128)(2,1)S(1)}, u32[]{:S(2)}, u32[]{:S(2)}) async-start(bf16[8,192,128]{2,1,0:T(8,128)(2,1)} %bitcast.22), calls=%async_computation | async-start | bytes 786432 | tf_op jit(solution)/shard_map/all_to_all | solution.py:413
  11.4 7.4 %all-to-all-done = bf16[8,192,128]{2,1,0:T(8,128)(2,1)S(1)} async-done(((bf16[8,192,128]{2,1,0:T(8,128)(2,1)}), bf16[8,192,128]{2,1,0:T(8,128)(2,1)S(1)}, u32[]{:S(2)}, u32[]{:S(2)}) %all-to-all-start) | async-done | bytes 393248 | tf_op jit(solution)/shard_map/all_to_all | solution.py:413
  18.9 2.4 %shard_map.138 = bf16[512,128]{1,0:T(8,128)(2,1)} custom-call(s32[1]{0:T(128)S(6)} %copy.17.length_ref, bf16[1536,128]{1,0:T(8,128)(2,1)S(1)} %bitcast.18), custom_call_target="tpu_custom_call" | custom-call | flops 268435456 | bytes 524288 | tf_op jit(solution)/shard_map/pallas_call | solution.py:168
  21.3 4.2 %all-to-all-start.1 = ((bf16[8,64,128]{2,1,0:T(8,128)(2,1)}), bf16[8,64,128]{2,1,0:T(8,128)(2,1)S(1)}, u32[]{:S(2)}, u32[]{:S(2)}) async-start(bf16[8,64,128]{2,1,0:T(8,128)(2,1)} %bitcast.3), calls=%async_computation.1 | async-start | bytes 262144 | tf_op jit(solution)/shard_map/all_to_all | solution.py:413
  25.4 0.0 copy-done.2
  25.4 0.0 copy-done.5
  25.4 0.0 copy-done.6
  25.4 0.6 shard_map.139.packed_ref
  26.1 0.0 copy-start.7
  26.1 4.6 %all-to-all-done.1 = bf16[8,64,128]{2,1,0:T(8,128)(2,1)S(1)} async-done(((bf16[8,64,128]{2,1,0:T(8,128)(2,1)}), bf16[8,64,128]{2,1,0:T(8,128)(2,1)S(1)}, u32[]{:S(2)}, u32[]{:S(2)}) %all-to-all-start.1) | async-done | bytes 131104 | tf_op jit(solution)/shard_map/all_to_all | solution.py:413
  30.7 0.0 copy-done.1
  30.7 0.0 copy-done.3
  30.7 1.1 %shard_map.140 = (bf16[128,1024]{1,0:T(8,128)(2,1)S(1)}, bf16[128,2,24,128]{3,2,1,0:T(8,128)(2,1)S(1)}) custom-call(bf16[512,128]{1,0:T(8,128)(2,1)S(1)} %bitcast.17, bf16[128,1024]{1,0:T(8,128)(2,1)S(1)} %bitcast.16, bf16[512,1024]{1,0:T(8,128)(2,1)S(1)} %copy-done.1, s32[3,1,128]{2,1,0:T(1,128)S(1)} %bitcast.21, ...), custom_call_target="tpu_custom_call", output_to_operand_aliasing={{1}: (5, {})} | custom-call | flops 234881024 | bytes 3145728 | tf_op jit(solution)/shard_map/pallas_call | solution.py:198
  31.9 0.0 copy-start.4
  31.9 32.9 %all_to_all.20.rows_ref = bf16[128,2,24,128]{3,2,1,0:T(8,128)(2,1)S(1)} all-to-all(bf16[128,2,24,128]{3,2,1,0:T(8,128)(2,1)S(1)} %get-tuple-element.14), channel_id=1, replica_groups=mesh['seq'=8,'exp'=16] {'seq','exp'}, dimensions={0} | all-to-all | bytes 3145728 | tf_op jit(solution)/shard_map/all_to_all | solution.py:413
  64.8 0.0 copy-done.4
  64.8 0.0 copy-done.7
  64.8 9.4 %shard_map.141 = (bf16[128,2,24,128]{3,2,1,0:T(8,128)(2,1)S(1)}, f32[1,1024]{1,0:T(1,128)}, bf16[256,6144]{1,0:T(8,128)(2,1)S(1)}) custom-call(bf16[128,2,24,128]{3,2,1,0:T(8,128)(2,1)S(1)} %all_to_all.20.rows_ref, bf16[1024,2048]{1,0:T(8,128)(2,1)} %bitcast.23, bf16[2048,1024]{1,0:T(8,128)(2,1)} %bitcast.24, f32[1,1024]{1,0:T(1,128)S(1)} %copy-done.7), custom_call_target="tpu_custom_call" | custom-call | flops 4294967296 | bytes 14680064 | tf_op jit(solution)/shard_map/pallas_call | solution.py:322
  74.1 0.0 copy-start
  74.1 1.1 %copy-done = bf16[128,2,24,128]{3,2,1,0:T(8,128)(2,1)} copy-done((bf16[128,2,24,128]{3,2,1,0:T(8,128)(2,1)}, bf16[128,2,24,128]{3,2,1,0:T(8,128)(2,1)S(1)}, u32[]{:S(2)}) %copy-start) | copy-done | bytes 1572888
  75.3 5.8 %all-to-all-start.3 = ((bf16[128,2,24,128]{3,2,1,0:T(8,128)(2,1)}), bf16[128,2,24,128]{3,2,1,0:T(8,128)(2,1)}, u32[]{:S(2)}, u32[]{:S(2)}) async-start(bf16[128,2,24,128]{3,2,1,0:T(8,128)(2,1)} %copy-done), calls=%async_computation.3 | async-start | bytes 3145728 | tf_op jit(solution)/shard_map/all_to_all | solution.py:413
  81.1 4.6 %shard_map.143 = (bf16[1024,2048]{1,0:T(8,128)(2,1)}, bf16[2048,1024]{1,0:T(8,128)(2,1)}) custom-call(bf16[256,6144]{1,0:T(8,128)(2,1)S(1)} %get-tuple-element.19.picked_ref.before_grad_ref.active_ref.out_grad_ref, bf16[256,6144]{1,0:T(8,128)(2,1)S(1)} %get-tuple-element.19.picked_ref.before_grad_ref.active_ref.out_grad_ref, ...), custom_call_target="tpu_custom_call" | custom-call | flops 2147483648 | bytes 11534336 | tf_op jit(solution)/shard_map/pallas_call | solution.py:354
  85.7 19.4 %all-to-all-done.3.rows_ref = bf16[128,2,24,128]{3,2,1,0:T(8,128)(2,1)} async-done(((bf16[128,2,24,128]{3,2,1,0:T(8,128)(2,1)}), bf16[128,2,24,128]{3,2,1,0:T(8,128)(2,1)}, u32[]{:S(2)}, u32[]{:S(2)}) %all-to-all-start.3) | async-done | bytes 1572896 | tf_op jit(solution)/shard_map/all_to_all | solution.py:413
  105.1 3.3 %shard_map.142 = (bf16[128,1024]{1,0:T(8,128)(2,1)}, bf16[128,1024]{1,0:T(8,128)(2,1)}) custom-call(bf16[128,2,24,128]{3,2,1,0:T(8,128)(2,1)} %all-to-all-done.3.rows_ref, s32[3,1,128]{2,1,0:T(1,128)} %bitcast.19, s32[1,128]{1,0:T(1,128)} %count_ref.5, bf16[128,1024]{1,0:T(8,128)(2,1)} %copy-done.4, bf16[128,1024]{1,0:T(8,128)(2,1)} %bitcast.13), custom_call_target="tpu_custom_call" | custom-call | flops 201326592 | bytes 3145728 | tf_op jit(solution)/shard_map/pallas_call | solution.py:401
Async XLA Ops:
  0.6 24.8 %copy-start.2 = (bf16[1,128,1024]{2,1,0:T(8,128)(2,1)S(1)}, bf16[1,128,1024]{2,1,0:T(8,128)(2,1)}, u32[]{:S(2)}) copy-start(bf16[1,128,1024]{2,1,0:T(8,128)(2,1)} %param.11) | copy-start | bytes 786436
  0.6 24.8 %copy-start.5 = (s32[1,128,3]{1,0,2:T(1,128)S(1)}, s32[1,128,3]{1,0,2:T(1,128)}, u32[]{:S(2)}) copy-start(s32[1,128,3]{1,0,2:T(1,128)} %param.18) | copy-start | bytes 4612
  0.7 24.8 %copy-start.6 = (s32[1,128]{1,0:T(1,128)S(1)}, s32[1,128]{1,0:T(1,128)}, u32[]{:S(2)}) copy-start(s32[1,128]{1,0:T(1,128)} %count_ref.5) | copy-start | bytes 1540
  4.8 25.9 %copy-start.1 = (bf16[512,1024]{1,0:T(8,128)(2,1)S(1)}, bf16[512,1024]{1,0:T(8,128)(2,1)}, u32[]{:S(2)}) copy-start(bf16[512,1024]{1,0:T(8,128)(2,1)} %weight_ref.1) | copy-start | bytes 3145732
  4.8 25.9 %copy-start.3 = (bf16[1,128,1024]{2,1,0:T(8,128)(2,1)S(1)}, bf16[1,128,1024]{2,1,0:T(8,128)(2,1)}, u32[]{:S(2)}) copy-start(bf16[1,128,1024]{2,1,0:T(8,128)(2,1)} %param.10) | copy-start | bytes 786436
  4.8 14.0 %all-to-all-start = ((bf16[8,192,128]{2,1,0:T(8,128)(2,1)}), bf16[8,192,128]{2,1,0:T(8,128)(2,1)S(1)}, u32[]{:S(2)}, u32[]{:S(2)}) async-start(bf16[8,192,128]{2,1,0:T(8,128)(2,1)} %bitcast.22), calls=%async_computation | async-start | bytes 786432 | tf_op jit(solution)/shard_map/all_to_all | solution.py:413
  21.3 9.4 %all-to-all-start.1 = ((bf16[8,64,128]{2,1,0:T(8,128)(2,1)}), bf16[8,64,128]{2,1,0:T(8,128)(2,1)S(1)}, u32[]{:S(2)}, u32[]{:S(2)}) async-start(bf16[8,64,128]{2,1,0:T(8,128)(2,1)} %bitcast.3), calls=%async_computation.1 | async-start | bytes 262144 | tf_op jit(solution)/shard_map/all_to_all | solution.py:413
  26.1 38.7 %copy-start.7 = (f32[1,1024]{1,0:T(1,128)S(1)}, f32[1,1024]{1,0:T(1,128)}, u32[]{:S(2)}) copy-start(f32[1,1024]{1,0:T(1,128)} %router_ref.1) | copy-start | bytes 12292
  31.9 32.9 %copy-start.4 = (bf16[128,1024]{1,0:T(8,128)(2,1)}, bf16[128,1024]{1,0:T(8,128)(2,1)S(1)}, u32[]{:S(2)}) copy-start(bf16[128,1024]{1,0:T(8,128)(2,1)S(1)} %get-tuple-element.16.resid_ref) | copy-start | bytes 786436
  74.1 1.1 %copy-start = (bf16[128,2,24,128]{3,2,1,0:T(8,128)(2,1)}, bf16[128,2,24,128]{3,2,1,0:T(8,128)(2,1)S(1)}, u32[]{:S(2)}) copy-start(bf16[128,2,24,128]{3,2,1,0:T(8,128)(2,1)S(1)} %get-tuple-element.15) | copy-start | bytes 4718596
  75.3 29.8 %all-to-all-start.3 = ((bf16[128,2,24,128]{3,2,1,0:T(8,128)(2,1)}), bf16[128,2,24,128]{3,2,1,0:T(8,128)(2,1)}, u32[]{:S(2)}, u32[]{:S(2)}) async-start(bf16[128,2,24,128]{3,2,1,0:T(8,128)(2,1)} %copy-done), calls=%async_computation.3 | async-start | bytes 3145728 | tf_op jit(solution)/shard_map/all_to_all | solution.py:413
